TPU v7x, 32 devices: a whole 2x2x4 slice. The times are simulated.
32 devices in a mesh: occ: 4 (over x, core), virt: 8 (over z, y).
Axes of the slice: x: 2, y: 2, z: 4, core: 2. Of those that a mesh axis runs over, the one named last changes fastest.
Arguments:
- integrals: bfloat16 [48, 1024, 2048], P('occ', 'virt'), may hold values from -1 to 1
- occ_energy: float32 [48], replicated, may hold values from -2 to -0.5
- virt_energy: float32 [1024], replicated, may hold values from 0.2 to 3
- partners: int32 [2], replicated, may hold values from 0 to 47
Outputs:
- gamma: bfloat16 [48, 1024, 2048], P('occ', 'virt')
All inputs are finite; a program needn't handle non-finite values.
Results may differ from a plain program's by a relative error of at most 0.0043.
Values may be sent and summed in bfloat16 or wider, within the bound.
No kernel may reach another device: no remote copies, remote signals or barrier semaphores. Data moves between devices by JAX's collectives and lax.ppermute only.
A program may use at most 64 MiB of HBM per device.

v0:
```python
import jax
import jax.numpy as jnp
from jax import lax
from jax.sharding import PartitionSpec as P


def broadcast(value, axis, source):
    kept = jnp.where(lax.axis_index(axis) == source, value, 0).astype(value.dtype)
    return lax.psum(kept, axis)


def per_device(integrals, occ_energy, virt_energy, partners):
    occ_dev, local_virt, aux_width = integrals.shape
    group_index = lax.axis_index("occ")
    my_index = lax.axis_index("virt")
    own_energy = lax.dynamic_slice_in_dim(occ_energy, group_index * occ_dev, occ_dev)
    local_energy = lax.dynamic_slice_in_dim(virt_energy, my_index * local_virt, local_virt)
    orbital_ids = jnp.arange(occ_energy.shape[0], dtype=jnp.int32)
    step_count = partners.shape[0]

    def fetch_partner(step_index):
        partner = partners[step_index]
        partner_local = lax.dynamic_index_in_dim(integrals, partner % occ_dev, 0, keepdims=False)
        partner_block = broadcast(partner_local, "occ", partner // occ_dev)
        pair_energy = jnp.sum(jnp.where(orbital_ids == partner, occ_energy, 0.0))
        return (partner_block, pair_energy)

    fetched = [fetch_partner(step_index) for step_index in range(step_count)]
    gamma_sum = jnp.zeros(integrals.shape, jnp.float32)
    for item in fetched:
        stacked = item[0][None]
        piece_rows = lax.all_gather(stacked, "virt", axis=1, tiled=True)
        columns = jnp.einsum(
            "iap,srp->siar", integrals, piece_rows, preferred_element_type=jnp.float32
        )
        denominator = (
            local_energy[None, None, :, None]
            + virt_energy[None, None, None, :]
            - own_energy[None, :, None, None]
            - item[1][None][:, None, None, None]
        )
        amplitudes = (columns / denominator).astype(jnp.bfloat16)
        gamma_sum = gamma_sum + jnp.einsum(
            "siab,sbp->iap", amplitudes, piece_rows, preferred_element_type=jnp.float32
        )
    return gamma_sum.astype(jnp.bfloat16)


def solution(mesh):
    in_specs = (P("occ", "virt", None), P(), P(), P())
    out_specs = P("occ", "virt", None)
    return jax.shard_map(
        per_device, mesh=mesh, in_specs=in_specs, out_specs=out_specs, check_vma=False
    )
```

profile of v0, /device:TPU:0, one launch (start us, length us, event | category | flops | bytes accessed | tf_op | source)
XLA Modules:
  0.0 233.2 jit_solution(2869226923946590510)
XLA Ops:
  6.5 0.0 all-reduce.3.cloned.1.call-start
  6.5 1.4 fusion.27
  11.8 2.2 dynamic-slice_select_fusion
  14.0 0.0 all-reduce.3.cloned.1.call-update
  14.0 0.0 all-gather.3.cloned.1.call-start
  14.1 38.9 %all-reduce.3.cloned.1.call-done = (bf16[1,128,2048]{2,1,0:T(8,128)(2,1)}, bf16[1,128,2048]{2,1,0:T(8,128)(2,1)}) async-done(((bf16[1,128,2048]{2,1,0:T(8,128)(2,1)}, bf16[1,128,2048]{2,1,0:T(8,128)(2,1)}), (bf16[1,128,2048]{2,1,0:T(8,128)(2,1)}, bf16[1,128,2048]{2,1,0:T(8,128)(2,1)})) %all-reduce.3.cloned.1.call-update) | async-done | bytes 1048592 | tf_op jit(solution)/shard_map/psum | solution.py:9
  53.0 0.0 all-gather.3.cloned.1.call-update
  53.0 0.0 all-gather.5.cloned.1.call-start
  53.1 0.7 all-gather.5.cloned.1.call-update
  53.8 0.7 dynamic_slice.15
  54.5 0.8 dynamic_slice.14
  55.2 2.6 %fusion.26 = (f32[]{:T(128)}, f32[]{:T(128)}) fusion(f32[48]{0:T(128)} %param.5, s32[]{:T(128)} %bitcast.6, s32[]{:T(128)} %bitcast), kind=kLoop, calls=%fused_computation.22 | loop fusion | flops 286 | bytes 208 | tf_op jit(solution)/shard_map/reduce_sum | solution.py:25
  57.8 0.9 broadcast_add_fusion
  58.7 70.5 %all-gather.3.cloned.1.call-done = bf16[1,1024,2048]{2,1,0:T(8,128)(2,1)} async-done(((bf16[1,128,2048]{2,1,0:T(8,128)(2,1)}), bf16[1,1024,2048]{2,1,0:T(8,128)(2,1)}) %all-gather.3.cloned.1.call-update) | async-done | bytes 4194320 | tf_op jit(solution)/shard_map/all_gather | solution.py:32
  129.2 34.5 %fusion.9 = f32[12,128,2048]{2,1,0:T(8,128)} fusion(bf16[1,1024,2048]{2,1,0:T(8,128)(2,1)} %all-gather.3.cloned.1.call-done, bf16[12,128,2048]{2,1,0:T(8,128)(2,1)} %param.4, f32[]{:T(128)} %get-tuple-element.6, f32[12]{0:T(128)S(1)} %dynamic_slice.15, f32[128,1024]{0,1:T(8,128)S(1)} %broadcast_add_fusion), kind=kOutput, calls=%fused_computation.10 | convolution fusion | flops 12891193344 | bytes 23593012 | tf_op jit(solution)/shard_map/siab,sbp->iap/dot_general | solution.py:43
  163.7 39.6 %all-gather.5.cloned.1.call-done = bf16[1,1024,2048]{2,1,0:T(8,128)(2,1)} async-done(((bf16[1,128,2048]{2,1,0:T(8,128)(2,1)}), bf16[1,1024,2048]{2,1,0:T(8,128)(2,1)}) %all-gather.5.cloned.1.call-update) | async-done | bytes 4194320 | tf_op jit(solution)/shard_map/all_gather | solution.py:32
  203.3 23.4 %add_convert_fusion = bf16[12,128,2048]{2,1,0:T(8,128)(2,1)} fusion(f32[12,128,2048]{2,1,0:T(8,128)} %fusion.9, bf16[1,1024,2048]{2,1,0:T(8,128)(2,1)} %all-gather.5.cloned.1.call-done, bf16[12,128,2048]{2,1,0:T(8,128)(2,1)} %param.4, f32[]{:T(128)} %get-tuple-element.5, f32[12]{0:T(128)S(1)} %dynamic_slice.15, f32[128,1024]{0,1:T(8,128)S(1)} %broadcast_add_fusion), kind=kOutput, calls=%fused_computation | convolution fusion | flops 12897484800 | bytes 29884468 | tf_op jit(solution)/shard_map/siab,sbp->iap/dot_general | solution.py:43
Async XLA Ops:
  6.5 46.5 %all-reduce.3.cloned.1.call-start = ((), (), s32[]{:S(2)}) async-start(), calls=%async_computation.2 | async-start | bytes 2097152 | tf_op jit(solution)/shard_map/psum | solution.py:9
  14.0 115.2 %all-gather.3.cloned.1.call-start = ((), (), s32[]{:S(2)}) async-start(), calls=%async_computation | async-start | bytes 4718592 | tf_op jit(solution)/shard_map/all_gather | solution.py:32
  53.0 150.3 %all-gather.5.cloned.1.call-start = ((), (), s32[]{:S(2)}) async-start(), calls=%async_computation.1 | async-start | bytes 4718592 | tf_op jit(solution)/shard_map/all_gather | solution.py:32
Sparse Core Ops, SparseCore 0:
  14.1 38.8 all-reduce.2
  55.3 73.8 all-gather.2
  131.6 71.6 all-gather.4
where the time goes:
time: 234 us; the launch traced here: 233 us
  waiting for transfers between devices  150 us (64%)
  matrix products  57.9 us (25%)
  between operations  17 us (7%)
  other arithmetic  5.7 us (2%)
  local copies, waits for them, and re-layouts  2.87 us (1%)
    all_gather x2, waiting for transfers between devices, per_device(): piece_rows = lax.all_gather(stacked, 'virt', axis=1, tiled=True)  110 us
    dot_general x2, matrix products, per_device(): jnp.einsum('siab,sbp->iap', amplitudes, piece_rows, preferred_element_typ...  57.9 us
    psum x1, waiting for transfers between devices, broadcast(): return lax.psum(kept, axis)  38.9 us
  transfers between devices with their start and end apart: 3, of which 3 were waited for; matrix products, arithmetic and copies ran while one was open for 17% of the time, Pallas kernels for 0%

commit v1 on v0

v1 whole, which is shorter than its diff:
```python
import jax
import jax.numpy as jnp
from jax import lax
from jax.experimental import pallas as pl
from jax.experimental.pallas import tpu as pltpu
from jax.sharding import PartitionSpec as P

TILE = 256


def contract(rows, blocks, row_energy, block_energy, total, out_dtype):
    height, width = rows.shape
    count, depth = len(blocks), blocks[0].shape[0]
    tile = min(TILE, height)
    while height % tile:
        tile //= 2

    def kernel(rows_ref, row_energy_ref, block_energy_ref, *rest):
        block_refs, rest = rest[:count], rest[count:]
        total_ref = rest[0] if total is not None else None
        out_ref, held, sems = rest[-3:]

        @pl.when(pl.program_id(0) == 0)
        def _():
            copies = [
                pltpu.make_async_copy(block_refs[k], held.at[pl.ds(k * depth, depth)], sems.at[k])
                for k in range(count)
            ]
            for copy in copies:
                copy.start()
            for copy in copies:
                copy.wait()

        scores = lax.dot_general(
            rows_ref[...], held[...], (((1,), (1,)), ((), ())), preferred_element_type=jnp.float32
        )
        amplitudes = (scores / (row_energy_ref[...] + block_energy_ref[...])).astype(jnp.bfloat16)
        result = jnp.dot(amplitudes, held[...], preferred_element_type=jnp.float32)
        if total_ref is not None:
            result = result + total_ref[...].astype(jnp.float32)
        out_ref[...] = result.astype(out_dtype)

    row_spec = pl.BlockSpec((tile, width), lambda i: (i, 0))
    specs = [row_spec, pl.BlockSpec((tile, 1), lambda i: (i, 0)), pl.BlockSpec((1, count * depth), lambda i: (0, 0))]
    specs += [pl.BlockSpec(memory_space=pl.ANY)] * count
    operands = [rows, row_energy, block_energy, *blocks]
    if total is not None:
        specs.append(row_spec)
        operands.append(total)
    return pl.pallas_call(
        kernel,
        grid=(height // tile,),
        in_specs=specs,
        out_specs=row_spec,
        out_shape=jax.ShapeDtypeStruct((height, width), out_dtype),
        scratch_shapes=[pltpu.VMEM((count * depth, width), jnp.bfloat16), pltpu.SemaphoreType.DMA((count,))],
        compiler_params=pltpu.CompilerParams(vmem_limit_bytes=48 << 20),
        cost_estimate=pl.CostEstimate(
            flops=4 * height * width * count * depth,
            bytes_accessed=2 * height * width * 2 + 2 * count * depth * width,
            transcendentals=0,
        ),
    )(*operands)


def per_device(occ_size, virt_size, integrals, occ_energy, virt_energy, partners):
    occ_dev, local_virt, aux_width = integrals.shape
    occ_index, virt_index = lax.axis_index("occ"), lax.axis_index("virt")
    core = occ_index % 2
    ring = virt_size // 2

    def swap_occ(value, bit):
        return lax.ppermute(value, "occ", [(o, o ^ bit) for o in range(occ_size)])

    def swap_pair(value):
        return lax.ppermute(value, "virt", [(v, v ^ 1) for v in range(virt_size)])

    def shift_ring(value):
        return lax.ppermute(value, "virt", [(v, (v + 2) % virt_size) for v in range(virt_size)])

    def kept(step):
        partner = partners[step]
        row = lax.dynamic_index_in_dim(integrals, partner % occ_dev, 0, keepdims=False)
        return jnp.where(partner // occ_dev == occ_index, row, 0).astype(row.dtype)

    def held_by(step, bits):
        return (partners[step] // occ_dev) & ~bits == occ_index & ~bits

    mine, other = core, 1 - core
    own = kept(mine)
    got = swap_occ(kept(other), 1)
    own = jnp.where(partners[mine] // occ_dev == occ_index, own, got)
    bit = 2
    while bit < occ_size:
        got = swap_occ(own, bit)
        own = jnp.where(held_by(mine, bit - 1), own, got)
        bit *= 2

    straight = [own]
    for _ in range(ring - 1):
        straight.append(shift_ring(straight[-1]))
    crossed = [swap_pair(block) for block in straight]

    own_energy = lax.dynamic_slice_in_dim(occ_energy, occ_index * occ_dev, occ_dev)
    local_energy = lax.dynamic_slice_in_dim(virt_energy, virt_index * local_virt, local_virt)
    row_energy = (local_energy[None, :] - own_energy[:, None]).reshape(-1, 1)

    def energy_of(step, position):
        values = lax.dynamic_slice_in_dim(virt_energy, position * local_virt, local_virt)
        return values - occ_energy[partners[step]]

    def pieces(block, position):
        return [(block, energy_of(mine, position)), (swap_occ(block, 1), energy_of(other, position))]

    rows = integrals.reshape(occ_dev * local_virt, aux_width)
    positions = [(virt_index - 2 * k) % virt_size for k in range(ring)]
    arrivals = []
    for k in range(ring):
        arrivals.append(pieces(straight[k], positions[k]))
        arrivals.append(pieces(crossed[k], positions[k] ^ 1))

    groups, total = group_arrivals(arrivals), None
    for index, group in enumerate(groups):
        last = index == len(groups) - 1
        total = contract(
            rows,
            [block for block, _ in group],
            row_energy,
            jnp.concatenate([energy for _, energy in group])[None, :],
            total,
            jnp.bfloat16 if last else jnp.float32,
        )
    return total.reshape(integrals.shape)


def group_arrivals(arrivals):
    count = len(arrivals)
    cuts = [0, 3 * count // 8, 5 * count // 8, 7 * count // 8, count]
    return [sum(arrivals[a:b], []) for a, b in zip(cuts, cuts[1:]) if b > a]


def solution(mesh):
    in_specs = (P("occ", "virt", None), P(), P(), P())
    out_specs = P("occ", "virt", None)

    def run(integrals, occ_energy, virt_energy, partners):
        return per_device(
            mesh.shape["occ"], mesh.shape["virt"], integrals, occ_energy, virt_energy, partners
        )

    return jax.shard_map(run, mesh=mesh, in_specs=in_specs, out_specs=out_specs, check_vma=False)
```

time: 234 us -> 123 us (0.53)
  waiting for transfers between devices: 150 us -> 25.6 us
  Pallas kernels: 0 us -> 62.2 us
  matrix products: 57.9 us -> 0 us
  starting transfers between devices: 0.08 us -> 10.5 us
  between operations: 17 us -> 8.32 us
  other arithmetic: 5.7 us -> 11.9 us
    all_gather x2 -> x0, waiting for transfers between devices: 110 us -> none  [per_device(): piece_rows = lax.all_gather(stacked, 'virt', axis=1, tiled=True)]
    pallas_call x0 -> x4, Pallas kernels: none -> 62.2 us  [contract(): pl.pallas_call(kernel, grid=(height // tile,), in_specs=specs, out_specs=...]
    dot_general x2 -> x0, matrix products: 57.9 us -> none  [per_device(): jnp.einsum('siab,sbp->iap', amplitudes, piece_rows, preferred_element_typ...]
    psum x1 -> x0, waiting for transfers between devices: 38.9 us -> none  [broadcast(): return lax.psum(kept, axis)]
    ppermute x0 -> x17, waiting for transfers between devices: none -> 25.6 us  [the longest x3 20.6 us: shift_ring(): lax.ppermute(value, 'virt', [(v, (v + 2) % virt_size) for v in range(virt...]
    ppermute x0 -> x17, starting transfers between devices: none -> 10.5 us  [the longest x10 4.56 us: swap_occ(): return lax.ppermute(value, 'occ', [(o, o ^ bit) for o in range(occ_size)])]
    unnamed x0 -> x7, other arithmetic: none -> 7.21 us
    reduce_sum x1 -> x0, other arithmetic: 2.58 us -> none  [fetch_partner(): pair_energy = jnp.sum(jnp.where(orbital_ids == partner, occ_energy, 0.0))]
  transfers between devices with their start and end apart: 3 -> 17, of which waited for: 3 -> 3; matrix products, arithmetic and copies ran while one was open for 17% -> 10% of each run, Pallas kernels for 0% -> 40%
where the time goes in v1:
time: 123 us; the launch traced here: 122 us
  Pallas kernels  62.2 us (51%)
  waiting for transfers between devices  25.6 us (21%)
  other arithmetic  11.9 us (10%)
  starting transfers between devices  10.5 us (9%)
  between operations  8.32 us (7%)
  local copies, waits for them, and re-layouts  3.83 us (3%)
    pallas_call x4, Pallas kernels, contract(): pl.pallas_call(kernel, grid=(height // tile,), in_specs=specs, out_specs=...  62.2 us
    ppermute x3, waiting for transfers between devices, shift_ring(): lax.ppermute(value, 'virt', [(v, (v + 2) % virt_size) for v in range(virt...  20.6 us
    unnamed x7, other arithmetic  7.21 us
    ppermute x10, waiting for transfers between devices, swap_occ(): return lax.ppermute(value, 'occ', [(o, o ^ bit) for o in range(occ_size)])  4.99 us
    ppermute x10, starting transfers between devices, swap_occ(): return lax.ppermute(value, 'occ', [(o, o ^ bit) for o in range(occ_size)])  4.56 us
    ppermute x4, starting transfers between devices, swap_pair(): return lax.ppermute(value, 'virt', [(v, v ^ 1) for v in range(virt_size)])  4.36 us
    dynamic_slice x2, local copies, waits for them, and re-layouts, energy_of(): return values - occ_energy[partners[step]]  2.79 us
  transfers between devices with their start and end apart: 17, of which 3 were waited for; matrix products, arithmetic and copies ran while one was open for 10% of the time, Pallas kernels for 40%

profile of v1, /device:TPU:0, one launch (start us, length us, event | category | flops | bytes accessed | tf_op | source)
XLA Modules:
  0.0 122.2 jit_solution(7550705995518265016)
XLA Ops:
  0.0 1.4 %fusion.1 = (s32[1]{0:T(128)}, s32[1]{0:T(128)}) fusion(s32[2]{0:T(128)} %param.7, s32[]{:T(128)S(6)} %select_n.168, s32[]{:T(128)S(6)} %select_n.170), kind=kLoop, calls=%fused_computation.25 | loop fusion | bytes 24 | tf_op jit(solution)/shard_map/dynamic_slice | solution.py:110
  3.5 1.1 select_bitcast_fusion
  4.6 0.5 collective-permute-start
  7.1 0.0 collective-permute-done
  7.1 1.1 bitcast_select_fusion
  8.2 2.6 %collective-permute-start.1 = (bf16[128,2048]{1,0:T(8,128)(2,1)S(1)}, bf16[128,2048]{1,0:T(8,128)(2,1)S(1)}, u32[]{:S(2)}, u32[]{:S(2)}) collective-permute-start(bf16[128,2048]{1,0:T(8,128)(2,1)S(1)} %bitcast_select_fusion), channel_id=1, source_target_pairs={{0,16},{8,24},{16,0},{24,8},{1,17},{9,25},{17,1},{25,9},{2,18},{10... | collective-permute-start | bytes 1572872 | tf_op jit(solution)/shard_map/ppermute | solution.py:73
  14.9 0.7 dynamic_slice.36
  15.6 1.4 %fusion = (f32[1]{0:T(128)}, f32[1]{0:T(128)}) fusion(f32[48]{0:T(128)} %param.5, s32[]{:T(128)S(6)} %select_n.169, s32[]{:T(128)S(6)} %select_n.171), kind=kLoop, calls=%fused_computation.24 | loop fusion | bytes 24 | tf_op jit(solution)/shard_map/dynamic_slice | solution.py:110
  17.0 1.4 %constant_dynamic-update-slice_fusion.5 = f32[768]{0:T(1024)S(1)} fusion(f32[768]{0:T(1024)S(1)} %custom-call, f32[]{:T(128)} %bitcast.2, f32[1024]{0:T(1024)} %param.6, s32[]{:T(128)S(6)} %select_n.195), kind=kLoop, calls=%fused_computation.10 | loop fusion | flops 128 | bytes 1032
  18.4 5.0 %collective-permute-done.1 = bf16[128,2048]{1,0:T(8,128)(2,1)S(1)} collective-permute-done((bf16[128,2048]{1,0:T(8,128)(2,1)S(1)}, bf16[128,2048]{1,0:T(8,128)(2,1)S(1)}, u32[]{:S(2)}, u32[]{:S(2)}) %collective-permute-start.1) | collective-permute-done | bytes 524320 | tf_op jit(solution)/shard_map/ppermute | solution.py:73
  23.4 0.1 broadcast_select_fusion.rest_0_
  23.4 1.8 %collective-permute-start.14 = (bf16[128,2048]{1,0:T(8,128)(2,1)S(1)}, bf16[128,2048]{1,0:T(8,128)(2,1)S(1)}, u32[]{:S(2)}, u32[]{:S(2)}) collective-permute-start(bf16[128,2048]{1,0:T(8,128)(2,1)S(1)} %broadcast_select_fusion.rest_0_), channel_id=1, source_target_pairs={{0,1},{1,0},{2,3},{3,2},{4,5},{5,4},{6,7},{7,6},{8,9},{9,8},{10,11... | collective-permute-start | bytes 1572872 | tf_op jit(solution)/shard_map/ppermute | solution.py:76
  25.2 1.6 %collective-permute-start.2 = (bf16[128,2048]{1,0:T(8,128)(2,1)S(1)}, bf16[128,2048]{1,0:T(8,128)(2,1)S(1)}, u32[]{:S(2)}, u32[]{:S(2)}) collective-permute-start(bf16[128,2048]{1,0:T(8,128)(2,1)S(1)} %broadcast_select_fusion.rest_0_), channel_id=1, source_target_pairs={{0,2},{1,3},{2,4},{3,5},{4,6},{5,7},{6,0},{7,1},{8,10},{9,11},{10,... | collective-permute-start | bytes 1572872 | tf_op jit(solution)/shard_map/ppermute | solution.py:79
  26.8 1.5 %constant_dynamic-update-slice_fusion.4 = f32[768]{0:T(1024)S(1)} fusion(f32[768]{0:T(1024)S(1)} %constant_dynamic-update-slice_fusion.5, f32[]{:T(128)} %bitcast.4, f32[1024]{0:T(1024)} %param.6, s32[]{:T(128)S(6)} %select_n.195), kind=kLoop, calls=%fused_computation.9 | loop fusion | flops 128 | bytes 1032
  28.3 1.4 %constant_dynamic-update-slice_fusion.3 = f32[768]{0:T(1024)S(1)} fusion(f32[768]{0:T(1024)S(1)} %constant_dynamic-update-slice_fusion.4, f32[]{:T(128)} %bitcast.2, f32[1024]{0:T(1024)} %param.6, s32[]{:T(128)S(6)} %select_n.196), kind=kLoop, calls=%fused_computation.8 | loop fusion | flops 128 | bytes 1032
  29.7 1.5 %constant_dynamic-update-slice_fusion.2 = f32[768]{0:T(1024)S(1)} fusion(f32[768]{0:T(1024)S(1)} %constant_dynamic-update-slice_fusion.3, f32[]{:T(128)} %bitcast.4, f32[1024]{0:T(1024)} %param.6, s32[]{:T(128)S(6)} %select_n.196), kind=kLoop, calls=%fused_computation.7 | loop fusion | flops 128 | bytes 1032
  31.1 1.4 %constant_dynamic-update-slice_fusion.1 = f32[768]{0:T(1024)S(1)} fusion(f32[768]{0:T(1024)S(1)} %constant_dynamic-update-slice_fusion.2, f32[]{:T(128)} %bitcast.2, f32[1024]{0:T(1024)} %param.6, s32[]{:T(128)S(6)} %select_n.197), kind=kLoop, calls=%fused_computation.6 | loop fusion | flops 128 | bytes 1032
  32.6 2.4 %constant_dynamic-update-slice_fusion = (f32[768]{0:T(1024)S(1)}, f32[128]{0:T(128)S(1)}, f32[128]{0:T(128)S(1)}, f32[128]{0:T(128)S(1)}, f32[128]{0:T(128)S(1)}...) fusion(f32[768]{0:T(1024)S(1)} %constant_dynamic-update-slice_f, ...), kind=kLoop, calls=%fused_computation.5 | loop fusion | flops 1408 | bytes 9764 | tf_op jit(solution)/shard_map/concatenate | solution.py:129
  34.9 0.1 collective-permute-start.13
  35.0 5.4 %collective-permute-done.2.rest_4_ = bf16[128,2048]{1,0:T(8,128)(2,1)S(1)} collective-permute-done((bf16[128,2048]{1,0:T(8,128)(2,1)S(1)}, bf16[128,2048]{1,0:T(8,128)(2,1)S(1)}, u32[]{:S(2)}, u32[]{:S(2)}) %collective-permute-start.2) | collective-permute-done | bytes 524320 | tf_op jit(solution)/shard_map/ppermute | solution.py:79
  40.4 0.0 collective-permute-start.16
  40.4 0.5 collective-permute-start.10
  40.9 0.0 collective-permute-start.3
  40.9 0.0 collective-permute-done.14.rest_2_
  40.9 0.2 collective-permute-start.15
  41.1 0.1 subtract_bitcast_fusion
  41.2 0.3 copy.10
  41.6 15.2 %collective-permute-done.3.rest_2_ = bf16[128,2048]{1,0:T(8,128)(2,1)S(1)} collective-permute-done((bf16[128,2048]{1,0:T(8,128)(2,1)S(1)}, bf16[128,2048]{1,0:T(8,128)(2,1)S(1)}, u32[]{:S(2)}, u32[]{:S(2)}) %collective-permute-start.3) | collective-permute-done | bytes 524320 | tf_op jit(solution)/shard_map/ppermute | solution.py:79
  56.7 0.0 collective-permute-start.12
  56.7 0.0 collective-permute-done.13.rest_1_
  56.7 1.5 %collective-permute-start.7 = (bf16[128,2048]{1,0:T(8,128)(2,1)S(1)}, bf16[128,2048]{1,0:T(8,128)(2,1)S(1)}, u32[]{:S(2)}, u32[]{:S(2)}) collective-permute-start(bf16[128,2048]{1,0:T(8,128)(2,1)S(1)} %collective-permute-done.3.rest_2_), channel_id=1, source_target_pairs={{0,1},{1,0},{2,3},{3,2},{4,5},{5,4},{6,7},{7,6},{8,9},{9,8},{10,11... | collective-permute-start | bytes 1572872 | tf_op jit(solution)/shard_map/ppermute | solution.py:76
  58.3 0.0 collective-permute-done.15.rest_3_
  58.3 0.0 collective-permute-start.4
  58.3 0.0 collective-permute-done.10.rest_0_
  58.3 0.3 collective-permute-start.11
  58.6 0.0 collective-permute-done.16.rest_5_
  58.6 17.2 %shard_map.46.rest_4_ = f32[1536,2048]{1,0:T(8,128)} custom-call(bf16[1536,2048]{1,0:T(8,128)(2,1)} %bitcast.27, f32[1536,1]{1,0:T(8,128)S(1)} %bitcast.20, f32[1,768]{1,0:T(1,128)S(1)} %broadcast_in_dim.23.block_energy_ref, bf16[128,2048]{1,0:T(8,128)(2,1)S(1)} %broadcast_select_fusion.rest_0_, bf16[128,2048]{1,0:T(8,128)(2,1)} %collective-permute-done.13.rest_1_, ...), custom_call_target="tpu_custom_call" | custom-call | flops 9663676416 | bytes 15728640 | tf_op jit(solution)/shard_map/pallas_call | solution.py:50
  75.7 0.0 collective-permute-done.4.rest_2_
  75.8 0.4 collective-permute-start.9
  76.1 0.5 collective-permute-start.5
  76.6 0.0 collective-permute-done.7.rest_0_
  76.6 0.0 collective-permute-start.8
  76.6 0.0 collective-permute-done.11.rest_1_
  76.6 0.0 collective-permute-done.12.rest_3_
  76.6 15.9 %shard_map.47.rest_4_ = f32[1536,2048]{1,0:T(8,128)} custom-call(bf16[1536,2048]{1,0:T(8,128)(2,1)} %bitcast.28, f32[1536,1]{1,0:T(8,128)S(1)} %bitcast.21, f32[1,512]{1,0:T(1,128)S(1)} %bitcast.25, bf16[128,2048]{1,0:T(8,128)(2,1)S(1)} %collective-permute-done.10.rest_0_, bf16[128,2048]{1,0:T(8,128)(2,1)S(1)} %collective-permute-done.11.rest_1_, ...), custom_call_target="tpu_custom_call" | custom-call | flops 6442450944 | bytes 14680064 | tf_op jit(solution)/shard_map/pallas_call | solution.py:50
  92.5 0.0 collective-permute-done.5.rest_0_
  92.5 0.6 collective-permute-start.6
  93.1 0.0 collective-permute-done.8.rest_1_
  93.1 0.0 collective-permute-done.9.rest_3_
  93.1 15.8 %shard_map.48.rest_2_ = f32[1536,2048]{1,0:T(8,128)} custom-call(bf16[1536,2048]{1,0:T(8,128)(2,1)} %bitcast.29, f32[1536,1]{1,0:T(8,128)S(1)} %bitcast.22, f32[1,512]{1,0:T(1,128)S(1)} %bitcast.24, bf16[128,2048]{1,0:T(8,128)(2,1)S(1)} %collective-permute-done.7.rest_0_, bf16[128,2048]{1,0:T(8,128)(2,1)S(1)} %collective-permute-done.8.rest_1_, ...), custom_call_target="tpu_custom_call" | custom-call | flops 6442450944 | bytes 14680064 | tf_op jit(solution)/shard_map/pallas_call | solution.py:50
  108.9 0.0 collective-permute-done.6.rest_1_
  108.9 13.3 %shard_map.49 = bf16[1536,2048]{1,0:T(8,128)(2,1)} custom-call(bf16[1536,2048]{1,0:T(8,128)(2,1)} %bitcast.30, f32[1536,1]{1,0:T(8,128)S(1)} %bitcast.23, f32[1,256]{1,0:T(1,128)S(1)} %bitcast.26, bf16[128,2048]{1,0:T(8,128)(2,1)S(1)} %collective-permute-done.5.rest_0_, bf16[128,2048]{1,0:T(8,128)(2,1)S(1)} %collective-permute-done.6.rest_1_, ...), custom_call_target="tpu_custom_call" | custom-call | flops 3221225472 | bytes 13631488 | tf_op jit(solution)/shard_map/pallas_call | solution.py:50
  (6 shorter events, 0.0 us)
Async XLA Ops:
  4.6 2.5 %collective-permute-start = (bf16[128,2048]{1,0:T(8,128)(2,1)S(1)}, bf16[128,2048]{1,0:T(8,128)(2,1)S(1)}, u32[]{:S(2)}, u32[]{:S(2)}) collective-permute-start(bf16[128,2048]{1,0:T(8,128)(2,1)S(1)} %select_bitcast_fusion), channel_id=1, source_target_pairs={{0,8},{8,0},{16,24},{24,16},{1,9},{9,1},{17,25},{25,17},{2,10},{10... | collective-permute-start | bytes 1572872 | tf_op jit(solution)/shard_map/ppermute | solution.py:73
  8.2 15.2 %collective-permute-start.1 = (bf16[128,2048]{1,0:T(8,128)(2,1)S(1)}, bf16[128,2048]{1,0:T(8,128)(2,1)S(1)}, u32[]{:S(2)}, u32[]{:S(2)}) collective-permute-start(bf16[128,2048]{1,0:T(8,128)(2,1)S(1)} %bitcast_select_fusion), channel_id=1, source_target_pairs={{0,16},{8,24},{16,0},{24,8},{1,17},{9,25},{17,1},{25,9},{2,18},{10... | collective-permute-start | bytes 1572872 | tf_op jit(solution)/shard_map/ppermute | solution.py:73
  23.4 17.5 %collective-permute-start.14 = (bf16[128,2048]{1,0:T(8,128)(2,1)S(1)}, bf16[128,2048]{1,0:T(8,128)(2,1)S(1)}, u32[]{:S(2)}, u32[]{:S(2)}) collective-permute-start(bf16[128,2048]{1,0:T(8,128)(2,1)S(1)} %broadcast_select_fusion.rest_0_), channel_id=1, source_target_pairs={{0,1},{1,0},{2,3},{3,2},{4,5},{5,4},{6,7},{7,6},{8,9},{9,8},{10,11... | collective-permute-start | bytes 1572872 | tf_op jit(solution)/shard_map/ppermute | solution.py:76
  25.2 15.1 %collective-permute-start.2 = (bf16[128,2048]{1,0:T(8,128)(2,1)S(1)}, bf16[128,2048]{1,0:T(8,128)(2,1)S(1)}, u32[]{:S(2)}, u32[]{:S(2)}) collective-permute-start(bf16[128,2048]{1,0:T(8,128)(2,1)S(1)} %broadcast_select_fusion.rest_0_), channel_id=1, source_target_pairs={{0,2},{1,3},{2,4},{3,5},{4,6},{5,7},{6,0},{7,1},{8,10},{9,11},{10,... | collective-permute-start | bytes 1572872 | tf_op jit(solution)/shard_map/ppermute | solution.py:79
  34.9 21.8 %collective-permute-start.13 = (bf16[128,2048]{1,0:T(8,128)(2,1)S(1)}, bf16[128,2048]{1,0:T(8,128)(2,1)}, u32[]{:S(2)}, u32[]{:S(2)}) collective-permute-start(bf16[128,2048]{1,0:T(8,128)(2,1)S(1)} %broadcast_select_fusion.rest_0_), channel_id=1, source_target_pairs={{0,8},{8,0},{16,24},{24,16},{1,9},{9,1},{17,25},{25,17},{2,10},{10... | collective-permute-start | bytes 1572872 | tf_op jit(solution)/shard_map/ppermute | solution.py:73
  40.4 18.2 %collective-permute-start.16 = (bf16[128,2048]{1,0:T(8,128)(2,1)S(1)}, bf16[128,2048]{1,0:T(8,128)(2,1)}, u32[]{:S(2)}, u32[]{:S(2)}) collective-permute-start(bf16[128,2048]{1,0:T(8,128)(2,1)S(1)} %collective-permute-done.2.rest_4_), channel_id=1, source_target_pairs={{0,8},{8,0},{16,24},{24,16},{1,9},{9,1},{17,25},{25,17},{2,10},{10... | collective-permute-start | bytes 1572872 | tf_op jit(solution)/shard_map/ppermute | solution.py:73
  40.4 17.9 %collective-permute-start.10 = (bf16[128,2048]{1,0:T(8,128)(2,1)S(1)}, bf16[128,2048]{1,0:T(8,128)(2,1)S(1)}, u32[]{:S(2)}, u32[]{:S(2)}) collective-permute-start(bf16[128,2048]{1,0:T(8,128)(2,1)S(1)} %collective-permute-done.2.rest_4_), channel_id=1, source_target_pairs={{0,1},{1,0},{2,3},{3,2},{4,5},{5,4},{6,7},{7,6},{8,9},{9,8},{10,11... | collective-permute-start | bytes 1572872 | tf_op jit(solution)/shard_map/ppermute | solution.py:76
  40.9 15.9 %collective-permute-start.3 = (bf16[128,2048]{1,0:T(8,128)(2,1)S(1)}, bf16[128,2048]{1,0:T(8,128)(2,1)S(1)}, u32[]{:S(2)}, u32[]{:S(2)}) collective-permute-start(bf16[128,2048]{1,0:T(8,128)(2,1)S(1)} %collective-permute-done.2.rest_4_), channel_id=1, source_target_pairs={{0,2},{1,3},{2,4},{3,5},{4,6},{5,7},{6,0},{7,1},{8,10},{9,11},{10,... | collective-permute-start | bytes 1572872 | tf_op jit(solution)/shard_map/ppermute | solution.py:79
  40.9 17.4 %collective-permute-start.15 = (bf16[128,2048]{1,0:T(8,128)(2,1)S(1)}, bf16[128,2048]{1,0:T(8,128)(2,1)}, u32[]{:S(2)}, u32[]{:S(2)}) collective-permute-start(bf16[128,2048]{1,0:T(8,128)(2,1)S(1)} %collective-permute-done.14.rest_2_), channel_id=1, source_target_pairs={{0,8},{8,0},{16,24},{24,16},{1,9},{9,1},{17,25},{25,17},{2,10},{10... | collective-permute-start | bytes 1572872 | tf_op jit(solution)/shard_map/ppermute | solution.py:73
  56.7 19.9 %collective-permute-start.12 = (bf16[128,2048]{1,0:T(8,128)(2,1)S(1)}, bf16[128,2048]{1,0:T(8,128)(2,1)S(1)}, u32[]{:S(2)}, u32[]{:S(2)}) collective-permute-start(bf16[128,2048]{1,0:T(8,128)(2,1)S(1)} %collective-permute-done.3.rest_2_), channel_id=1, source_target_pairs={{0,8},{8,0},{16,24},{24,16},{1,9},{9,1},{17,25},{25,17},{2,10},{10... | collective-permute-start | bytes 1572872 | tf_op jit(solution)/shard_map/ppermute | solution.py:73
  56.7 19.9 %collective-permute-start.7 = (bf16[128,2048]{1,0:T(8,128)(2,1)S(1)}, bf16[128,2048]{1,0:T(8,128)(2,1)S(1)}, u32[]{:S(2)}, u32[]{:S(2)}) collective-permute-start(bf16[128,2048]{1,0:T(8,128)(2,1)S(1)} %collective-permute-done.3.rest_2_), channel_id=1, source_target_pairs={{0,1},{1,0},{2,3},{3,2},{4,5},{5,4},{6,7},{7,6},{8,9},{9,8},{10,11... | collective-permute-start | bytes 1572872 | tf_op jit(solution)/shard_map/ppermute | solution.py:76
  58.3 17.5 %collective-permute-start.4 = (bf16[128,2048]{1,0:T(8,128)(2,1)S(1)}, bf16[128,2048]{1,0:T(8,128)(2,1)S(1)}, u32[]{:S(2)}, u32[]{:S(2)}) collective-permute-start(bf16[128,2048]{1,0:T(8,128)(2,1)S(1)} %collective-permute-done.3.rest_2_), channel_id=1, source_target_pairs={{0,2},{1,3},{2,4},{3,5},{4,6},{5,7},{6,0},{7,1},{8,10},{9,11},{10,... | collective-permute-start | bytes 1572872 | tf_op jit(solution)/shard_map/ppermute | solution.py:79
  58.3 18.3 %collective-permute-start.11 = (bf16[128,2048]{1,0:T(8,128)(2,1)S(1)}, bf16[128,2048]{1,0:T(8,128)(2,1)S(1)}, u32[]{:S(2)}, u32[]{:S(2)}) collective-permute-start(bf16[128,2048]{1,0:T(8,128)(2,1)S(1)} %collective-permute-done.10.rest_0_), channel_id=1, source_target_pairs={{0,8},{8,0},{16,24},{24,16},{1,9},{9,1},{17,25},{25,17},{2,10},{10... | collective-permute-start | bytes 1572872 | tf_op jit(solution)/shard_map/ppermute | solution.py:73
  75.8 17.3 %collective-permute-start.9 = (bf16[128,2048]{1,0:T(8,128)(2,1)S(1)}, bf16[128,2048]{1,0:T(8,128)(2,1)S(1)}, u32[]{:S(2)}, u32[]{:S(2)}) collective-permute-start(bf16[128,2048]{1,0:T(8,128)(2,1)S(1)} %collective-permute-done.4.rest_2_), channel_id=1, source_target_pairs={{0,8},{8,0},{16,24},{24,16},{1,9},{9,1},{17,25},{25,17},{2,10},{10... | collective-permute-start | bytes 1572872 | tf_op jit(solution)/shard_map/ppermute | solution.py:73
  76.1 16.4 %collective-permute-start.5 = (bf16[128,2048]{1,0:T(8,128)(2,1)S(1)}, bf16[128,2048]{1,0:T(8,128)(2,1)S(1)}, u32[]{:S(2)}, u32[]{:S(2)}) collective-permute-start(bf16[128,2048]{1,0:T(8,128)(2,1)S(1)} %collective-permute-done.4.rest_2_), channel_id=1, source_target_pairs={{0,1},{1,0},{2,3},{3,2},{4,5},{5,4},{6,7},{7,6},{8,9},{9,8},{10,11... | collective-permute-start | bytes 1572872 | tf_op jit(solution)/shard_map/ppermute | solution.py:76
  76.6 16.5 %collective-permute-start.8 = (bf16[128,2048]{1,0:T(8,128)(2,1)S(1)}, bf16[128,2048]{1,0:T(8,128)(2,1)S(1)}, u32[]{:S(2)}, u32[]{:S(2)}) collective-permute-start(bf16[128,2048]{1,0:T(8,128)(2,1)S(1)} %collective-permute-done.7.rest_0_), channel_id=1, source_target_pairs={{0,8},{8,0},{16,24},{24,16},{1,9},{9,1},{17,25},{25,17},{2,10},{10... | collective-permute-start | bytes 1572872 | tf_op jit(solution)/shard_map/ppermute | solution.py:73
  92.5 16.4 %collective-permute-start.6 = (bf16[128,2048]{1,0:T(8,128)(2,1)S(1)}, bf16[128,2048]{1,0:T(8,128)(2,1)S(1)}, u32[]{:S(2)}, u32[]{:S(2)}) collective-permute-start(bf16[128,2048]{1,0:T(8,128)(2,1)S(1)} %collective-permute-done.5.rest_0_), channel_id=1, source_target_pairs={{0,8},{8,0},{16,24},{24,16},{1,9},{9,1},{17,25},{25,17},{2,10},{10... | collective-permute-start | bytes 1572872 | tf_op jit(solution)/shard_map/ppermute | solution.py:73

commit v2 on v0

v2 whole, which is shorter than its diff:
```python
import jax
import jax.numpy as jnp
from jax import lax
from jax.experimental import pallas as pl
from jax.experimental.pallas import tpu as pltpu
from jax.sharding import PartitionSpec as P

VMEM = pl.BlockSpec(memory_space=pltpu.VMEM)
ANY = pl.BlockSpec(memory_space=pl.ANY)


def tile_of(height, largest):
    return max(t for t in range(16, largest + 1, 16) if height % t == 0)


def bring(rows):
    def kernel(rows_ref, out_ref):
        pltpu.sync_copy(rows_ref, out_ref)

    return pl.pallas_call(
        kernel,
        in_specs=[ANY],
        out_specs=VMEM,
        out_shape=pltpu.VMEM(rows.shape, rows.dtype),
        compiler_params=pltpu.CompilerParams(vmem_limit_bytes=8 << 20),
    )(rows)


def contract(rows, blocks, row_energy, block_energy, total, last):
    height, width = rows.shape
    count, depth = len(blocks), blocks[0].shape[0]
    tile = tile_of(height, 512)
    tiles = height // tile

    def kernel(rows_ref, row_energy_ref, block_energy_ref, *rest):
        block_refs, rest = rest[:count], rest[count:]
        total_ref, rest = (rest[0], rest[1:]) if total is not None else (None, rest)
        out_ref, token_ref, held, sems = rest[:4]
        copies = [
            pltpu.make_async_copy(block_refs[k], held.at[pl.ds(k * depth, depth)], sems.at[k]) for k in range(count)
        ]
        for copy in copies:
            copy.start()
        token_ref[...] = jnp.zeros_like(token_ref)
        for copy in copies:
            copy.wait()
        writes = []
        for i in range(tiles):
            at = pl.ds(i * tile, tile)
            scores = lax.dot_general(
                rows_ref[at, :], held[...], (((1,), (1,)), ((), ())), preferred_element_type=jnp.float32
            )
            amplitudes = (scores / (row_energy_ref[at, :] + block_energy_ref[...])).astype(jnp.bfloat16)
            result = jnp.dot(amplitudes, held[...], preferred_element_type=jnp.float32)
            if total_ref is not None:
                result = result + total_ref[at, :]
            if last:
                staged, write_sems = rest[4:]
                if i >= 2:
                    writes[i - 2].wait()
                staged[i % 2] = result.astype(jnp.bfloat16)
                write = pltpu.make_async_copy(staged.at[i % 2], out_ref.at[at, :], write_sems.at[i])
                write.start()
                writes.append(write)
            else:
                out_ref[at, :] = result
        for write in writes[-2:]:
            write.wait()

    operands = [rows, row_energy, block_energy, *blocks]
    specs = [VMEM] * 3 + [ANY] * count
    if total is not None:
        operands.append(total)
        specs.append(VMEM)
    scratch = [pltpu.VMEM((count * depth, width), jnp.bfloat16), pltpu.SemaphoreType.DMA((count,))]
    if last:
        scratch += [pltpu.VMEM((2, tile, width), jnp.bfloat16), pltpu.SemaphoreType.DMA((tiles,))]
        out = jax.ShapeDtypeStruct((height, width), jnp.bfloat16)
    else:
        out = pltpu.VMEM((height, width), jnp.float32)
    return pl.pallas_call(
        kernel,
        in_specs=specs,
        out_specs=(ANY if last else VMEM, VMEM),
        out_shape=(out, jax.ShapeDtypeStruct((8, 128), jnp.float32)),
        scratch_shapes=scratch,
        input_output_aliases={3 + count: 0} if total is not None and not last else {},
        compiler_params=pltpu.CompilerParams(vmem_limit_bytes=16 << 20),
        cost_estimate=pl.CostEstimate(
            flops=4 * height * width * count * depth, bytes_accessed=2 * count * depth * width, transcendentals=0
        ),
    )(*operands)


def gate(tokens, values):
    count, skip = len(values), len(tokens)

    def kernel(*refs):
        del refs

    return pl.pallas_call(
        kernel,
        in_specs=[ANY] * (skip + count),
        out_specs=[ANY] * count,
        out_shape=[jax.ShapeDtypeStruct(value.shape, value.dtype) for value in values],
        input_output_aliases={skip + k: k for k in range(count)},
        compiler_params=pltpu.CompilerParams(vmem_limit_bytes=1 << 20),
    )(*tokens, *values)


def per_device(occ_size, virt_size, integrals, occ_energy, virt_energy, partners):
    occ_dev, local_virt, aux_width = integrals.shape
    occ_index, virt_index = lax.axis_index("occ"), lax.axis_index("virt")
    core, plane = occ_index % 2, occ_index // 2 % 2
    ring, half = virt_size // 2, local_virt // 2

    def swap_occ(value, bit):
        return lax.ppermute(value, "occ", [(o, o ^ bit) for o in range(occ_size)])

    def swap_pair(value):
        return lax.ppermute(value, "virt", [(v, v ^ 1) for v in range(virt_size)])

    def shift_ring(value):
        return lax.ppermute(value, "virt", [(v, (v - 2) % virt_size) for v in range(virt_size)])

    mine, other = partners[core], partners[1 - core]
    owner = mine // occ_dev
    own = lax.dynamic_index_in_dim(integrals, mine % occ_dev, 0, keepdims=False)
    sent = lax.dynamic_index_in_dim(integrals, other % occ_dev, 0, keepdims=False)
    own = jnp.where(owner == occ_index, own, swap_occ(sent, 1))

    def half_of(which):
        return lax.dynamic_slice_in_dim(own, which * half, half)

    halves = [half_of(plane), half_of(1 - plane)]
    bit = 2
    while bit < occ_size:
        sent = halves[::-1] if bit == 2 else halves
        held = owner & ~(bit - 1) == occ_index & ~(bit - 1)
        halves = [jnp.where(held, kept, swap_occ(value, bit)) for kept, value in zip(halves, sent)]
        bit *= 2

    rows = bring(integrals.reshape(occ_dev * local_virt, aux_width))
    own_energy = lax.dynamic_slice_in_dim(occ_energy, occ_index * occ_dev, occ_dev)
    local_energy = lax.dynamic_slice_in_dim(virt_energy, virt_index * local_virt, local_virt)
    row_energy = (local_energy[None, :] - own_energy[:, None]).reshape(-1, 1)
    ringed = lax.dynamic_slice_in_dim(
        jnp.concatenate([virt_energy, virt_energy]), virt_index // 2 * 2 * local_virt, virt_size * local_virt
    ).reshape(ring, 2, 2, half)
    ringed = jnp.where(virt_index % 2 == 0, ringed, ringed[:, ::-1])
    ringed = jnp.where(plane == 0, ringed, ringed[:, :, ::-1])
    pair = jnp.stack([occ_energy[mine], occ_energy[other]])
    block_energy = (ringed[:, :, :, None] - pair[None, None, None, :, None]).reshape(ring * 2, 1, 4 * half)

    def both(blocks):
        return [block for value in blocks for block in (value, swap_occ(value, 1))]

    def energy(first, count):
        return block_energy[first : first + count].reshape(1, -1)

    straight = [*gate([rows, row_energy, block_energy], halves[:1]), halves[1]]
    total, token = contract(rows, both(straight), row_energy, energy(0, 1), None, False)
    shifted, crossed = [], []
    for k in range(1, ring):
        arrived, crossed = [], []
        for block in straight:
            moved = gate([token], [shift_ring(block), swap_pair(block)])
            arrived.append(moved[0])
            crossed.append(moved[1])
        blocks = [*both(crossed), *both(arrived)]
        straight = arrived
        total, token = contract(rows, blocks, row_energy, energy(2 * k - 1, 2), total, False)
    crossed = [swap_pair(straight[0]), shift_ring(crossed[1])]
    crossed = gate([token], crossed)
    total, token = contract(rows, both(crossed), row_energy, energy(2 * ring - 1, 1), total, True)
    return total.reshape(integrals.shape)


def solution(mesh):
    in_specs = (P("occ", "virt", None), P(), P(), P())
    out_specs = P("occ", "virt", None)

    def run(integrals, occ_energy, virt_energy, partners):
        return per_device(
            mesh.shape["occ"], mesh.shape["virt"], integrals, occ_energy, virt_energy, partners
        )

    return jax.shard_map(run, mesh=mesh, in_specs=in_specs, out_specs=out_specs, check_vma=False)
```

time: 234 us -> 104 us (0.44)
  waiting for transfers between devices: 150 us -> 16.4 us
  matrix products: 57.9 us -> 0 us
  Pallas kernels: 0 us -> 36.1 us
  starting transfers between devices: 0.08 us -> 27.2 us
  local copies, waits for them, and re-layouts: 2.87 us -> 14.2 us
  between operations: 17 us -> 6.66 us
    all_gather x2 -> x0, waiting for transfers between devices: 110 us -> none  [per_device(): piece_rows = lax.all_gather(stacked, 'virt', axis=1, tiled=True)]
    dot_general x2 -> x0, matrix products: 57.9 us -> none  [per_device(): jnp.einsum('siab,sbp->iap', amplitudes, piece_rows, preferred_element_typ...]
    psum x1 -> x0, waiting for transfers between devices: 38.9 us -> none  [broadcast(): return lax.psum(kept, axis)]
    pallas_call x0 -> x14, Pallas kernels: none -> 36.1 us  [the longest x5 35.7 us: contract(): pl.pallas_call(kernel, in_specs=specs, out_specs=(ANY if last else VMEM,...]
    ppermute x0 -> x33, starting transfers between devices: none -> 27.2 us  [the longest x7 10.9 us: shift_ring(): lax.ppermute(value, 'virt', [(v, (v - 2) % virt_size) for v in range(virt...]
    ppermute x0 -> x33, waiting for transfers between devices: none -> 16.4 us  [the longest x7 7.24 us: shift_ring(): lax.ppermute(value, 'virt', [(v, (v - 2) % virt_size) for v in range(virt...]
    unnamed x0 -> x10, local copies, waits for them, and re-layouts: none -> 8.57 us
    dynamic_slice x2 -> x5, local copies, waits for them, and re-layouts: 1.49 us -> 4.16 us  [the longest x1 1.32 us: per_device(): pair = jnp.stack([occ_energy[mine], occ_energy[other]])]
  transfers between devices with their start and end apart: 3 -> 33, of which waited for: 3 -> 9; matrix products, arithmetic and copies ran while one was open for 17% -> 6% of each run, Pallas kernels for 0% -> 27%
where the time goes in v2:
time: 104 us
  Pallas kernels  36.1 us (35%)
  starting transfers between devices  27.2 us (26%)
  waiting for transfers between devices  16.4 us (16%)
  local copies, waits for them, and re-layouts  14.2 us (14%)
  between operations  6.66 us (6%)
  other arithmetic  3.44 us (3%)
    pallas_call x5, Pallas kernels, contract(): pl.pallas_call(kernel, in_specs=specs, out_specs=(ANY if last else VMEM,...  35.7 us
    ppermute x7, starting transfers between devices, shift_ring(): lax.ppermute(value, 'virt', [(v, (v - 2) % virt_size) for v in range(virt...  10.9 us
    unnamed x10, local copies, waits for them, and re-layouts  8.57 us
    ppermute x19, starting transfers between devices, swap_occ(): return lax.ppermute(value, 'occ', [(o, o ^ bit) for o in range(occ_size)])  8.21 us
    ppermute x7, starting transfers between devices, swap_pair(): return lax.ppermute(value, 'virt', [(v, v ^ 1) for v in range(virt_size)])  8.02 us
    ppermute x7, waiting for transfers between devices, shift_ring(): lax.ppermute(value, 'virt', [(v, (v - 2) % virt_size) for v in range(virt...  7.24 us
    ppermute x7, waiting for transfers between devices, swap_pair(): return lax.ppermute(value, 'virt', [(v, v ^ 1) for v in range(virt_size)])  5.82 us
    ppermute x19, waiting for transfers between devices, swap_occ(): return lax.ppermute(value, 'occ', [(o, o ^ bit) for o in range(occ_size)])  3.3 us
  transfers between devices with their start and end apart: 33, of which 9 were waited for; matrix products, arithmetic and copies ran while one was open for 6% of the time, Pallas kernels for 27%

profile of v2, /device:TPU:0, one launch (start us, length us, event | category | flops | bytes accessed | tf_op | source)
XLA Modules:
  0.0 103.9 jit_solution(7591417045508579161)
XLA Ops:
  0.0 1.3 %fusion.3 = (s32[1]{0:T(128)}, s32[1]{0:T(128)}) fusion(s32[2]{0:T(128)} %param.7, s32[]{:T(128)S(6)} %select_n.113, s32[]{:T(128)S(6)} %select_n.115), kind=kLoop, calls=%fused_computation.19 | loop fusion | bytes 24 | tf_op jit(solution)/shard_map/dynamic_slice | solution.py:126
  1.9 1.1 %dynamic-slice_bitcast_fusion = bf16[128,2048]{1,0:T(8,128)(2,1)S(1)} fusion(bf16[12,128,2048]{2,1,0:T(8,128)(2,1)} %param.4, s32[]{:T(128)S(6)} %select_n.123), kind=kLoop, calls=%fused_computation.1 | loop fusion | bytes 1048580 | tf_op jit(solution)/shard_map/jit(dynamic_index_in_dim)/squeeze | solution.py:129
  3.0 0.5 collective-permute-start
  5.5 0.8 dynamic_slice.34
  6.3 0.8 fusion
  7.1 0.1 reshape.87
  7.2 0.7 dynamic_slice.35
  7.9 1.1 %bitcast_select_fusion = bf16[128,2048]{1,0:T(8,128)(2,1)S(1)} fusion(bf16[128,2048]{1,0:T(8,128)(2,1)S(1)} %collective-permute-done, bf16[12,128,2048]{2,1,0:T(8,128)(2,1)} %param.4, s32[]{:T(128)S(6)} %select_n.121, pred[]{:T(512)S(6)} %eq.21), kind=kLoop, calls=%fused_computation | loop fusion | flops 262144 | bytes 1572869 | tf_op jit(solution)/shard_map/jit(_where)/select_n | solution.py:130
  9.1 2.6 %collective-permute-start.3 = (bf16[64,2048]{1,0:T(8,128)(2,1)S(1)}, bf16[64,2048]{1,0:T(8,128)(2,1)S(1)}, u32[]{:S(2)}, u32[]{:S(2)}) collective-permute-start(bf16[64,2048]{1,0:T(8,128)(2,1)S(1)} %constant_dynamic-slice_fusion.1), channel_id=1, source_target_pairs={{0,16},{8,24},{16,0},{24,8},{1,17},{9,25},{17,1},{25,9},{2,18},{10... | collective-permute-start | bytes 786440 | tf_op jit(solution)/shard_map/ppermute | solution.py:118
  11.6 0.1 subtract_bitcast_fusion
  15.4 1.3 %fusion.2 = (f32[1]{0:T(128)}, f32[1]{0:T(128)}) fusion(f32[48]{0:T(128)} %param.5, s32[]{:T(128)S(6)} %select_n.114, s32[]{:T(128)S(6)} %select_n.116), kind=kLoop, calls=%fused_computation.18 | loop fusion | bytes 24 | tf_op jit(solution)/shard_map/dynamic_slice | solution.py:152
  16.7 1.9 %collective-permute-done.3 = bf16[64,2048]{1,0:T(8,128)(2,1)S(1)} collective-permute-done((bf16[64,2048]{1,0:T(8,128)(2,1)S(1)}, bf16[64,2048]{1,0:T(8,128)(2,1)S(1)}, u32[]{:S(2)}, u32[]{:S(2)}) %collective-permute-start.3) | collective-permute-done | bytes 262176 | tf_op jit(solution)/shard_map/ppermute | solution.py:118
  18.6 0.1 broadcast_select_fusion
  18.7 1.8 %collective-permute-start.1 = (bf16[64,2048]{1,0:T(8,128)(2,1)S(1)}, bf16[64,2048]{1,0:T(8,128)(2,1)S(1)}, u32[]{:S(2)}, u32[]{:S(2)}) collective-permute-start(bf16[64,2048]{1,0:T(8,128)(2,1)S(1)} %get-tuple-element.52), channel_id=1, source_target_pairs={{0,16},{8,24},{16,0},{24,8},{1,17},{9,25},{17,1},{25,9},{2,18},{10... | collective-permute-start | bytes 786440 | tf_op jit(solution)/shard_map/ppermute | solution.py:118
  20.5 1.3 %pad_maximum_fusion = f32[2]{0:T(128)S(1)} fusion(f32[1]{0:T(128)} %get-tuple-element.59, f32[1]{0:T(128)} %get-tuple-element.58), kind=kLoop, calls=%fused_computation.16 | loop fusion | flops 2 | bytes 16 | tf_op jit(solution)/shard_map/stack | solution.py:152
  21.7 2.8 %copy-done.3 = bf16[12,128,2048]{2,1,0:T(8,128)(2,1)S(1)} copy-done((bf16[12,128,2048]{2,1,0:T(8,128)(2,1)S(1)}, bf16[12,128,2048]{2,1,0:T(8,128)(2,1)}, u32[]{:S(2)}) %copy-start.3) | copy-done | bytes 6291480
  24.5 0.4 shard_map.46.refs_0_.rows_ref
  24.9 0.0 copy-start
  25.0 2.7 %copy-done = bf16[1536,2048]{1,0:T(8,128)(2,1)} copy-done((bf16[1536,2048]{1,0:T(8,128)(2,1)}, bf16[1536,2048]{1,0:T(8,128)(2,1)S(1)}, u32[]{:S(2)}) %copy-start) | copy-done | bytes 6291480
  27.7 0.3 copy.30
  28.0 0.1 sub.72
  28.1 0.1 sub.74
  28.1 0.1 sub.75
  28.2 0.1 collective-permute-start.4
  28.3 0.1 broadcast_select_fusion.1.refs_3_
  28.4 0.0 copy-start.1
  28.4 2.8 %copy-done.1 = bf16[1536,2048]{1,0:T(8,128)(2,1)S(1)} copy-done((bf16[1536,2048]{1,0:T(8,128)(2,1)S(1)}, bf16[1536,2048]{1,0:T(8,128)(2,1)}, u32[]{:S(2)}) %copy-start.1) | copy-done | bytes 6291480
  31.2 0.5 collective-permute-start.2
  31.7 3.6 %collective-permute-start.8 = (bf16[64,2048]{1,0:T(8,128)(2,1)S(1)}, bf16[64,2048]{1,0:T(8,128)(2,1)S(1)}, u32[]{:S(2)}, u32[]{:S(2)}) collective-permute-start(bf16[64,2048]{1,0:T(8,128)(2,1)S(1)} %get-tuple-element.51.rest_2_), channel_id=1, source_target_pairs={{0,6},{1,7},{2,0},{3,1},{4,2},{5,3},{6,4},{7,5},{8,14},{9,15},{10,... | collective-permute-start | bytes 786440 | tf_op jit(solution)/shard_map/ppermute | solution.py:124
  35.3 1.5 %collective-permute-start.9 = (bf16[64,2048]{1,0:T(8,128)(2,1)S(1)}, bf16[64,2048]{1,0:T(8,128)(2,1)S(1)}, u32[]{:S(2)}, u32[]{:S(2)}) collective-permute-start(bf16[64,2048]{1,0:T(8,128)(2,1)S(1)} %get-tuple-element.51.rest_2_), channel_id=1, source_target_pairs={{0,1},{1,0},{2,3},{3,2},{4,5},{5,4},{6,7},{7,6},{8,9},{9,8},{10,11... | collective-permute-start | bytes 786440 | tf_op jit(solution)/shard_map/ppermute | solution.py:121
  36.8 0.4 collective-permute-start.5
  37.2 0.5 collective-permute-start.6
  37.8 5.7 %shard_map.48 = (f32[1536,2048]{1,0:T(8,128)S(1)}, f32[8,128]{1,0:T(8,128)S(1)}) custom-call(bf16[1536,2048]{1,0:T(8,128)(2,1)S(1)} %copy-done.2, f32[1536,1]{1,0:T(8,128)S(1)} %bitcast.24, f32[1,256]{1,0:T(1,128)S(1)} %get-tuple-element.53.block_energy_ref, bf16[64,2048]{1,0:T(8,128)(2,1)S(1)} %shard_map.47.rest_0_, ...), custom_call_target="tpu_custom_call" | custom-call | flops 3221225472 | bytes 1048576 | tf_op jit(solution)/shard_map/pallas_call | solution.py:81
  43.5 3.2 %collective-permute-done.5.refs_1_ = bf16[64,2048]{1,0:T(8,128)(2,1)S(1)} collective-permute-done((bf16[64,2048]{1,0:T(8,128)(2,1)S(1)}, bf16[64,2048]{1,0:T(8,128)(2,1)S(1)}, u32[]{:S(2)}, u32[]{:S(2)}) %collective-permute-start.5) | collective-permute-done | bytes 262176 | tf_op jit(solution)/shard_map/ppermute | solution.py:124
  46.7 2.2 %collective-permute-done.6.refs_2_ = bf16[64,2048]{1,0:T(8,128)(2,1)S(1)} collective-permute-done((bf16[64,2048]{1,0:T(8,128)(2,1)S(1)}, bf16[64,2048]{1,0:T(8,128)(2,1)S(1)}, u32[]{:S(2)}, u32[]{:S(2)}) %collective-permute-start.6) | collective-permute-done | bytes 262176 | tf_op jit(solution)/shard_map/ppermute | solution.py:121
  48.9 0.5 collective-permute-start.10
  49.4 0.1 collective-permute-start.11
  49.5 0.4 collective-permute-start.12
  49.9 2.1 %collective-permute-start.13 = (bf16[64,2048]{1,0:T(8,128)(2,1)S(1)}, bf16[64,2048]{1,0:T(8,128)(2,1)S(1)}, u32[]{:S(2)}, u32[]{:S(2)}) collective-permute-start(bf16[64,2048]{1,0:T(8,128)(2,1)S(1)} %get-tuple-element.31.rest_4_), channel_id=1, source_target_pairs={{0,6},{1,7},{2,0},{3,1},{4,2},{5,3},{6,4},{7,5},{8,14},{9,15},{10,... | collective-permute-start | bytes 786440 | tf_op jit(solution)/shard_map/ppermute | solution.py:124
  52.0 1.5 %collective-permute-start.14 = (bf16[64,2048]{1,0:T(8,128)(2,1)S(1)}, bf16[64,2048]{1,0:T(8,128)(2,1)S(1)}, u32[]{:S(2)}, u32[]{:S(2)}) collective-permute-start(bf16[64,2048]{1,0:T(8,128)(2,1)S(1)} %get-tuple-element.31.rest_4_), channel_id=1, source_target_pairs={{0,1},{1,0},{2,3},{3,2},{4,5},{5,4},{6,7},{7,6},{8,9},{9,8},{10,11... | collective-permute-start | bytes 786440 | tf_op jit(solution)/shard_map/ppermute | solution.py:121
  53.5 0.5 collective-permute-start.16
  54.0 0.5 collective-permute-start.17
  54.5 7.4 %shard_map.51 = (f32[1536,2048]{1,0:T(8,128)S(1)}, f32[8,128]{1,0:T(8,128)S(1)}) custom-call(bf16[1536,2048]{1,0:T(8,128)(2,1)S(1)} %copy-done.2, f32[1536,1]{1,0:T(8,128)S(1)} %bitcast.25, f32[1,512]{1,0:T(1,128)S(1)} %bitcast.31, bf16[64,2048]{1,0:T(8,128)(2,1)S(1)} %get-tuple-element.29.rest_0_, ...), custom_call_target="tpu_custom_call", output_to_operand_aliasing={{0}: (11, {})} | custom-call | flops 6442450944 | bytes 2097152 | tf_op jit(solution)/shard_map/pallas_call | solution.py:81
  61.9 0.1 collective-permute-start.15
  62.0 1.8 %collective-permute-done.16.refs_1_ = bf16[64,2048]{1,0:T(8,128)(2,1)S(1)} collective-permute-done((bf16[64,2048]{1,0:T(8,128)(2,1)S(1)}, bf16[64,2048]{1,0:T(8,128)(2,1)S(1)}, u32[]{:S(2)}, u32[]{:S(2)}) %collective-permute-start.16) | collective-permute-done | bytes 262176 | tf_op jit(solution)/shard_map/ppermute | solution.py:124
  63.8 1.8 %collective-permute-done.17.refs_2_ = bf16[64,2048]{1,0:T(8,128)(2,1)S(1)} collective-permute-done((bf16[64,2048]{1,0:T(8,128)(2,1)S(1)}, bf16[64,2048]{1,0:T(8,128)(2,1)S(1)}, u32[]{:S(2)}, u32[]{:S(2)}) %collective-permute-start.17) | collective-permute-done | bytes 262176 | tf_op jit(solution)/shard_map/ppermute | solution.py:121
  65.6 0.5 collective-permute-start.19
  66.1 2.1 %collective-permute-start.21 = (bf16[64,2048]{1,0:T(8,128)(2,1)S(1)}, bf16[64,2048]{1,0:T(8,128)(2,1)S(1)}, u32[]{:S(2)}, u32[]{:S(2)}) collective-permute-start(bf16[64,2048]{1,0:T(8,128)(2,1)S(1)} %get-tuple-element.37.rest_4_), channel_id=1, source_target_pairs={{0,6},{1,7},{2,0},{3,1},{4,2},{5,3},{6,4},{7,5},{8,14},{9,15},{10,... | collective-permute-start | bytes 786440 | tf_op jit(solution)/shard_map/ppermute | solution.py:124
  68.3 1.5 %collective-permute-start.22 = (bf16[64,2048]{1,0:T(8,128)(2,1)S(1)}, bf16[64,2048]{1,0:T(8,128)(2,1)S(1)}, u32[]{:S(2)}, u32[]{:S(2)}) collective-permute-start(bf16[64,2048]{1,0:T(8,128)(2,1)S(1)} %get-tuple-element.37.rest_4_), channel_id=1, source_target_pairs={{0,1},{1,0},{2,3},{3,2},{4,5},{5,4},{6,7},{7,6},{8,9},{9,8},{10,11... | collective-permute-start | bytes 786440 | tf_op jit(solution)/shard_map/ppermute | solution.py:121
  69.8 0.0 collective-permute-start.24
  69.8 0.9 collective-permute-start.25
  70.8 7.4 %shard_map.54 = (f32[1536,2048]{1,0:T(8,128)S(1)}, f32[8,128]{1,0:T(8,128)S(1)}) custom-call(bf16[1536,2048]{1,0:T(8,128)(2,1)S(1)} %copy-done.2, f32[1536,1]{1,0:T(8,128)S(1)} %bitcast.26, f32[1,512]{1,0:T(1,128)S(1)} %bitcast.30, bf16[64,2048]{1,0:T(8,128)(2,1)S(1)} %get-tuple-element.35.rest_0_, ...), custom_call_target="tpu_custom_call", output_to_operand_aliasing={{0}: (11, {})} | custom-call | flops 6442450944 | bytes 2097152 | tf_op jit(solution)/shard_map/pallas_call | solution.py:81
  78.2 0.1 collective-permute-start.23
  78.3 2.2 %collective-permute-done.24.refs_1_ = bf16[64,2048]{1,0:T(8,128)(2,1)S(1)} collective-permute-done((bf16[64,2048]{1,0:T(8,128)(2,1)S(1)}, bf16[64,2048]{1,0:T(8,128)(2,1)S(1)}, u32[]{:S(2)}, u32[]{:S(2)}) %collective-permute-start.24) | collective-permute-done | bytes 262176 | tf_op jit(solution)/shard_map/ppermute | solution.py:124
  80.5 1.8 %collective-permute-done.25.refs_2_ = bf16[64,2048]{1,0:T(8,128)(2,1)S(1)} collective-permute-done((bf16[64,2048]{1,0:T(8,128)(2,1)S(1)}, bf16[64,2048]{1,0:T(8,128)(2,1)S(1)}, u32[]{:S(2)}, u32[]{:S(2)}) %collective-permute-start.25) | collective-permute-done | bytes 262176 | tf_op jit(solution)/shard_map/ppermute | solution.py:121
  82.3 0.5 collective-permute-start.27
  82.8 1.5 %collective-permute-start.29 = (bf16[64,2048]{1,0:T(8,128)(2,1)S(1)}, bf16[64,2048]{1,0:T(8,128)(2,1)S(1)}, u32[]{:S(2)}, u32[]{:S(2)}) collective-permute-start(bf16[64,2048]{1,0:T(8,128)(2,1)S(1)} %get-tuple-element.43.rest_4_), channel_id=1, source_target_pairs={{0,1},{1,0},{2,3},{3,2},{4,5},{5,4},{6,7},{7,6},{8,9},{9,8},{10,11... | collective-permute-start | bytes 786440 | tf_op jit(solution)/shard_map/ppermute | solution.py:121
  84.3 2.1 %collective-permute-start.30 = (bf16[64,2048]{1,0:T(8,128)(2,1)S(1)}, bf16[64,2048]{1,0:T(8,128)(2,1)S(1)}, u32[]{:S(2)}, u32[]{:S(2)}) collective-permute-start(bf16[64,2048]{1,0:T(8,128)(2,1)S(1)} %get-tuple-element.42.rest_2_), channel_id=1, source_target_pairs={{0,6},{1,7},{2,0},{3,1},{4,2},{5,3},{6,4},{7,5},{8,14},{9,15},{10,... | collective-permute-start | bytes 786440 | tf_op jit(solution)/shard_map/ppermute | solution.py:124
  86.5 7.4 %shard_map.57 = (f32[1536,2048]{1,0:T(8,128)S(1)}, f32[8,128]{1,0:T(8,128)S(1)}) custom-call(bf16[1536,2048]{1,0:T(8,128)(2,1)S(1)} %copy-done.2, f32[1536,1]{1,0:T(8,128)S(1)} %bitcast.27, f32[1,512]{1,0:T(1,128)S(1)} %bitcast.29, bf16[64,2048]{1,0:T(8,128)(2,1)S(1)} %get-tuple-element.41.rest_0_, ...), custom_call_target="tpu_custom_call", output_to_operand_aliasing={{0}: (11, {})} | custom-call | flops 6442450944 | bytes 2097152 | tf_op jit(solution)/shard_map/pallas_call | solution.py:81
  93.9 0.1 collective-permute-start.31
  94.0 0.5 collective-permute-start.32
  94.5 1.0 collective-permute-done.31.rest_1_
  95.5 0.4 collective-permute-done.32.rest_3_
  95.9 7.8 %shard_map.59 = (bf16[1536,2048]{1,0:T(8,128)(2,1)}, f32[8,128]{1,0:T(8,128)}) custom-call(bf16[1536,2048]{1,0:T(8,128)(2,1)S(1)} %copy-done.2, f32[1536,1]{1,0:T(8,128)S(1)} %bitcast.28, f32[1,256]{1,0:T(1,128)S(1)} %get-tuple-element.54.block_energy_ref, bf16[64,2048]{1,0:T(8,128)(2,1)S(1)} %get-tuple-element.47.rest_0_, ...), custom_call_target="tpu_custom_call" | custom-call | flops 3221225472 | bytes 1048576 | tf_op jit(solution)/shard_map/pallas_call | solution.py:81
  (49 shorter events, 0.2 us)
Async XLA Ops:
  3.0 4.9 %collective-permute-start = (bf16[128,2048]{1,0:T(8,128)(2,1)S(1)}, bf16[128,2048]{1,0:T(8,128)(2,1)S(1)}, u32[]{:S(2)}, u32[]{:S(2)}) collective-permute-start(bf16[128,2048]{1,0:T(8,128)(2,1)S(1)} %dynamic-slice_bitcast_fusion), channel_id=1, source_target_pairs={{0,8},{8,0},{16,24},{24,16},{1,9},{9,1},{17,25},{25,17},{2,10},{10... | collective-permute-start | bytes 1572872 | tf_op jit(solution)/shard_map/ppermute | solution.py:118
  9.1 9.5 %collective-permute-start.3 = (bf16[64,2048]{1,0:T(8,128)(2,1)S(1)}, bf16[64,2048]{1,0:T(8,128)(2,1)S(1)}, u32[]{:S(2)}, u32[]{:S(2)}) collective-permute-start(bf16[64,2048]{1,0:T(8,128)(2,1)S(1)} %constant_dynamic-slice_fusion.1), channel_id=1, source_target_pairs={{0,16},{8,24},{16,0},{24,8},{1,17},{9,25},{17,1},{25,9},{2,18},{10... | collective-permute-start | bytes 786440 | tf_op jit(solution)/shard_map/ppermute | solution.py:118
  18.7 9.7 %collective-permute-start.1 = (bf16[64,2048]{1,0:T(8,128)(2,1)S(1)}, bf16[64,2048]{1,0:T(8,128)(2,1)S(1)}, u32[]{:S(2)}, u32[]{:S(2)}) collective-permute-start(bf16[64,2048]{1,0:T(8,128)(2,1)S(1)} %get-tuple-element.52), channel_id=1, source_target_pairs={{0,16},{8,24},{16,0},{24,8},{1,17},{9,25},{17,1},{25,9},{2,18},{10... | collective-permute-start | bytes 786440 | tf_op jit(solution)/shard_map/ppermute | solution.py:118
  21.7 2.8 %copy-start.3 = (bf16[12,128,2048]{2,1,0:T(8,128)(2,1)S(1)}, bf16[12,128,2048]{2,1,0:T(8,128)(2,1)}, u32[]{:S(2)}) copy-start(bf16[12,128,2048]{2,1,0:T(8,128)(2,1)} %param.4) | copy-start | bytes 18874372
  24.9 2.7 %copy-start = (bf16[1536,2048]{1,0:T(8,128)(2,1)}, bf16[1536,2048]{1,0:T(8,128)(2,1)S(1)}, u32[]{:S(2)}) copy-start(bf16[1536,2048]{1,0:T(8,128)(2,1)S(1)} %shard_map.46.refs_0_.rows_ref) | copy-start | bytes 18874372
  28.2 9.0 %collective-permute-start.4 = (bf16[64,2048]{1,0:T(8,128)(2,1)S(1)}, bf16[64,2048]{1,0:T(8,128)(2,1)S(1)}, u32[]{:S(2)}, u32[]{:S(2)}) collective-permute-start(bf16[64,2048]{1,0:T(8,128)(2,1)S(1)} %get-tuple-element.51.rest_2_), channel_id=1, source_target_pairs={{0,8},{8,0},{16,24},{24,16},{1,9},{9,1},{17,25},{25,17},{2,10},{10... | collective-permute-start | bytes 786440 | tf_op jit(solution)/shard_map/ppermute | solution.py:118
  28.4 2.8 %copy-start.1 = (bf16[1536,2048]{1,0:T(8,128)(2,1)S(1)}, bf16[1536,2048]{1,0:T(8,128)(2,1)}, u32[]{:S(2)}) copy-start(bf16[1536,2048]{1,0:T(8,128)(2,1)} %copy-done) | copy-start | bytes 18874372
  31.2 6.6 %copy-start.2 = (bf16[1536,2048]{1,0:T(8,128)(2,1)S(1)}, bf16[1536,2048]{1,0:T(8,128)(2,1)}, u32[]{:S(2)}) copy-start(bf16[1536,2048]{1,0:T(8,128)(2,1)} %copy-done) | copy-start | bytes 18874372
  31.2 6.6 %collective-permute-start.2 = (bf16[64,2048]{1,0:T(8,128)(2,1)S(1)}, bf16[64,2048]{1,0:T(8,128)(2,1)S(1)}, u32[]{:S(2)}, u32[]{:S(2)}) collective-permute-start(bf16[64,2048]{1,0:T(8,128)(2,1)S(1)} %shard_map.47.rest_0_), channel_id=1, source_target_pairs={{0,8},{8,0},{16,24},{24,16},{1,9},{9,1},{17,25},{25,17},{2,10},{10... | collective-permute-start | bytes 786440 | tf_op jit(solution)/shard_map/ppermute | solution.py:118
  31.7 17.2 %collective-permute-start.8 = (bf16[64,2048]{1,0:T(8,128)(2,1)S(1)}, bf16[64,2048]{1,0:T(8,128)(2,1)S(1)}, u32[]{:S(2)}, u32[]{:S(2)}) collective-permute-start(bf16[64,2048]{1,0:T(8,128)(2,1)S(1)} %get-tuple-element.51.rest_2_), channel_id=1, source_target_pairs={{0,6},{1,7},{2,0},{3,1},{4,2},{5,3},{6,4},{7,5},{8,14},{9,15},{10,... | collective-permute-start | bytes 786440 | tf_op jit(solution)/shard_map/ppermute | solution.py:124
  35.3 13.6 %collective-permute-start.9 = (bf16[64,2048]{1,0:T(8,128)(2,1)S(1)}, bf16[64,2048]{1,0:T(8,128)(2,1)S(1)}, u32[]{:S(2)}, u32[]{:S(2)}) collective-permute-start(bf16[64,2048]{1,0:T(8,128)(2,1)S(1)} %get-tuple-element.51.rest_2_), channel_id=1, source_target_pairs={{0,1},{1,0},{2,3},{3,2},{4,5},{5,4},{6,7},{7,6},{8,9},{9,8},{10,11... | collective-permute-start | bytes 786440 | tf_op jit(solution)/shard_map/ppermute | solution.py:121
  36.8 9.9 %collective-permute-start.5 = (bf16[64,2048]{1,0:T(8,128)(2,1)S(1)}, bf16[64,2048]{1,0:T(8,128)(2,1)S(1)}, u32[]{:S(2)}, u32[]{:S(2)}) collective-permute-start(bf16[64,2048]{1,0:T(8,128)(2,1)S(1)} %shard_map.47.rest_0_), channel_id=1, source_target_pairs={{0,6},{1,7},{2,0},{3,1},{4,2},{5,3},{6,4},{7,5},{8,14},{9,15},{10,... | collective-permute-start | bytes 786440 | tf_op jit(solution)/shard_map/ppermute | solution.py:124
  37.2 11.6 %collective-permute-start.6 = (bf16[64,2048]{1,0:T(8,128)(2,1)S(1)}, bf16[64,2048]{1,0:T(8,128)(2,1)S(1)}, u32[]{:S(2)}, u32[]{:S(2)}) collective-permute-start(bf16[64,2048]{1,0:T(8,128)(2,1)S(1)} %shard_map.47.rest_0_), channel_id=1, source_target_pairs={{0,1},{1,0},{2,3},{3,2},{4,5},{5,4},{6,7},{7,6},{8,9},{9,8},{10,11... | collective-permute-start | bytes 786440 | tf_op jit(solution)/shard_map/ppermute | solution.py:121
  48.9 3.1 %collective-permute-start.7 = (bf16[64,2048]{1,0:T(8,128)(2,1)S(1)}, bf16[64,2048]{1,0:T(8,128)(2,1)S(1)}, u32[]{:S(2)}, u32[]{:S(2)}) collective-permute-start(bf16[64,2048]{1,0:T(8,128)(2,1)S(1)} %get-tuple-element.29.rest_0_), channel_id=1, source_target_pairs={{0,8},{8,0},{16,24},{24,16},{1,9},{9,1},{17,25},{25,17},{2,10},{10... | collective-permute-start | bytes 786440 | tf_op jit(solution)/shard_map/ppermute | solution.py:118
  48.9 4.6 %collective-permute-start.10 = (bf16[64,2048]{1,0:T(8,128)(2,1)S(1)}, bf16[64,2048]{1,0:T(8,128)(2,1)S(1)}, u32[]{:S(2)}, u32[]{:S(2)}) collective-permute-start(bf16[64,2048]{1,0:T(8,128)(2,1)S(1)} %get-tuple-element.30.rest_2_), channel_id=1, source_target_pairs={{0,8},{8,0},{16,24},{24,16},{1,9},{9,1},{17,25},{25,17},{2,10},{10... | collective-permute-start | bytes 786440 | tf_op jit(solution)/shard_map/ppermute | solution.py:118
  49.4 4.6 %collective-permute-start.11 = (bf16[64,2048]{1,0:T(8,128)(2,1)S(1)}, bf16[64,2048]{1,0:T(8,128)(2,1)S(1)}, u32[]{:S(2)}, u32[]{:S(2)}) collective-permute-start(bf16[64,2048]{1,0:T(8,128)(2,1)S(1)} %get-tuple-element.31.rest_4_), channel_id=1, source_target_pairs={{0,8},{8,0},{16,24},{24,16},{1,9},{9,1},{17,25},{25,17},{2,10},{10... | collective-permute-start | bytes 786440 | tf_op jit(solution)/shard_map/ppermute | solution.py:118
  49.5 5.1 %collective-permute-start.12 = (bf16[64,2048]{1,0:T(8,128)(2,1)S(1)}, bf16[64,2048]{1,0:T(8,128)(2,1)S(1)}, u32[]{:S(2)}, u32[]{:S(2)}) collective-permute-start(bf16[64,2048]{1,0:T(8,128)(2,1)S(1)} %get-tuple-element.32.rest_6_), channel_id=1, source_target_pairs={{0,8},{8,0},{16,24},{24,16},{1,9},{9,1},{17,25},{25,17},{2,10},{10... | collective-permute-start | bytes 786440 | tf_op jit(solution)/shard_map/ppermute | solution.py:118
  49.9 12.0 %collective-permute-start.13 = (bf16[64,2048]{1,0:T(8,128)(2,1)S(1)}, bf16[64,2048]{1,0:T(8,128)(2,1)S(1)}, u32[]{:S(2)}, u32[]{:S(2)}) collective-permute-start(bf16[64,2048]{1,0:T(8,128)(2,1)S(1)} %get-tuple-element.31.rest_4_), channel_id=1, source_target_pairs={{0,6},{1,7},{2,0},{3,1},{4,2},{5,3},{6,4},{7,5},{8,14},{9,15},{10,... | collective-permute-start | bytes 786440 | tf_op jit(solution)/shard_map/ppermute | solution.py:124
  52.0 9.9 %collective-permute-start.14 = (bf16[64,2048]{1,0:T(8,128)(2,1)S(1)}, bf16[64,2048]{1,0:T(8,128)(2,1)S(1)}, u32[]{:S(2)}, u32[]{:S(2)}) collective-permute-start(bf16[64,2048]{1,0:T(8,128)(2,1)S(1)} %get-tuple-element.31.rest_4_), channel_id=1, source_target_pairs={{0,1},{1,0},{2,3},{3,2},{4,5},{5,4},{6,7},{7,6},{8,9},{9,8},{10,11... | collective-permute-start | bytes 786440 | tf_op jit(solution)/shard_map/ppermute | solution.py:121
  53.5 10.3 %collective-permute-start.16 = (bf16[64,2048]{1,0:T(8,128)(2,1)S(1)}, bf16[64,2048]{1,0:T(8,128)(2,1)S(1)}, u32[]{:S(2)}, u32[]{:S(2)}) collective-permute-start(bf16[64,2048]{1,0:T(8,128)(2,1)S(1)} %get-tuple-element.32.rest_6_), channel_id=1, source_target_pairs={{0,6},{1,7},{2,0},{3,1},{4,2},{5,3},{6,4},{7,5},{8,14},{9,15},{10,... | collective-permute-start | bytes 786440 | tf_op jit(solution)/shard_map/ppermute | solution.py:124
  54.0 11.6 %collective-permute-start.17 = (bf16[64,2048]{1,0:T(8,128)(2,1)S(1)}, bf16[64,2048]{1,0:T(8,128)(2,1)S(1)}, u32[]{:S(2)}, u32[]{:S(2)}) collective-permute-start(bf16[64,2048]{1,0:T(8,128)(2,1)S(1)} %get-tuple-element.32.rest_6_), channel_id=1, source_target_pairs={{0,1},{1,0},{2,3},{3,2},{4,5},{5,4},{6,7},{7,6},{8,9},{9,8},{10,11... | collective-permute-start | bytes 786440 | tf_op jit(solution)/shard_map/ppermute | solution.py:121
  61.9 6.3 %collective-permute-start.15 = (bf16[64,2048]{1,0:T(8,128)(2,1)S(1)}, bf16[64,2048]{1,0:T(8,128)(2,1)S(1)}, u32[]{:S(2)}, u32[]{:S(2)}) collective-permute-start(bf16[64,2048]{1,0:T(8,128)(2,1)S(1)} %get-tuple-element.35.rest_0_), channel_id=1, source_target_pairs={{0,8},{8,0},{16,24},{24,16},{1,9},{9,1},{17,25},{25,17},{2,10},{10... | collective-permute-start | bytes 786440 | tf_op jit(solution)/shard_map/ppermute | solution.py:118
  65.6 4.2 %collective-permute-start.18 = (bf16[64,2048]{1,0:T(8,128)(2,1)S(1)}, bf16[64,2048]{1,0:T(8,128)(2,1)S(1)}, u32[]{:S(2)}, u32[]{:S(2)}) collective-permute-start(bf16[64,2048]{1,0:T(8,128)(2,1)S(1)} %get-tuple-element.36.rest_2_), channel_id=1, source_target_pairs={{0,8},{8,0},{16,24},{24,16},{1,9},{9,1},{17,25},{25,17},{2,10},{10... | collective-permute-start | bytes 786440 | tf_op jit(solution)/shard_map/ppermute | solution.py:118
  65.6 4.2 %collective-permute-start.19 = (bf16[64,2048]{1,0:T(8,128)(2,1)S(1)}, bf16[64,2048]{1,0:T(8,128)(2,1)S(1)}, u32[]{:S(2)}, u32[]{:S(2)}) collective-permute-start(bf16[64,2048]{1,0:T(8,128)(2,1)S(1)} %get-tuple-element.37.rest_4_), channel_id=1, source_target_pairs={{0,8},{8,0},{16,24},{24,16},{1,9},{9,1},{17,25},{25,17},{2,10},{10... | collective-permute-start | bytes 786440 | tf_op jit(solution)/shard_map/ppermute | solution.py:118
  66.1 4.6 %collective-permute-start.20 = (bf16[64,2048]{1,0:T(8,128)(2,1)S(1)}, bf16[64,2048]{1,0:T(8,128)(2,1)S(1)}, u32[]{:S(2)}, u32[]{:S(2)}) collective-permute-start(bf16[64,2048]{1,0:T(8,128)(2,1)S(1)} %get-tuple-element.38.rest_6_), channel_id=1, source_target_pairs={{0,8},{8,0},{16,24},{24,16},{1,9},{9,1},{17,25},{25,17},{2,10},{10... | collective-permute-start | bytes 786440 | tf_op jit(solution)/shard_map/ppermute | solution.py:118
  66.1 12.0 %collective-permute-start.21 = (bf16[64,2048]{1,0:T(8,128)(2,1)S(1)}, bf16[64,2048]{1,0:T(8,128)(2,1)S(1)}, u32[]{:S(2)}, u32[]{:S(2)}) collective-permute-start(bf16[64,2048]{1,0:T(8,128)(2,1)S(1)} %get-tuple-element.37.rest_4_), channel_id=1, source_target_pairs={{0,6},{1,7},{2,0},{3,1},{4,2},{5,3},{6,4},{7,5},{8,14},{9,15},{10,... | collective-permute-start | bytes 786440 | tf_op jit(solution)/shard_map/ppermute | solution.py:124
  68.3 9.9 %collective-permute-start.22 = (bf16[64,2048]{1,0:T(8,128)(2,1)S(1)}, bf16[64,2048]{1,0:T(8,128)(2,1)S(1)}, u32[]{:S(2)}, u32[]{:S(2)}) collective-permute-start(bf16[64,2048]{1,0:T(8,128)(2,1)S(1)} %get-tuple-element.37.rest_4_), channel_id=1, source_target_pairs={{0,1},{1,0},{2,3},{3,2},{4,5},{5,4},{6,7},{7,6},{8,9},{9,8},{10,11... | collective-permute-start | bytes 786440 | tf_op jit(solution)/shard_map/ppermute | solution.py:121
  69.8 10.7 %collective-permute-start.24 = (bf16[64,2048]{1,0:T(8,128)(2,1)S(1)}, bf16[64,2048]{1,0:T(8,128)(2,1)S(1)}, u32[]{:S(2)}, u32[]{:S(2)}) collective-permute-start(bf16[64,2048]{1,0:T(8,128)(2,1)S(1)} %get-tuple-element.38.rest_6_), channel_id=1, source_target_pairs={{0,6},{1,7},{2,0},{3,1},{4,2},{5,3},{6,4},{7,5},{8,14},{9,15},{10,... | collective-permute-start | bytes 786440 | tf_op jit(solution)/shard_map/ppermute | solution.py:124
  69.8 12.4 %collective-permute-start.25 = (bf16[64,2048]{1,0:T(8,128)(2,1)S(1)}, bf16[64,2048]{1,0:T(8,128)(2,1)S(1)}, u32[]{:S(2)}, u32[]{:S(2)}) collective-permute-start(bf16[64,2048]{1,0:T(8,128)(2,1)S(1)} %get-tuple-element.38.rest_6_), channel_id=1, source_target_pairs={{0,1},{1,0},{2,3},{3,2},{4,5},{5,4},{6,7},{7,6},{8,9},{9,8},{10,11... | collective-permute-start | bytes 786440 | tf_op jit(solution)/shard_map/ppermute | solution.py:121
  78.2 6.1 %collective-permute-start.23 = (bf16[64,2048]{1,0:T(8,128)(2,1)S(1)}, bf16[64,2048]{1,0:T(8,128)(2,1)S(1)}, u32[]{:S(2)}, u32[]{:S(2)}) collective-permute-start(bf16[64,2048]{1,0:T(8,128)(2,1)S(1)} %get-tuple-element.41.rest_0_), channel_id=1, source_target_pairs={{0,8},{8,0},{16,24},{24,16},{1,9},{9,1},{17,25},{25,17},{2,10},{10... | collective-permute-start | bytes 786440 | tf_op jit(solution)/shard_map/ppermute | solution.py:118
  82.3 4.2 %collective-permute-start.26 = (bf16[64,2048]{1,0:T(8,128)(2,1)S(1)}, bf16[64,2048]{1,0:T(8,128)(2,1)S(1)}, u32[]{:S(2)}, u32[]{:S(2)}) collective-permute-start(bf16[64,2048]{1,0:T(8,128)(2,1)S(1)} %get-tuple-element.42.rest_2_), channel_id=1, source_target_pairs={{0,8},{8,0},{16,24},{24,16},{1,9},{9,1},{17,25},{25,17},{2,10},{10... | collective-permute-start | bytes 786440 | tf_op jit(solution)/shard_map/ppermute | solution.py:118
  82.3 4.2 %collective-permute-start.27 = (bf16[64,2048]{1,0:T(8,128)(2,1)S(1)}, bf16[64,2048]{1,0:T(8,128)(2,1)S(1)}, u32[]{:S(2)}, u32[]{:S(2)}) collective-permute-start(bf16[64,2048]{1,0:T(8,128)(2,1)S(1)} %get-tuple-element.43.rest_4_), channel_id=1, source_target_pairs={{0,8},{8,0},{16,24},{24,16},{1,9},{9,1},{17,25},{25,17},{2,10},{10... | collective-permute-start | bytes 786440 | tf_op jit(solution)/shard_map/ppermute | solution.py:118
  82.8 3.7 %collective-permute-start.28 = (bf16[64,2048]{1,0:T(8,128)(2,1)S(1)}, bf16[64,2048]{1,0:T(8,128)(2,1)S(1)}, u32[]{:S(2)}, u32[]{:S(2)}) collective-permute-start(bf16[64,2048]{1,0:T(8,128)(2,1)S(1)} %get-tuple-element.44.rest_6_), channel_id=1, source_target_pairs={{0,8},{8,0},{16,24},{24,16},{1,9},{9,1},{17,25},{25,17},{2,10},{10... | collective-permute-start | bytes 786440 | tf_op jit(solution)/shard_map/ppermute | solution.py:118
  82.8 11.1 %collective-permute-start.29 = (bf16[64,2048]{1,0:T(8,128)(2,1)S(1)}, bf16[64,2048]{1,0:T(8,128)(2,1)S(1)}, u32[]{:S(2)}, u32[]{:S(2)}) collective-permute-start(bf16[64,2048]{1,0:T(8,128)(2,1)S(1)} %get-tuple-element.43.rest_4_), channel_id=1, source_target_pairs={{0,1},{1,0},{2,3},{3,2},{4,5},{5,4},{6,7},{7,6},{8,9},{9,8},{10,11... | collective-permute-start | bytes 786440 | tf_op jit(solution)/shard_map/ppermute | solution.py:121
  84.3 9.6 %collective-permute-start.30 = (bf16[64,2048]{1,0:T(8,128)(2,1)S(1)}, bf16[64,2048]{1,0:T(8,128)(2,1)S(1)}, u32[]{:S(2)}, u32[]{:S(2)}) collective-permute-start(bf16[64,2048]{1,0:T(8,128)(2,1)S(1)} %get-tuple-element.42.rest_2_), channel_id=1, source_target_pairs={{0,6},{1,7},{2,0},{3,1},{4,2},{5,3},{6,4},{7,5},{8,14},{9,15},{10,... | collective-permute-start | bytes 786440 | tf_op jit(solution)/shard_map/ppermute | solution.py:124
  93.9 1.6 %collective-permute-start.31 = (bf16[64,2048]{1,0:T(8,128)(2,1)S(1)}, bf16[64,2048]{1,0:T(8,128)(2,1)S(1)}, u32[]{:S(2)}, u32[]{:S(2)}) collective-permute-start(bf16[64,2048]{1,0:T(8,128)(2,1)S(1)} %get-tuple-element.47.rest_0_), channel_id=1, source_target_pairs={{0,8},{8,0},{16,24},{24,16},{1,9},{9,1},{17,25},{25,17},{2,10},{10... | collective-permute-start | bytes 786440 | tf_op jit(solution)/shard_map/ppermute | solution.py:118
  94.0 1.9 %collective-permute-start.32 = (bf16[64,2048]{1,0:T(8,128)(2,1)S(1)}, bf16[64,2048]{1,0:T(8,128)(2,1)S(1)}, u32[]{:S(2)}, u32[]{:S(2)}) collective-permute-start(bf16[64,2048]{1,0:T(8,128)(2,1)S(1)} %get-tuple-element.48.rest_2_), channel_id=1, source_target_pairs={{0,8},{8,0},{16,24},{24,16},{1,9},{9,1},{17,25},{25,17},{2,10},{10... | collective-permute-start | bytes 786440 | tf_op jit(solution)/shard_map/ppermute | solution.py:118

commit v3 on v2

v3 whole, which is shorter than its diff:
```python
import jax
import jax.numpy as jnp
from jax import lax
from jax.experimental import pallas as pl
from jax.experimental.pallas import tpu as pltpu
from jax.sharding import PartitionSpec as P

FIRST, SECOND, WHOLE = range(3)

VMEM = pl.BlockSpec(memory_space=pltpu.VMEM)
SMEM = pl.BlockSpec(memory_space=pltpu.SMEM)
ANY = pl.BlockSpec(memory_space=pl.ANY)
TOKEN = jax.ShapeDtypeStruct((8, 128), jnp.float32)


def call(kernel, operands, in_specs, outs, scratch=(), aliases=None, vmem=2):
    return pl.pallas_call(
        kernel,
        in_specs=in_specs,
        out_specs=[spec for spec, _ in outs],
        out_shape=[shape for _, shape in outs],
        scratch_shapes=list(scratch),
        input_output_aliases=aliases or {},
        compiler_params=pltpu.CompilerParams(vmem_limit_bytes=vmem << 20),
        cost_estimate=pl.CostEstimate(flops=0, bytes_accessed=0, transcendentals=0),
    )(*operands)


def extract(partners, integrals):
    occ_dev = integrals.shape[0]
    shape = pltpu.VMEM(integrals.shape[1:], integrals.dtype)

    def kernel(partners_ref, integrals_ref, own_ref, sent_ref, sems):
        core = lax.rem(lax.axis_index("occ"), 2)
        copies = []
        for k, (out_ref, step) in enumerate(((sent_ref, 1 - core), (own_ref, core))):
            row = lax.rem(partners_ref[step], occ_dev)
            copies.append(pltpu.make_async_copy(integrals_ref.at[row], out_ref, sems.at[k]))
        for copy in copies:
            copy.start()
        for copy in copies:
            copy.wait()

    return call(
        kernel,
        [partners, integrals],
        [SMEM, ANY],
        [(VMEM, shape)] * 2,
        [pltpu.SemaphoreType.DMA((2,))],
        vmem=56,
    )


def choose(where, partners, occ_dev, bit, own, got, token=None):
    height, width = own.shape
    half = height // 2
    outs = [(ANY, jax.ShapeDtypeStruct(own.shape, own.dtype))]
    if token is not None:
        outs.append((ANY, jax.ShapeDtypeStruct((half, width), own.dtype)))

    def kernel(where_ref, partners_ref, own_ref, got_ref, *rest):
        out_refs, sems = rest[-1 - len(outs) : -1], rest[-1]
        occ_index = where_ref[1]
        owner = lax.div(partners_ref[lax.rem(occ_index, 2)], occ_dev)
        held = lax.div(owner, bit) == lax.div(occ_index, bit)
        plane = lax.rem(lax.div(occ_index, 2), 2)

        def copy_from(source_ref):
            copies = [pltpu.make_async_copy(source_ref, out_refs[0], sems.at[0])]
            if token is not None:
                source = source_ref.at[pl.ds(pl.multiple_of(plane * half, half), half)]
                copies.append(pltpu.make_async_copy(source, out_refs[1], sems.at[1]))
            for copy in copies:
                copy.start()
            for copy in copies:
                copy.wait()

        pl.when(held)(lambda: copy_from(own_ref))
        pl.when(jnp.logical_not(held))(lambda: copy_from(got_ref))

    operands, specs = [where, partners, own, got], [SMEM, SMEM, ANY, ANY]
    if token is not None:
        operands.append(token)
        specs.append(ANY)
    return call(kernel, operands, specs, outs, [pltpu.SemaphoreType.DMA((2,))], vmem=48 if token is None else 2)


def prepare(where, partners, occ_energy, column, virt_halves, rows, groups, ready):
    height = rows.shape[0]
    local_virt, half = column.shape[0], virt_halves.shape[1]
    occ_dev, virt_size = height // local_virt, virt_halves.shape[0] // 2
    widths = [sum(half * (2 if which == WHOLE else 1) for _, _, which, _ in places) for places in groups]

    def kernel(where_ref, partners_ref, occ_energy_ref, column_ref, virt_ref, rows_ref, *rest):
        rest = rest[1:]
        out_ref, row_energy_ref, token_ref = rest[:3]
        energy_refs, sem = rest[3:-1], rest[-1]
        load = pltpu.make_async_copy(rows_ref, out_ref, sem)
        load.start()
        virt_index, occ_index = where_ref[0], where_ref[1]
        plane = lax.rem(lax.div(occ_index, 2), 2)
        token_ref[...] = jnp.zeros_like(token_ref)
        for i in range(occ_dev):
            own = occ_energy_ref[occ_index * occ_dev + i]
            row_energy_ref[pl.ds(i * local_virt, local_virt), :] = column_ref[...] - own
        for places, energy_ref in zip(groups, energy_refs):
            start = 0
            for ring_step, side, which, step in places:
                position = lax.rem(virt_index + 2 * ring_step, virt_size)
                position = position + side * (1 - 2 * lax.rem(position, 2))
                pair = occ_energy_ref[partners_ref[lax.rem(occ_index + step, 2)]]
                for part in {FIRST: [plane], SECOND: [1 - plane], WHOLE: [0, 1]}[which]:
                    energy_ref[:, start : start + half] = virt_ref[pl.ds(2 * position + part, 1), :] - pair
                    start += half
        load.wait()

    outs = [(VMEM, pltpu.VMEM(rows.shape, rows.dtype)), (VMEM, pltpu.VMEM((height, 1), jnp.float32)), (VMEM, TOKEN)]
    outs += [(VMEM, pltpu.VMEM((1, width), jnp.float32)) for width in widths]
    rows, row_energy, token, *energies = call(
        kernel,
        [where, partners, occ_energy, column, virt_halves, rows, ready],
        [SMEM] * 3 + [VMEM] * 2 + [ANY] * 2,
        outs,
        [pltpu.SemaphoreType.DMA],
        vmem=16,
    )
    return rows, row_energy, token, energies


def contract(rows, row_energy, block_energy, blocks, total, last):
    height, width = rows.shape
    count, depths = len(blocks), [block.shape[0] for block in blocks]
    starts, depth = [sum(depths[:k]) for k in range(count)], sum(depths)
    tile = max(t for t in range(16, 513, 16) if height % t == 0)
    tiles = height // tile

    def kernel(rows_ref, row_energy_ref, block_energy_ref, *rest):
        block_refs, rest = rest[:count], rest[count:]
        total_ref, rest = (rest[0], rest[1:]) if total is not None else (None, rest)
        out_ref, token_ref, held, sems = rest[:4]
        copies = [
            pltpu.make_async_copy(block_refs[k], held.at[pl.ds(starts[k], depths[k])], sems.at[k])
            for k in range(count)
        ]
        for copy in copies:
            copy.start()
        token_ref[...] = jnp.zeros_like(token_ref)
        for copy in copies:
            copy.wait()
        writes = []
        for i in range(tiles):
            at = pl.ds(i * tile, tile)
            scores = lax.dot_general(
                rows_ref[at, :], held[...], (((1,), (1,)), ((), ())), preferred_element_type=jnp.float32
            )
            amplitudes = (scores / (row_energy_ref[at, :] + block_energy_ref[...])).astype(jnp.bfloat16)
            result = jnp.dot(amplitudes, held[...], preferred_element_type=jnp.float32)
            if total_ref is not None:
                result = result + total_ref[at, :]
            if last:
                staged, write_sems = rest[4:]
                if i >= 2:
                    writes[i - 2].wait()
                staged[i % 2] = result.astype(jnp.bfloat16)
                write = pltpu.make_async_copy(staged.at[i % 2], out_ref.at[at, :], write_sems.at[i])
                write.start()
                writes.append(write)
            else:
                out_ref[at, :] = result
        for write in writes[-2:]:
            write.wait()

    operands, specs = [rows, row_energy, block_energy, *blocks], [VMEM] * 3 + [ANY] * count
    if total is not None:
        operands.append(total)
        specs.append(VMEM)
    scratch = [pltpu.VMEM((depth, width), jnp.bfloat16), pltpu.SemaphoreType.DMA((count,))]
    if last:
        scratch += [pltpu.VMEM((2, tile, width), jnp.bfloat16), pltpu.SemaphoreType.DMA((tiles,))]
        out = (ANY, jax.ShapeDtypeStruct((height, width), jnp.bfloat16))
    else:
        out = (VMEM, pltpu.VMEM((height, width), jnp.float32))
    aliases = {3 + count: 0} if total is not None and not last else {}
    return call(kernel, operands, specs, [out, (VMEM, TOKEN)], scratch, aliases, vmem=16)


def gate(tokens, values):
    skip = len(tokens)

    def kernel(*refs):
        del refs

    outs = [(ANY, jax.ShapeDtypeStruct(value.shape, value.dtype)) for value in values]
    aliases = {skip + k: k for k in range(len(values))}
    return call(kernel, [*tokens, *values], [ANY] * (skip + len(values)), outs, aliases=aliases, vmem=1)


def per_device(occ_size, virt_size, integrals, occ_energy, virt_energy, partners):
    occ_dev, local_virt, aux_width = integrals.shape
    occ_index, virt_index = lax.axis_index("occ"), lax.axis_index("virt")
    ring, half = virt_size // 2, local_virt // 2

    def swap_occ(value, bit):
        return lax.ppermute(value, "occ", [(o, o ^ bit) for o in range(occ_size)])

    def swap_pair(value):
        return lax.ppermute(value, "virt", [(v, v ^ 1) for v in range(virt_size)])

    def shift_ring(value, k):
        return lax.ppermute(value, "virt", [(v, (v - 2 * k) % virt_size) for v in range(virt_size)])

    shifts = sorted(range(1, ring), key=lambda k: min(k, ring - k))
    early, late = shifts[: ring // 2], shifts[ring // 2 :]
    even, odd, reach = early[0::2], early[1::2], (len(early) + 1) // 2
    groups = [
        [(0, 0, WHOLE)],
        [(0, 1, WHOLE)] + [(k, 0, FIRST) for k in early],
        [(k, 1, FIRST) for k in even] + [(k, 0, FIRST) for k in late] + [(k, 0, SECOND) for k in early],
        [(k, 0, SECOND) for k in late] + [(k, 1, FIRST) for k in late + odd] + [(k, 1, SECOND) for k in even],
        [(k, 1, SECOND) for k in odd + late],
    ]
    places = [[(*place, step) for place in group for step in range(2)] for group in groups]

    where = jnp.stack([virt_index, occ_index]).astype(jnp.int32)
    column = lax.dynamic_slice_in_dim(virt_energy, virt_index * local_virt, local_virt)[:, None]
    virt_halves = virt_energy.reshape(2 * virt_size, half)
    own, sent = extract(partners, integrals)
    (own,) = choose(where, partners, occ_dev, 1, own, swap_occ(sent, 1))
    rows, row_energy, token, energies = prepare(
        where, partners, occ_energy, column, virt_halves, integrals.reshape(-1, aux_width), places, own
    )
    bit = 2
    while bit < occ_size:
        own, *first_half = choose(where, partners, occ_dev, bit, own, swap_occ(own, bit), token)
        bit *= 2

    blocks = {(0, 0, WHOLE): own, (0, 1, WHOLE): swap_pair(own)}
    for k in early:
        blocks[k, 0, FIRST] = shift_ring(first_half[0], k)
    total = None
    for n, group in enumerate(groups):
        if n > 0:
            for name in group:
                (blocks[name],) = gate([token], [blocks[name]])
        if n == 1:
            for k in early:
                blocks[k, 0, SECOND] = swap_occ(blocks[k, 0, FIRST], 2)
                blocks[k, 1, FIRST] = swap_pair(blocks[k, 0, FIRST])
            for k in late:
                near, step = (k - reach, reach) if k - reach in early else (k + reach, -reach)
                blocks[k, 0, FIRST] = shift_ring(blocks[near, 0, FIRST], step)
        if n == 2:
            for k in odd:
                (blocks[k, 1, FIRST],) = gate([token], [blocks[k, 1, FIRST]])
            for k in late:
                blocks[k, 0, SECOND] = swap_occ(blocks[k, 0, FIRST], 2)
                blocks[k, 1, FIRST] = swap_pair(blocks[k, 0, FIRST])
            for k in even:
                blocks[k, 1, SECOND] = swap_pair(blocks[k, 0, SECOND])
            for k in odd:
                blocks[k, 1, SECOND] = swap_occ(blocks[k, 1, FIRST], 2)
        if n == 3:
            for k in late:
                blocks[k, 1, SECOND] = swap_pair(blocks[k, 0, SECOND])
        pairs = [block for name in group for block in (blocks[name], swap_occ(blocks[name], 1))]
        total, token = contract(rows, row_energy, energies[n], pairs, total, n == len(groups) - 1)
    return total.reshape(integrals.shape)


def solution(mesh):
    in_specs = (P("occ", "virt", None), P(), P(), P())
    out_specs = P("occ", "virt", None)

    def run(integrals, occ_energy, virt_energy, partners):
        return per_device(
            mesh.shape["occ"], mesh.shape["virt"], integrals, occ_energy, virt_energy, partners
        )

    return jax.shard_map(run, mesh=mesh, in_specs=in_specs, out_specs=out_specs, check_vma=False)
```

time: 104 us -> 88.5 us (0.85)
  local copies, waits for them, and re-layouts: 14.2 us -> 6.37 us
  between operations: 6.66 us -> 0.4 us
  Pallas kernels: 36.1 us -> 40.3 us
  other arithmetic: 3.44 us -> 0.07 us
  starting transfers between devices: 27.2 us -> 23.9 us
    ppermute x19 -> x20, waiting for transfers between devices: 3.3 us -> 9.32 us  [swap_occ(): return lax.ppermute(value, 'occ', [(o, o ^ bit) for o in range(occ_size)])]
    ppermute x7 -> x3, waiting for transfers between devices: 7.24 us -> 2.26 us  [shift_ring(): lax.ppermute(value, 'virt', [(v, (v - 2 * k) % virt_size) for v in range(...]
    ppermute x7 -> x3, starting transfers between devices: 10.9 us -> 6.64 us  [shift_ring(): lax.ppermute(value, 'virt', [(v, (v - 2 * k) % virt_size) for v in range(...]
    pallas_call x14 -> x23, Pallas kernels: 36.1 us -> 40.3 us  [call(): pl.pallas_call(kernel, in_specs=in_specs, out_specs=[spec for spec, _ in...]
    dynamic_slice x5 -> x0, local copies, waits for them, and re-layouts: 4.16 us -> none  [the longest x1 1.32 us: per_device(): pair = jnp.stack([occ_energy[mine], occ_energy[other]])]
    unnamed x10 -> x8, local copies, waits for them, and re-layouts: 8.57 us -> 4.75 us
    ppermute x19 -> x20, starting transfers between devices: 8.21 us -> 10.3 us  [swap_occ(): return lax.ppermute(value, 'occ', [(o, o ^ bit) for o in range(occ_size)])]
    select_n x5 -> x0, other arithmetic: 1.25 us -> none  [the longest x1 1.1 us: per_device(): own = jnp.where(owner == occ_index, own, swap_occ(sent, 1))]
  transfers between devices with their start and end apart: 33 -> 29, of which waited for: 9 -> 10; matrix products, arithmetic and copies ran while one was open for 6% -> 2% of each run, Pallas kernels for 27% -> 33%
where the time goes in v3:
time: 88.5 us; the launch traced here: 88.2 us
  Pallas kernels  40.3 us (46%)
  starting transfers between devices  23.9 us (27%)
  waiting for transfers between devices  17.2 us (19%)
  local copies, waits for them, and re-layouts  6.37 us (7%)
    pallas_call x23, Pallas kernels, call(): pl.pallas_call(kernel, in_specs=in_specs, out_specs=[spec for spec, _ in...  40.3 us
    ppermute x20, starting transfers between devices, swap_occ(): return lax.ppermute(value, 'occ', [(o, o ^ bit) for o in range(occ_size)])  10.3 us
    ppermute x20, waiting for transfers between devices, swap_occ(): return lax.ppermute(value, 'occ', [(o, o ^ bit) for o in range(occ_size)])  9.32 us
    ppermute x6, starting transfers between devices, swap_pair(): return lax.ppermute(value, 'virt', [(v, v ^ 1) for v in range(virt_size)])  6.98 us
    ppermute x3, starting transfers between devices, shift_ring(): lax.ppermute(value, 'virt', [(v, (v - 2 * k) % virt_size) for v in range(...  6.64 us
    ppermute x6, waiting for transfers between devices, swap_pair(): return lax.ppermute(value, 'virt', [(v, v ^ 1) for v in range(virt_size)])  5.59 us
    unnamed x8, local copies, waits for them, and re-layouts  4.75 us
    ppermute x3, waiting for transfers between devices, shift_ring(): lax.ppermute(value, 'virt', [(v, (v - 2 * k) % virt_size) for v in range(...  2.26 us
  transfers between devices with their start and end apart: 29, of which 10 were waited for; matrix products, arithmetic and copies ran while one was open for 2% of the time, Pallas kernels for 33%

profile of v3, /device:TPU:0, one launch (start us, length us, event | category | flops | bytes accessed | tf_op | source)
XLA Modules:
  0.0 88.2 jit_solution(13393935292686620603)
XLA Ops:
  0.0 1.9 %shard_map.46 = (bf16[128,2048]{1,0:T(8,128)(2,1)S(1)}, bf16[128,2048]{1,0:T(8,128)(2,1)S(1)}) custom-call(s32[2]{0:T(128)} %partners_ref.7, bf16[12,128,2048]{2,1,0:T(8,128)(2,1)} %integrals_ref.1), custom_call_target="tpu_custom_call" | custom-call | tf_op jit(solution)/shard_map/pallas_call | solution.py:17
  1.9 0.5 collective-permute-start
  2.4 0.1 pad_add_fusion.where_ref
  2.5 1.5 %collective-permute-done.got_ref = bf16[128,2048]{1,0:T(8,128)(2,1)S(1)} collective-permute-done((bf16[128,2048]{1,0:T(8,128)(2,1)S(1)}, bf16[128,2048]{1,0:T(8,128)(2,1)S(1)}, u32[]{:S(2)}, u32[]{:S(2)}) %collective-permute-start) | collective-permute-done | bytes 524320 | tf_op jit(solution)/shard_map/ppermute | solution.py:204
  4.0 0.7 copy-done.1
  4.6 0.6 shard_map.47.rest_0_.own_ref
  5.2 2.9 %collective-permute-start.1 = (bf16[128,2048]{1,0:T(8,128)(2,1)S(1)}, bf16[128,2048]{1,0:T(8,128)(2,1)S(1)}, u32[]{:S(2)}, u32[]{:S(2)}) collective-permute-start(bf16[128,2048]{1,0:T(8,128)(2,1)S(1)} %shard_map.47.rest_0_.own_ref), channel_id=1, source_target_pairs={{0,16},{8,24},{16,0},{24,8},{1,17},{9,25},{17,1},{25,9},{2,18},{10... | collective-permute-start | bytes 1572872 | tf_op jit(solution)/shard_map/ppermute | solution.py:204
  8.2 0.8 reshape.9.virt_ref
  8.9 0.8 dynamic-slice_bitcast_fusion
  9.7 0.1 copy.22.column_ref
  9.8 2.8 %copy-done = bf16[12,128,2048]{2,1,0:T(8,128)(2,1)S(1)} copy-done((bf16[12,128,2048]{2,1,0:T(8,128)(2,1)S(1)}, bf16[12,128,2048]{2,1,0:T(8,128)(2,1)}, u32[]{:S(2)}) %copy-start) | copy-done | bytes 6291480
  12.6 0.7 copy-done.2
  13.2 0.7 copy-done.3
  13.9 1.1 %shard_map.48 = (bf16[1536,2048]{1,0:T(8,128)(2,1)S(1)}, f32[1536,1]{1,0:T(8,128)S(1)}, f32[8,128]{1,0:T(8,128)S(1)}, f32[1,256]{1,0:T(1,128)S(1)}, f32[1,512]{1...) custom-call(s32[2]{0:T(128)S(1)} %pad_add_fusion.where_ref, s32[2]{0:T(128)S(1)} %copy-done.2, ...), custom_call_target="tpu_custom_call" | custom-call | tf_op jit(solution)/shard_map/pallas_call | solution.py:17
  15.0 5.4 %collective-permute-done.1.got_ref = bf16[128,2048]{1,0:T(8,128)(2,1)S(1)} collective-permute-done((bf16[128,2048]{1,0:T(8,128)(2,1)S(1)}, bf16[128,2048]{1,0:T(8,128)(2,1)S(1)}, u32[]{:S(2)}, u32[]{:S(2)}) %collective-permute-start.1) | collective-permute-done | bytes 524320 | tf_op jit(solution)/shard_map/ppermute | solution.py:204
  20.4 0.6 shard_map.49
  21.0 0.1 collective-permute-start.2
  21.1 1.8 %collective-permute-start.3 = (bf16[128,2048]{1,0:T(8,128)(2,1)S(1)}, bf16[128,2048]{1,0:T(8,128)(2,1)S(1)}, u32[]{:S(2)}, u32[]{:S(2)}) collective-permute-start(bf16[128,2048]{1,0:T(8,128)(2,1)S(1)} %get-tuple-element.36.rest_0_), channel_id=1, source_target_pairs={{0,1},{1,0},{2,3},{3,2},{4,5},{5,4},{6,7},{7,6},{8,9},{9,8},{10,11... | collective-permute-start | bytes 1572872 | tf_op jit(solution)/shard_map/ppermute | solution.py:207
  23.0 1.6 %collective-permute-start.7 = (bf16[64,2048]{1,0:T(8,128)(2,1)S(1)}, bf16[64,2048]{1,0:T(8,128)(2,1)S(1)}, u32[]{:S(2)}, u32[]{:S(2)}) collective-permute-start(bf16[64,2048]{1,0:T(8,128)(2,1)S(1)} %get-tuple-element.38), channel_id=1, source_target_pairs={{0,2},{1,3},{2,4},{3,5},{4,6},{5,7},{6,0},{7,1},{8,10},{9,11},{10,... | collective-permute-start | bytes 786440 | tf_op jit(solution)/shard_map/ppermute | solution.py:210
  24.5 2.2 %collective-permute-start.5 = (bf16[64,2048]{1,0:T(8,128)(2,1)S(1)}, bf16[64,2048]{1,0:T(8,128)(2,1)S(1)}, u32[]{:S(2)}, u32[]{:S(2)}) collective-permute-start(bf16[64,2048]{1,0:T(8,128)(2,1)S(1)} %get-tuple-element.38), channel_id=1, source_target_pairs={{0,6},{1,7},{2,0},{3,1},{4,2},{5,3},{6,4},{7,5},{8,14},{9,15},{10,... | collective-permute-start | bytes 786440 | tf_op jit(solution)/shard_map/ppermute | solution.py:210
  26.8 0.0 collective-permute-done.2.rest_1_
  26.8 5.7 %shard_map.50 = (f32[1536,2048]{1,0:T(8,128)S(1)}, f32[8,128]{1,0:T(8,128)S(1)}) custom-call(bf16[1536,2048]{1,0:T(8,128)(2,1)S(1)} %get-tuple-element.28.rows_ref, f32[1536,1]{1,0:T(8,128)S(1)} %get-tuple-element.29.row_energy_ref, f32[1,256]{1,0:T(1,128)S(1)} %get-tuple-element.34.block_energy_ref, bf16[128,2048]{1,0:T(8,128)(2,1)S(1)} %get-tuple-element.36.rest_0_, ...), custom_call_target="tpu_custom_call" | custom-call | tf_op jit(solution)/shard_map/pallas_call | solution.py:17
  32.5 3.0 %collective-permute-done.3.refs_1_ = bf16[128,2048]{1,0:T(8,128)(2,1)S(1)} collective-permute-done((bf16[128,2048]{1,0:T(8,128)(2,1)S(1)}, bf16[128,2048]{1,0:T(8,128)(2,1)S(1)}, u32[]{:S(2)}, u32[]{:S(2)}) %collective-permute-start.3) | collective-permute-done | bytes 524320 | tf_op jit(solution)/shard_map/ppermute | solution.py:207
  35.5 0.0 collective-permute-start.4
  35.5 0.0 collective-permute-done.7.refs_1_
  35.5 0.5 collective-permute-start.8
  36.0 2.3 %collective-permute-done.5.refs_1_ = bf16[64,2048]{1,0:T(8,128)(2,1)S(1)} collective-permute-done((bf16[64,2048]{1,0:T(8,128)(2,1)S(1)}, bf16[64,2048]{1,0:T(8,128)(2,1)S(1)}, u32[]{:S(2)}, u32[]{:S(2)}) %collective-permute-start.5) | collective-permute-done | bytes 262176 | tf_op jit(solution)/shard_map/ppermute | solution.py:210
  38.3 0.0 collective-permute-start.6
  38.3 1.5 %collective-permute-start.15 = (bf16[64,2048]{1,0:T(8,128)(2,1)S(1)}, bf16[64,2048]{1,0:T(8,128)(2,1)S(1)}, u32[]{:S(2)}, u32[]{:S(2)}) collective-permute-start(bf16[64,2048]{1,0:T(8,128)(2,1)S(1)} %shard_map.53.rest_4_), channel_id=1, source_target_pairs={{0,16},{8,24},{16,0},{24,8},{1,17},{9,25},{17,1},{25,9},{2,18},{10... | collective-permute-start | bytes 786440 | tf_op jit(solution)/shard_map/ppermute | solution.py:204
  39.7 0.5 collective-permute-start.13
  40.3 0.0 collective-permute-done.8.rest_5_
  40.3 2.8 %collective-permute-start.11 = (bf16[64,2048]{1,0:T(8,128)(2,1)S(1)}, bf16[64,2048]{1,0:T(8,128)(2,1)S(1)}, u32[]{:S(2)}, u32[]{:S(2)}) collective-permute-start(bf16[64,2048]{1,0:T(8,128)(2,1)S(1)} %shard_map.52.rest_2_), channel_id=1, source_target_pairs={{0,6},{1,7},{2,0},{3,1},{4,2},{5,3},{6,4},{7,5},{8,14},{9,15},{10,... | collective-permute-start | bytes 786440 | tf_op jit(solution)/shard_map/ppermute | solution.py:210
  43.1 0.0 collective-permute-done.6.rest_3_
  43.1 0.5 collective-permute-start.9
  43.6 1.5 %collective-permute-start.21 = (bf16[64,2048]{1,0:T(8,128)(2,1)S(1)}, bf16[64,2048]{1,0:T(8,128)(2,1)S(1)}, u32[]{:S(2)}, u32[]{:S(2)}) collective-permute-start(bf16[64,2048]{1,0:T(8,128)(2,1)S(1)} %shard_map.53.rest_4_), channel_id=1, source_target_pairs={{0,1},{1,0},{2,3},{3,2},{4,5},{5,4},{6,7},{7,6},{8,9},{9,8},{10,11... | collective-permute-start | bytes 786440 | tf_op jit(solution)/shard_map/ppermute | solution.py:207
  45.1 7.4 %shard_map.54 = (f32[1536,2048]{1,0:T(8,128)S(1)}, f32[8,128]{1,0:T(8,128)S(1)}) custom-call(bf16[1536,2048]{1,0:T(8,128)(2,1)S(1)} %get-tuple-element.28.rows_ref, f32[1536,1]{1,0:T(8,128)S(1)} %get-tuple-element.29.row_energy_ref, f32[1,512]{1,0:T(1,128)S(1)} %get-tuple-element.33.block_energy_ref, ...), custom_call_target="tpu_custom_call", output_to_operand_aliasing={{0}: (9, {})} | custom-call | tf_op jit(solution)/shard_map/pallas_call | solution.py:17
  52.5 0.1 collective-permute-start.16
  52.6 0.0 collective-permute-done.13.refs_1_
  52.6 0.5 collective-permute-start.14
  53.1 0.1 collective-permute-start.12
  53.2 0.0 collective-permute-done.9.refs_1_
  53.2 0.4 collective-permute-start.10
  53.6 2.5 %collective-permute-done.21.refs_1_ = bf16[64,2048]{1,0:T(8,128)(2,1)S(1)} collective-permute-done((bf16[64,2048]{1,0:T(8,128)(2,1)S(1)}, bf16[64,2048]{1,0:T(8,128)(2,1)S(1)}, u32[]{:S(2)}, u32[]{:S(2)}) %collective-permute-start.21) | collective-permute-done | bytes 262176 | tf_op jit(solution)/shard_map/ppermute | solution.py:207
  56.2 0.7 collective-permute-start.23
  56.9 0.0 collective-permute-done.16.rest_7_
  56.9 1.5 %collective-permute-start.25 = (bf16[64,2048]{1,0:T(8,128)(2,1)S(1)}, bf16[64,2048]{1,0:T(8,128)(2,1)S(1)}, u32[]{:S(2)}, u32[]{:S(2)}) collective-permute-start(bf16[64,2048]{1,0:T(8,128)(2,1)S(1)} %shard_map.62.refs_1_), channel_id=1, source_target_pairs={{0,16},{8,24},{16,0},{24,8},{1,17},{9,25},{17,1},{25,9},{2,18},{10... | collective-permute-start | bytes 786440 | tf_op jit(solution)/shard_map/ppermute | solution.py:204
  58.4 0.0 collective-permute-done.14.rest_5_
  58.4 1.3 %collective-permute-start.19 = (bf16[64,2048]{1,0:T(8,128)(2,1)S(1)}, bf16[64,2048]{1,0:T(8,128)(2,1)S(1)}, u32[]{:S(2)}, u32[]{:S(2)}) collective-permute-start(bf16[64,2048]{1,0:T(8,128)(2,1)S(1)} %shard_map.56.rest_2_), channel_id=1, source_target_pairs={{0,1},{1,0},{2,3},{3,2},{4,5},{5,4},{6,7},{7,6},{8,9},{9,8},{10,11... | collective-permute-start | bytes 786440 | tf_op jit(solution)/shard_map/ppermute | solution.py:207
  59.7 0.5 collective-permute-start.17
  60.2 0.0 collective-permute-done.10.rest_1_
  60.2 7.4 %shard_map.59 = (f32[1536,2048]{1,0:T(8,128)S(1)}, f32[8,128]{1,0:T(8,128)S(1)}) custom-call(bf16[1536,2048]{1,0:T(8,128)(2,1)S(1)} %get-tuple-element.28.rows_ref, f32[1536,1]{1,0:T(8,128)S(1)} %get-tuple-element.29.row_energy_ref, f32[1,512]{1,0:T(1,128)S(1)} %get-tuple-element.32.block_energy_ref, ...), custom_call_target="tpu_custom_call", output_to_operand_aliasing={{0}: (11, {})} | custom-call | tf_op jit(solution)/shard_map/pallas_call | solution.py:17
  67.7 0.1 collective-permute-start.24
  67.8 0.5 collective-permute-start.22
  68.2 0.1 collective-permute-done.19.refs_1_
  68.3 0.0 collective-permute-start.20
  68.3 0.6 collective-permute-done.17.refs_1_
  69.0 1.1 %collective-permute-start.27 = (bf16[64,2048]{1,0:T(8,128)(2,1)S(1)}, bf16[64,2048]{1,0:T(8,128)(2,1)S(1)}, u32[]{:S(2)}, u32[]{:S(2)}) collective-permute-start(bf16[64,2048]{1,0:T(8,128)(2,1)S(1)} %shard_map.60.rest_0_), channel_id=1, source_target_pairs={{0,1},{1,0},{2,3},{3,2},{4,5},{5,4},{6,7},{7,6},{8,9},{9,8},{10,11... | collective-permute-start | bytes 786440 | tf_op jit(solution)/shard_map/ppermute | solution.py:207
  70.1 0.4 collective-permute-done.18.rest_1_
  70.5 7.6 %shard_map.65 = (f32[1536,2048]{1,0:T(8,128)S(1)}, f32[8,128]{1,0:T(8,128)S(1)}) custom-call(bf16[1536,2048]{1,0:T(8,128)(2,1)S(1)} %get-tuple-element.28.rows_ref, f32[1536,1]{1,0:T(8,128)S(1)} %get-tuple-element.29.row_energy_ref, f32[1,512]{1,0:T(1,128)S(1)} %get-tuple-element.31.block_energy_ref, ...), custom_call_target="tpu_custom_call", output_to_operand_aliasing={{0}: (11, {})} | custom-call | tf_op jit(solution)/shard_map/pallas_call | solution.py:17
  78.2 0.2 collective-permute-start.28
  78.4 0.4 collective-permute-start.26
  78.7 1.0 %collective-permute-done.28.rest_3_ = bf16[64,2048]{1,0:T(8,128)(2,1)S(1)} collective-permute-done((bf16[64,2048]{1,0:T(8,128)(2,1)S(1)}, bf16[64,2048]{1,0:T(8,128)(2,1)S(1)}, u32[]{:S(2)}, u32[]{:S(2)}) %collective-permute-start.28) | collective-permute-done | bytes 262176 | tf_op jit(solution)/shard_map/ppermute | solution.py:204
  79.8 0.4 collective-permute-done.26.rest_1_
  80.1 7.9 %shard_map.68 = (bf16[1536,2048]{1,0:T(8,128)(2,1)}, f32[8,128]{1,0:T(8,128)}) custom-call(bf16[1536,2048]{1,0:T(8,128)(2,1)S(1)} %get-tuple-element.28.rows_ref, f32[1536,1]{1,0:T(8,128)S(1)} %get-tuple-element.29.row_energy_ref, f32[1,256]{1,0:T(1,128)S(1)} %get-tuple-element.30.block_energy_ref, bf16[64,2048]{1,0:T(8,128)(2,1)S(1)} %shard_map.66.rest_0_, ...), custom_call_target="tpu_custom_call" | custom-call | tf_op jit(solution)/shard_map/pallas_call | solution.py:17
  (29 shorter events, 0.1 us)
Async XLA Ops:
  1.9 2.1 %collective-permute-start = (bf16[128,2048]{1,0:T(8,128)(2,1)S(1)}, bf16[128,2048]{1,0:T(8,128)(2,1)S(1)}, u32[]{:S(2)}, u32[]{:S(2)}) collective-permute-start(bf16[128,2048]{1,0:T(8,128)(2,1)S(1)} %get-tuple-element.27), channel_id=1, source_target_pairs={{0,8},{8,0},{16,24},{24,16},{1,9},{9,1},{17,25},{25,17},{2,10},{10... | collective-permute-start | bytes 1572872 | tf_op jit(solution)/shard_map/ppermute | solution.py:204
  4.0 0.7 copy-start.1
  5.2 15.2 %collective-permute-start.1 = (bf16[128,2048]{1,0:T(8,128)(2,1)S(1)}, bf16[128,2048]{1,0:T(8,128)(2,1)S(1)}, u32[]{:S(2)}, u32[]{:S(2)}) collective-permute-start(bf16[128,2048]{1,0:T(8,128)(2,1)S(1)} %shard_map.47.rest_0_.own_ref), channel_id=1, source_target_pairs={{0,16},{8,24},{16,0},{24,8},{1,17},{9,25},{17,1},{25,9},{2,18},{10... | collective-permute-start | bytes 1572872 | tf_op jit(solution)/shard_map/ppermute | solution.py:204
  9.8 2.8 %copy-start = (bf16[12,128,2048]{2,1,0:T(8,128)(2,1)S(1)}, bf16[12,128,2048]{2,1,0:T(8,128)(2,1)}, u32[]{:S(2)}) copy-start(bf16[12,128,2048]{2,1,0:T(8,128)(2,1)} %integrals_ref.1) | copy-start | bytes 18874372
  12.6 0.7 copy-start.2
  13.2 0.7 copy-start.3
  21.0 5.7 %collective-permute-start.2 = (bf16[128,2048]{1,0:T(8,128)(2,1)S(1)}, bf16[128,2048]{1,0:T(8,128)(2,1)S(1)}, u32[]{:S(2)}, u32[]{:S(2)}) collective-permute-start(bf16[128,2048]{1,0:T(8,128)(2,1)S(1)} %get-tuple-element.36.rest_0_), channel_id=1, source_target_pairs={{0,8},{8,0},{16,24},{24,16},{1,9},{9,1},{17,25},{25,17},{2,10},{10... | collective-permute-start | bytes 1572872 | tf_op jit(solution)/shard_map/ppermute | solution.py:204
  21.1 14.4 %collective-permute-start.3 = (bf16[128,2048]{1,0:T(8,128)(2,1)S(1)}, bf16[128,2048]{1,0:T(8,128)(2,1)S(1)}, u32[]{:S(2)}, u32[]{:S(2)}) collective-permute-start(bf16[128,2048]{1,0:T(8,128)(2,1)S(1)} %get-tuple-element.36.rest_0_), channel_id=1, source_target_pairs={{0,1},{1,0},{2,3},{3,2},{4,5},{5,4},{6,7},{7,6},{8,9},{9,8},{10,11... | collective-permute-start | bytes 1572872 | tf_op jit(solution)/shard_map/ppermute | solution.py:207
  23.0 12.5 %collective-permute-start.7 = (bf16[64,2048]{1,0:T(8,128)(2,1)S(1)}, bf16[64,2048]{1,0:T(8,128)(2,1)S(1)}, u32[]{:S(2)}, u32[]{:S(2)}) collective-permute-start(bf16[64,2048]{1,0:T(8,128)(2,1)S(1)} %get-tuple-element.38), channel_id=1, source_target_pairs={{0,2},{1,3},{2,4},{3,5},{4,6},{5,7},{6,0},{7,1},{8,10},{9,11},{10,... | collective-permute-start | bytes 786440 | tf_op jit(solution)/shard_map/ppermute | solution.py:210
  24.5 13.7 %collective-permute-start.5 = (bf16[64,2048]{1,0:T(8,128)(2,1)S(1)}, bf16[64,2048]{1,0:T(8,128)(2,1)S(1)}, u32[]{:S(2)}, u32[]{:S(2)}) collective-permute-start(bf16[64,2048]{1,0:T(8,128)(2,1)S(1)} %get-tuple-element.38), channel_id=1, source_target_pairs={{0,6},{1,7},{2,0},{3,1},{4,2},{5,3},{6,4},{7,5},{8,14},{9,15},{10,... | collective-permute-start | bytes 786440 | tf_op jit(solution)/shard_map/ppermute | solution.py:210
  35.5 8.1 %collective-permute-start.4 = (bf16[128,2048]{1,0:T(8,128)(2,1)S(1)}, bf16[128,2048]{1,0:T(8,128)(2,1)S(1)}, u32[]{:S(2)}, u32[]{:S(2)}) collective-permute-start(bf16[128,2048]{1,0:T(8,128)(2,1)S(1)} %shard_map.51.rest_0_), channel_id=1, source_target_pairs={{0,8},{8,0},{16,24},{24,16},{1,9},{9,1},{17,25},{25,17},{2,10},{10... | collective-permute-start | bytes 1572872 | tf_op jit(solution)/shard_map/ppermute | solution.py:204
  35.5 4.8 %collective-permute-start.8 = (bf16[64,2048]{1,0:T(8,128)(2,1)S(1)}, bf16[64,2048]{1,0:T(8,128)(2,1)S(1)}, u32[]{:S(2)}, u32[]{:S(2)}) collective-permute-start(bf16[64,2048]{1,0:T(8,128)(2,1)S(1)} %shard_map.53.rest_4_), channel_id=1, source_target_pairs={{0,8},{8,0},{16,24},{24,16},{1,9},{9,1},{17,25},{25,17},{2,10},{10... | collective-permute-start | bytes 786440 | tf_op jit(solution)/shard_map/ppermute | solution.py:204
  38.3 4.9 %collective-permute-start.6 = (bf16[64,2048]{1,0:T(8,128)(2,1)S(1)}, bf16[64,2048]{1,0:T(8,128)(2,1)S(1)}, u32[]{:S(2)}, u32[]{:S(2)}) collective-permute-start(bf16[64,2048]{1,0:T(8,128)(2,1)S(1)} %shard_map.52.rest_2_), channel_id=1, source_target_pairs={{0,8},{8,0},{16,24},{24,16},{1,9},{9,1},{17,25},{25,17},{2,10},{10... | collective-permute-start | bytes 786440 | tf_op jit(solution)/shard_map/ppermute | solution.py:204
  38.3 14.3 %collective-permute-start.15 = (bf16[64,2048]{1,0:T(8,128)(2,1)S(1)}, bf16[64,2048]{1,0:T(8,128)(2,1)S(1)}, u32[]{:S(2)}, u32[]{:S(2)}) collective-permute-start(bf16[64,2048]{1,0:T(8,128)(2,1)S(1)} %shard_map.53.rest_4_), channel_id=1, source_target_pairs={{0,16},{8,24},{16,0},{24,8},{1,17},{9,25},{17,1},{25,9},{2,18},{10... | collective-permute-start | bytes 786440 | tf_op jit(solution)/shard_map/ppermute | solution.py:204
  39.7 12.9 %collective-permute-start.13 = (bf16[64,2048]{1,0:T(8,128)(2,1)S(1)}, bf16[64,2048]{1,0:T(8,128)(2,1)S(1)}, u32[]{:S(2)}, u32[]{:S(2)}) collective-permute-start(bf16[64,2048]{1,0:T(8,128)(2,1)S(1)} %shard_map.52.rest_2_), channel_id=1, source_target_pairs={{0,16},{8,24},{16,0},{24,8},{1,17},{9,25},{17,1},{25,9},{2,18},{10... | collective-permute-start | bytes 786440 | tf_op jit(solution)/shard_map/ppermute | solution.py:204
  40.3 12.8 %collective-permute-start.11 = (bf16[64,2048]{1,0:T(8,128)(2,1)S(1)}, bf16[64,2048]{1,0:T(8,128)(2,1)S(1)}, u32[]{:S(2)}, u32[]{:S(2)}) collective-permute-start(bf16[64,2048]{1,0:T(8,128)(2,1)S(1)} %shard_map.52.rest_2_), channel_id=1, source_target_pairs={{0,6},{1,7},{2,0},{3,1},{4,2},{5,3},{6,4},{7,5},{8,14},{9,15},{10,... | collective-permute-start | bytes 786440 | tf_op jit(solution)/shard_map/ppermute | solution.py:210
  43.1 10.1 %collective-permute-start.9 = (bf16[64,2048]{1,0:T(8,128)(2,1)S(1)}, bf16[64,2048]{1,0:T(8,128)(2,1)S(1)}, u32[]{:S(2)}, u32[]{:S(2)}) collective-permute-start(bf16[64,2048]{1,0:T(8,128)(2,1)S(1)} %shard_map.52.rest_2_), channel_id=1, source_target_pairs={{0,1},{1,0},{2,3},{3,2},{4,5},{5,4},{6,7},{7,6},{8,9},{9,8},{10,11... | collective-permute-start | bytes 786440 | tf_op jit(solution)/shard_map/ppermute | solution.py:207
  43.6 12.6 %collective-permute-start.21 = (bf16[64,2048]{1,0:T(8,128)(2,1)S(1)}, bf16[64,2048]{1,0:T(8,128)(2,1)S(1)}, u32[]{:S(2)}, u32[]{:S(2)}) collective-permute-start(bf16[64,2048]{1,0:T(8,128)(2,1)S(1)} %shard_map.53.rest_4_), channel_id=1, source_target_pairs={{0,1},{1,0},{2,3},{3,2},{4,5},{5,4},{6,7},{7,6},{8,9},{9,8},{10,11... | collective-permute-start | bytes 786440 | tf_op jit(solution)/shard_map/ppermute | solution.py:207
  52.5 4.4 %collective-permute-start.16 = (bf16[64,2048]{1,0:T(8,128)(2,1)S(1)}, bf16[64,2048]{1,0:T(8,128)(2,1)S(1)}, u32[]{:S(2)}, u32[]{:S(2)}) collective-permute-start(bf16[64,2048]{1,0:T(8,128)(2,1)S(1)} %shard_map.58.rest_6_), channel_id=1, source_target_pairs={{0,8},{8,0},{16,24},{24,16},{1,9},{9,1},{17,25},{25,17},{2,10},{10... | collective-permute-start | bytes 786440 | tf_op jit(solution)/shard_map/ppermute | solution.py:204
  52.6 5.8 %collective-permute-start.14 = (bf16[64,2048]{1,0:T(8,128)(2,1)S(1)}, bf16[64,2048]{1,0:T(8,128)(2,1)S(1)}, u32[]{:S(2)}, u32[]{:S(2)}) collective-permute-start(bf16[64,2048]{1,0:T(8,128)(2,1)S(1)} %shard_map.57.rest_4_), channel_id=1, source_target_pairs={{0,8},{8,0},{16,24},{24,16},{1,9},{9,1},{17,25},{25,17},{2,10},{10... | collective-permute-start | bytes 786440 | tf_op jit(solution)/shard_map/ppermute | solution.py:204
  53.1 6.6 %collective-permute-start.12 = (bf16[64,2048]{1,0:T(8,128)(2,1)S(1)}, bf16[64,2048]{1,0:T(8,128)(2,1)S(1)}, u32[]{:S(2)}, u32[]{:S(2)}) collective-permute-start(bf16[64,2048]{1,0:T(8,128)(2,1)S(1)} %shard_map.56.rest_2_), channel_id=1, source_target_pairs={{0,8},{8,0},{16,24},{24,16},{1,9},{9,1},{17,25},{25,17},{2,10},{10... | collective-permute-start | bytes 786440 | tf_op jit(solution)/shard_map/ppermute | solution.py:204
  53.2 7.0 %collective-permute-start.10 = (bf16[64,2048]{1,0:T(8,128)(2,1)S(1)}, bf16[64,2048]{1,0:T(8,128)(2,1)S(1)}, u32[]{:S(2)}, u32[]{:S(2)}) collective-permute-start(bf16[64,2048]{1,0:T(8,128)(2,1)S(1)} %shard_map.55.rest_0_), channel_id=1, source_target_pairs={{0,8},{8,0},{16,24},{24,16},{1,9},{9,1},{17,25},{25,17},{2,10},{10... | collective-permute-start | bytes 786440 | tf_op jit(solution)/shard_map/ppermute | solution.py:204
  56.2 11.5 %collective-permute-start.23 = (bf16[64,2048]{1,0:T(8,128)(2,1)S(1)}, bf16[64,2048]{1,0:T(8,128)(2,1)S(1)}, u32[]{:S(2)}, u32[]{:S(2)}) collective-permute-start(bf16[64,2048]{1,0:T(8,128)(2,1)S(1)} %shard_map.57.rest_4_), channel_id=1, source_target_pairs={{0,1},{1,0},{2,3},{3,2},{4,5},{5,4},{6,7},{7,6},{8,9},{9,8},{10,11... | collective-permute-start | bytes 786440 | tf_op jit(solution)/shard_map/ppermute | solution.py:207
  56.9 10.8 %collective-permute-start.25 = (bf16[64,2048]{1,0:T(8,128)(2,1)S(1)}, bf16[64,2048]{1,0:T(8,128)(2,1)S(1)}, u32[]{:S(2)}, u32[]{:S(2)}) collective-permute-start(bf16[64,2048]{1,0:T(8,128)(2,1)S(1)} %shard_map.62.refs_1_), channel_id=1, source_target_pairs={{0,16},{8,24},{16,0},{24,8},{1,17},{9,25},{17,1},{25,9},{2,18},{10... | collective-permute-start | bytes 786440 | tf_op jit(solution)/shard_map/ppermute | solution.py:204
  58.4 9.9 %collective-permute-start.19 = (bf16[64,2048]{1,0:T(8,128)(2,1)S(1)}, bf16[64,2048]{1,0:T(8,128)(2,1)S(1)}, u32[]{:S(2)}, u32[]{:S(2)}) collective-permute-start(bf16[64,2048]{1,0:T(8,128)(2,1)S(1)} %shard_map.56.rest_2_), channel_id=1, source_target_pairs={{0,1},{1,0},{2,3},{3,2},{4,5},{5,4},{6,7},{7,6},{8,9},{9,8},{10,11... | collective-permute-start | bytes 786440 | tf_op jit(solution)/shard_map/ppermute | solution.py:207
  59.7 9.3 %collective-permute-start.17 = (bf16[64,2048]{1,0:T(8,128)(2,1)S(1)}, bf16[64,2048]{1,0:T(8,128)(2,1)S(1)}, u32[]{:S(2)}, u32[]{:S(2)}) collective-permute-start(bf16[64,2048]{1,0:T(8,128)(2,1)S(1)} %shard_map.56.rest_2_), channel_id=1, source_target_pairs={{0,16},{8,24},{16,0},{24,8},{1,17},{9,25},{17,1},{25,9},{2,18},{10... | collective-permute-start | bytes 786440 | tf_op jit(solution)/shard_map/ppermute | solution.py:204
  67.7 2.4 %collective-permute-start.24 = (bf16[64,2048]{1,0:T(8,128)(2,1)S(1)}, bf16[64,2048]{1,0:T(8,128)(2,1)S(1)}, u32[]{:S(2)}, u32[]{:S(2)}) collective-permute-start(bf16[64,2048]{1,0:T(8,128)(2,1)S(1)} %shard_map.64.rest_6_), channel_id=1, source_target_pairs={{0,8},{8,0},{16,24},{24,16},{1,9},{9,1},{17,25},{25,17},{2,10},{10... | collective-permute-start | bytes 786440 | tf_op jit(solution)/shard_map/ppermute | solution.py:204
  67.8 2.3 %collective-permute-start.22 = (bf16[64,2048]{1,0:T(8,128)(2,1)S(1)}, bf16[64,2048]{1,0:T(8,128)(2,1)S(1)}, u32[]{:S(2)}, u32[]{:S(2)}) collective-permute-start(bf16[64,2048]{1,0:T(8,128)(2,1)S(1)} %shard_map.63.rest_4_), channel_id=1, source_target_pairs={{0,8},{8,0},{16,24},{24,16},{1,9},{9,1},{17,25},{25,17},{2,10},{10... | collective-permute-start | bytes 786440 | tf_op jit(solution)/shard_map/ppermute | solution.py:204
  68.3 1.8 %collective-permute-start.20 = (bf16[64,2048]{1,0:T(8,128)(2,1)S(1)}, bf16[64,2048]{1,0:T(8,128)(2,1)S(1)}, u32[]{:S(2)}, u32[]{:S(2)}) collective-permute-start(bf16[64,2048]{1,0:T(8,128)(2,1)S(1)} %shard_map.61.rest_2_), channel_id=1, source_target_pairs={{0,8},{8,0},{16,24},{24,16},{1,9},{9,1},{17,25},{25,17},{2,10},{10... | collective-permute-start | bytes 786440 | tf_op jit(solution)/shard_map/ppermute | solution.py:204
  69.0 1.5 %collective-permute-start.18 = (bf16[64,2048]{1,0:T(8,128)(2,1)S(1)}, bf16[64,2048]{1,0:T(8,128)(2,1)S(1)}, u32[]{:S(2)}, u32[]{:S(2)}) collective-permute-start(bf16[64,2048]{1,0:T(8,128)(2,1)S(1)} %shard_map.60.rest_0_), channel_id=1, source_target_pairs={{0,8},{8,0},{16,24},{24,16},{1,9},{9,1},{17,25},{25,17},{2,10},{10... | collective-permute-start | bytes 786440 | tf_op jit(solution)/shard_map/ppermute | solution.py:204
  69.0 9.2 %collective-permute-start.27 = (bf16[64,2048]{1,0:T(8,128)(2,1)S(1)}, bf16[64,2048]{1,0:T(8,128)(2,1)S(1)}, u32[]{:S(2)}, u32[]{:S(2)}) collective-permute-start(bf16[64,2048]{1,0:T(8,128)(2,1)S(1)} %shard_map.60.rest_0_), channel_id=1, source_target_pairs={{0,1},{1,0},{2,3},{3,2},{4,5},{5,4},{6,7},{7,6},{8,9},{9,8},{10,11... | collective-permute-start | bytes 786440 | tf_op jit(solution)/shard_map/ppermute | solution.py:207
  78.2 1.6 %collective-permute-start.28 = (bf16[64,2048]{1,0:T(8,128)(2,1)S(1)}, bf16[64,2048]{1,0:T(8,128)(2,1)S(1)}, u32[]{:S(2)}, u32[]{:S(2)}) collective-permute-start(bf16[64,2048]{1,0:T(8,128)(2,1)S(1)} %shard_map.67.rest_2_), channel_id=1, source_target_pairs={{0,8},{8,0},{16,24},{24,16},{1,9},{9,1},{17,25},{25,17},{2,10},{10... | collective-permute-start | bytes 786440 | tf_op jit(solution)/shard_map/ppermute | solution.py:204
  78.4 1.8 %collective-permute-start.26 = (bf16[64,2048]{1,0:T(8,128)(2,1)S(1)}, bf16[64,2048]{1,0:T(8,128)(2,1)S(1)}, u32[]{:S(2)}, u32[]{:S(2)}) collective-permute-start(bf16[64,2048]{1,0:T(8,128)(2,1)S(1)} %shard_map.66.rest_0_), channel_id=1, source_target_pairs={{0,8},{8,0},{16,24},{24,16},{1,9},{9,1},{17,25},{25,17},{2,10},{10... | collective-permute-start | bytes 786440 | tf_op jit(solution)/shard_map/ppermute | solution.py:204

commit v4 on v3

--- a/solution.py
+++ b/solution.py
@@ -5,7 +5,7 @@
 from jax.experimental.pallas import tpu as pltpu
 from jax.sharding import PartitionSpec as P
 
-FIRST, SECOND, WHOLE = range(3)
+FIRST, SECOND = range(2)
 
 VMEM = pl.BlockSpec(memory_space=pltpu.VMEM)
 SMEM = pl.BlockSpec(memory_space=pltpu.SMEM)
@@ -26,70 +26,62 @@
     )(*operands)
 
 
-def extract(partners, integrals):
+def extract(bits, partners, integrals):
     occ_dev = integrals.shape[0]
     shape = pltpu.VMEM(integrals.shape[1:], integrals.dtype)
 
-    def kernel(partners_ref, integrals_ref, own_ref, sent_ref, sems):
-        core = lax.rem(lax.axis_index("occ"), 2)
+    def kernel(partners_ref, integrals_ref, own_ref, sent_ref, held_ref, sems):
+        occ_index = lax.axis_index("occ")
+        core = lax.rem(occ_index, 2)
         copies = []
         for k, (out_ref, step) in enumerate(((sent_ref, 1 - core), (own_ref, core))):
             row = lax.rem(partners_ref[step], occ_dev)
             copies.append(pltpu.make_async_copy(integrals_ref.at[row], out_ref, sems.at[k]))
         for copy in copies:
             copy.start()
+        owner = lax.div(partners_ref[core], occ_dev)
+        for k, bit in enumerate(bits):
+            held = jnp.where(lax.div(owner, bit) == lax.div(occ_index, bit), 1, 0)
+            held_ref[pl.ds(8 * k, 8), :] = jnp.full((8, 128), held, jnp.int32)
         for copy in copies:
             copy.wait()
 
+    flags = pltpu.VMEM((8 * len(bits), 128), jnp.int32)
     return call(
         kernel,
         [partners, integrals],
         [SMEM, ANY],
-        [(VMEM, shape)] * 2,
+        [(VMEM, shape), (VMEM, shape), (VMEM, flags)],
         [pltpu.SemaphoreType.DMA((2,))],
         vmem=56,
     )
 
 
-def choose(where, partners, occ_dev, bit, own, got, token=None):
-    height, width = own.shape
-    half = height // 2
-    outs = [(ANY, jax.ShapeDtypeStruct(own.shape, own.dtype))]
-    if token is not None:
-        outs.append((ANY, jax.ShapeDtypeStruct((half, width), own.dtype)))
-
-    def kernel(where_ref, partners_ref, own_ref, got_ref, *rest):
-        out_refs, sems = rest[-1 - len(outs) : -1], rest[-1]
-        occ_index = where_ref[1]
-        owner = lax.div(partners_ref[lax.rem(occ_index, 2)], occ_dev)
-        held = lax.div(owner, bit) == lax.div(occ_index, bit)
-        plane = lax.rem(lax.div(occ_index, 2), 2)
-
-        def copy_from(source_ref):
-            copies = [pltpu.make_async_copy(source_ref, out_refs[0], sems.at[0])]
-            if token is not None:
-                source = source_ref.at[pl.ds(pl.multiple_of(plane * half, half), half)]
-                copies.append(pltpu.make_async_copy(source, out_refs[1], sems.at[1]))
-            for copy in copies:
-                copy.start()
-            for copy in copies:
-                copy.wait()
-
-        pl.when(held)(lambda: copy_from(own_ref))
-        pl.when(jnp.logical_not(held))(lambda: copy_from(got_ref))
-
-    operands, specs = [where, partners, own, got], [SMEM, SMEM, ANY, ANY]
+def choose(held, n, own, got, token=None):
+    halves = 2 if n == 0 else 1
+    depth, width = own.shape[0] // halves, own.shape[1]
+
+    def kernel(held_ref, own_ref, got_ref, *rest):
+        out_refs = rest[-halves:]
+        plane = lax.rem(lax.div(lax.axis_index("occ"), 2), 2)
+        flag = held_ref[8 * n : 8 * n + 1, 0:1] == 1
+        for k in range(halves):
+            at = pl.multiple_of(lax.rem(plane + k, 2) * depth, depth) if halves == 2 else 0
+            rows = pl.ds(at, depth)
+            out_refs[k][...] = jnp.where(flag, own_ref[rows, :], got_ref[rows, :])
+
+    operands, specs = [held, own, got], [VMEM] * 3
     if token is not None:
         operands.append(token)
         specs.append(ANY)
-    return call(kernel, operands, specs, outs, [pltpu.SemaphoreType.DMA((2,))], vmem=48 if token is None else 2)
+    return call(kernel, operands, specs, [(VMEM, pltpu.VMEM((depth, width), own.dtype))] * halves)
 
 
 def prepare(where, partners, occ_energy, column, virt_halves, rows, groups, ready):
     height = rows.shape[0]
     local_virt, half = column.shape[0], virt_halves.shape[1]
     occ_dev, virt_size = height // local_virt, virt_halves.shape[0] // 2
-    widths = [sum(half * (2 if which == WHOLE else 1) for _, _, which, _ in places) for places in groups]
+    widths = [half * len(places) for places in groups]
 
     def kernel(where_ref, partners_ref, occ_energy_ref, column_ref, virt_ref, rows_ref, *rest):
         rest = rest[1:]
@@ -104,14 +96,12 @@
             own = occ_energy_ref[occ_index * occ_dev + i]
             row_energy_ref[pl.ds(i * local_virt, local_virt), :] = column_ref[...] - own
         for places, energy_ref in zip(groups, energy_refs):
-            start = 0
-            for ring_step, side, which, step in places:
+            for k, (ring_step, side, which, step) in enumerate(places):
                 position = lax.rem(virt_index + 2 * ring_step, virt_size)
                 position = position + side * (1 - 2 * lax.rem(position, 2))
                 pair = occ_energy_ref[partners_ref[lax.rem(occ_index + step, 2)]]
-                for part in {FIRST: [plane], SECOND: [1 - plane], WHOLE: [0, 1]}[which]:
-                    energy_ref[:, start : start + half] = virt_ref[pl.ds(2 * position + part, 1), :] - pair
-                    start += half
+                part = lax.rem(plane + which, 2)
+                energy_ref[:, k * half : (k + 1) * half] = virt_ref[pl.ds(2 * position + part, 1), :] - pair
         load.wait()
 
     outs = [(VMEM, pltpu.VMEM(rows.shape, rows.dtype)), (VMEM, pltpu.VMEM((height, 1), jnp.float32)), (VMEM, TOKEN)]
@@ -127,7 +117,7 @@
     return rows, row_energy, token, energies
 
 
-def contract(rows, row_energy, block_energy, blocks, total, last):
+def contract(rows, row_energy, block_energy, blocks, waits, total, last):
     height, width = rows.shape
     count, depths = len(blocks), [block.shape[0] for block in blocks]
     starts, depth = [sum(depths[:k]) for k in range(count)], sum(depths)
@@ -135,7 +125,7 @@
     tiles = height // tile
 
     def kernel(rows_ref, row_energy_ref, block_energy_ref, *rest):
-        block_refs, rest = rest[:count], rest[count:]
+        block_refs, rest = rest[:count], rest[count + len(waits) :]
         total_ref, rest = (rest[0], rest[1:]) if total is not None else (None, rest)
         out_ref, token_ref, held, sems = rest[:4]
         copies = [
@@ -170,7 +160,8 @@
         for write in writes[-2:]:
             write.wait()
 
-    operands, specs = [rows, row_energy, block_energy, *blocks], [VMEM] * 3 + [ANY] * count
+    operands = [rows, row_energy, block_energy, *blocks, *waits]
+    specs = [VMEM] * 3 + [ANY] * (count + len(waits))
     if total is not None:
         operands.append(total)
         specs.append(VMEM)
@@ -180,7 +171,7 @@
         out = (ANY, jax.ShapeDtypeStruct((height, width), jnp.bfloat16))
     else:
         out = (VMEM, pltpu.VMEM((height, width), jnp.float32))
-    aliases = {3 + count: 0} if total is not None and not last else {}
+    aliases = {len(operands) - 1: 0} if total is not None and not last else {}
     return call(kernel, operands, specs, [out, (VMEM, TOKEN)], scratch, aliases, vmem=16)
 
 
@@ -213,45 +204,52 @@
     early, late = shifts[: ring // 2], shifts[ring // 2 :]
     even, odd, reach = early[0::2], early[1::2], (len(early) + 1) // 2
     groups = [
-        [(0, 0, WHOLE)],
-        [(0, 1, WHOLE)] + [(k, 0, FIRST) for k in early],
-        [(k, 1, FIRST) for k in even] + [(k, 0, FIRST) for k in late] + [(k, 0, SECOND) for k in early],
-        [(k, 0, SECOND) for k in late] + [(k, 1, FIRST) for k in late + odd] + [(k, 1, SECOND) for k in even],
-        [(k, 1, SECOND) for k in odd + late],
+        [(0, 0, FIRST)],
+        [(0, 0, SECOND), (0, 1, FIRST)] + [(k, 0, FIRST) for k in early],
+        [(k, 0, FIRST) for k in late] + [(k, 0, SECOND) for k in early] + [(k, 1, FIRST) for k in odd],
+        [(k, 0, SECOND) for k in late] + [(k, 1, FIRST) for k in late + even] + [(0, 1, SECOND)],
+        [(k, 1, SECOND) for k in early + late],
     ]
+    awaited = [[(0, 0, SECOND)], [], [(0, 1, SECOND)], [(k, 1, SECOND) for k in early], []]
     places = [[(*place, step) for place in group for step in range(2)] for group in groups]
 
     where = jnp.stack([virt_index, occ_index]).astype(jnp.int32)
     column = lax.dynamic_slice_in_dim(virt_energy, virt_index * local_virt, local_virt)[:, None]
     virt_halves = virt_energy.reshape(2 * virt_size, half)
-    own, sent = extract(partners, integrals)
-    (own,) = choose(where, partners, occ_dev, 1, own, swap_occ(sent, 1))
+    bits = [1 << n for n in range(occ_size.bit_length() - 1)]
+    own, sent, held = extract(bits, partners, integrals)
+    first, second = choose(held, 0, own, swap_occ(sent, 1))
     rows, row_energy, token, energies = prepare(
-        where, partners, occ_energy, column, virt_halves, integrals.reshape(-1, aux_width), places, own
+        where, partners, occ_energy, column, virt_halves, integrals.reshape(-1, aux_width), places, first
     )
-    bit = 2
-    while bit < occ_size:
-        own, *first_half = choose(where, partners, occ_dev, bit, own, swap_occ(own, bit), token)
-        bit *= 2
-
-    blocks = {(0, 0, WHOLE): own, (0, 1, WHOLE): swap_pair(own)}
+    sent = [second, first]
+    for n, bit in list(enumerate(bits))[1:]:
+        (first,) = choose(held, n, first, swap_occ(sent[0] if bit == 2 else first, bit), token)
+    blocks = {(0, 0, FIRST): first, (0, 1, FIRST): swap_pair(first)}
     for k in early:
-        blocks[k, 0, FIRST] = shift_ring(first_half[0], k)
+        blocks[k, 0, FIRST] = shift_ring(first, k)
+    for n, bit in list(enumerate(bits))[1:]:
+        got = swap_occ(sent[1] if bit == 2 else second, bit)
+        (second,) = choose(held, n, second, got, token)
+    blocks[0, 0, SECOND] = second
     total = None
     for n, group in enumerate(groups):
         if n > 0:
-            for name in group:
-                (blocks[name],) = gate([token], [blocks[name]])
+            for name in [*group, *awaited[n]]:
+                if n == 1 or name not in awaited[n - 1]:
+                    (blocks[name],) = gate([token], [blocks[name]])
         if n == 1:
-            for k in early:
-                blocks[k, 0, SECOND] = swap_occ(blocks[k, 0, FIRST], 2)
-                blocks[k, 1, FIRST] = swap_pair(blocks[k, 0, FIRST])
             for k in late:
                 near, step = (k - reach, reach) if k - reach in early else (k + reach, -reach)
                 blocks[k, 0, FIRST] = shift_ring(blocks[near, 0, FIRST], step)
+            for k in early:
+                blocks[k, 0, SECOND] = swap_occ(blocks[k, 0, FIRST], 2)
+            for k in odd:
+                blocks[k, 1, FIRST] = swap_pair(blocks[k, 0, FIRST])
+            for k in even:
+                blocks[k, 1, FIRST] = shift_ring(blocks[0, 1, FIRST], k)
+            blocks[0, 1, SECOND] = swap_pair(blocks[0, 0, SECOND])
         if n == 2:
-            for k in odd:
-                (blocks[k, 1, FIRST],) = gate([token], [blocks[k, 1, FIRST]])
             for k in late:
                 blocks[k, 0, SECOND] = swap_occ(blocks[k, 0, FIRST], 2)
                 blocks[k, 1, FIRST] = swap_pair(blocks[k, 0, FIRST])
@@ -263,7 +261,8 @@
             for k in late:
                 blocks[k, 1, SECOND] = swap_pair(blocks[k, 0, SECOND])
         pairs = [block for name in group for block in (blocks[name], swap_occ(blocks[name], 1))]
-        total, token = contract(rows, row_energy, energies[n], pairs, total, n == len(groups) - 1)
+        waits = [blocks[name] for name in awaited[n]]
+        total, token = contract(rows, row_energy, energies[n], pairs, waits, total, n == len(groups) - 1)
     return total.reshape(integrals.shape)
 
 

time: 88.5 us -> 84.3 us (0.953)
  waiting for transfers between devices: 17.2 us -> 10.3 us
  starting transfers between devices: 23.9 us -> 27.1 us
    ppermute x6, waiting for transfers between devices: 5.59 us -> 0.02 us  [swap_pair(): return lax.ppermute(value, 'virt', [(v, v ^ 1) for v in range(virt_size)])]
    ppermute x20 -> x23, waiting for transfers between devices: 9.32 us -> 5.88 us  [swap_occ(): return lax.ppermute(value, 'occ', [(o, o ^ bit) for o in range(occ_size)])]
    ppermute x3 -> x4, starting transfers between devices: 6.64 us -> 9.44 us  [shift_ring(): lax.ppermute(value, 'virt', [(v, (v - 2 * k) % virt_size) for v in range(...]
    ppermute x3 -> x4, waiting for transfers between devices: 2.26 us -> 4.43 us  [shift_ring(): lax.ppermute(value, 'virt', [(v, (v - 2 * k) % virt_size) for v in range(...]
    unnamed x8 -> x6, local copies, waits for them, and re-layouts: 4.75 us -> 4.09 us
    ppermute x20 -> x23, starting transfers between devices: 10.3 us -> 10.7 us  [swap_occ(): return lax.ppermute(value, 'occ', [(o, o ^ bit) for o in range(occ_size)])]
    pallas_call x23 -> x25, Pallas kernels: 40.3 us -> 40.4 us  [call(): pl.pallas_call(kernel, in_specs=in_specs, out_specs=[spec for spec, _ in...]
  transfers between devices with their start and end apart: 29 -> 33, of which waited for: 10 -> 6; matrix products, arithmetic and copies ran while one was open for 2% -> 2% of each run, Pallas kernels for 33% -> 35%
where the time goes in v4:
time: 84.3 us; the launch traced here: 84 us
  Pallas kernels  40.4 us (48%)
  starting transfers between devices  27.1 us (32%)
  waiting for transfers between devices  10.3 us (12%)
  local copies, waits for them, and re-layouts  5.72 us (7%)
    pallas_call x25, Pallas kernels, call(): pl.pallas_call(kernel, in_specs=in_specs, out_specs=[spec for spec, _ in...  40.4 us
    ppermute x23, starting transfers between devices, swap_occ(): return lax.ppermute(value, 'occ', [(o, o ^ bit) for o in range(occ_size)])  10.7 us
    ppermute x4, starting transfers between devices, shift_ring(): lax.ppermute(value, 'virt', [(v, (v - 2 * k) % virt_size) for v in range(...  9.44 us
    ppermute x6, starting transfers between devices, swap_pair(): return lax.ppermute(value, 'virt', [(v, v ^ 1) for v in range(virt_size)])  6.9 us
    ppermute x23, waiting for transfers between devices, swap_occ(): return lax.ppermute(value, 'occ', [(o, o ^ bit) for o in range(occ_size)])  5.88 us
    ppermute x4, waiting for transfers between devices, shift_ring(): lax.ppermute(value, 'virt', [(v, (v - 2 * k) % virt_size) for v in range(...  4.43 us
    unnamed x6, local copies, waits for them, and re-layouts  4.09 us
  transfers between devices with their start and end apart: 33, of which 6 were waited for; matrix products, arithmetic and copies ran while one was open for 2% of the time, Pallas kernels for 35%

profile of v4, /device:TPU:0, one launch (start us, length us, event | category | flops | bytes accessed | tf_op | source)
XLA Modules:
  0.0 84.0 jit_solution(4856594046603033064)
XLA Ops:
  0.0 1.9 %shard_map.46 = (bf16[128,2048]{1,0:T(8,128)(2,1)S(1)}, bf16[128,2048]{1,0:T(8,128)(2,1)S(1)}, s32[16,128]{1,0:T(8,128)S(1)}) custom-call(s32[2]{0:T(128)} %partners_ref.3, bf16[12,128,2048]{2,1,0:T(8,128)(2,1)} %integrals_ref.1), custom_call_target="tpu_custom_call" | custom-call | tf_op jit(solution)/shard_map/pallas_call | solution.py:17
  1.9 0.5 collective-permute-start
  2.4 1.5 %collective-permute-done.got_ref = bf16[128,2048]{1,0:T(8,128)(2,1)S(1)} collective-permute-done((bf16[128,2048]{1,0:T(8,128)(2,1)S(1)}, bf16[128,2048]{1,0:T(8,128)(2,1)S(1)}, u32[]{:S(2)}, u32[]{:S(2)}) %collective-permute-start) | collective-permute-done | bytes 524320 | tf_op jit(solution)/shard_map/ppermute | solution.py:195
  4.0 0.1 shard_map.47
  4.1 2.9 %collective-permute-start.1 = (bf16[64,2048]{1,0:T(8,128)(2,1)S(1)}, bf16[64,2048]{1,0:T(8,128)(2,1)S(1)}, u32[]{:S(2)}, u32[]{:S(2)}) collective-permute-start(bf16[64,2048]{1,0:T(8,128)(2,1)S(1)} %get-tuple-element.37.own_ref), channel_id=1, source_target_pairs={{0,16},{8,24},{16,0},{24,8},{1,17},{9,25},{17,1},{25,9},{2,18},{10... | collective-permute-start | bytes 786440 | tf_op jit(solution)/shard_map/ppermute | solution.py:195
  7.0 0.8 reshape.9.virt_ref
  7.7 0.8 dynamic-slice_bitcast_fusion
  8.5 0.1 copy.23.column_ref
  8.6 0.1 pad_add_fusion.where_ref
  8.7 0.0 collective-permute-start.3
  8.7 2.8 %copy-done = bf16[12,128,2048]{2,1,0:T(8,128)(2,1)S(1)} copy-done((bf16[12,128,2048]{2,1,0:T(8,128)(2,1)S(1)}, bf16[12,128,2048]{2,1,0:T(8,128)(2,1)}, u32[]{:S(2)}) %copy-start) | copy-done | bytes 6291480
  11.5 0.7 copy-done.1
  12.2 0.7 copy-done.2
  12.8 1.1 %shard_map.48 = (bf16[1536,2048]{1,0:T(8,128)(2,1)S(1)}, f32[1536,1]{1,0:T(8,128)S(1)}, f32[8,128]{1,0:T(8,128)S(1)}, f32[1,128]{1,0:T(1,128)S(1)}, f32[1,512]{1...) custom-call(s32[2]{0:T(128)S(1)} %pad_add_fusion.where_ref, s32[2]{0:T(128)S(1)} %copy-done.1, ...), custom_call_target="tpu_custom_call" | custom-call | tf_op jit(solution)/shard_map/pallas_call | solution.py:17
  14.0 0.1 collective-permute-done.1.got_ref
  14.1 0.1 shard_map.49.rest_0_
  14.1 0.1 collective-permute-start.2
  14.2 2.2 %collective-permute-start.9 = (bf16[64,2048]{1,0:T(8,128)(2,1)S(1)}, bf16[64,2048]{1,0:T(8,128)(2,1)S(1)}, u32[]{:S(2)}, u32[]{:S(2)}) collective-permute-start(bf16[64,2048]{1,0:T(8,128)(2,1)S(1)} %shard_map.49.rest_0_), channel_id=1, source_target_pairs={{0,2},{1,3},{2,4},{3,5},{4,6},{5,7},{6,0},{7,1},{8,10},{9,11},{10,... | collective-permute-start | bytes 786440 | tf_op jit(solution)/shard_map/ppermute | solution.py:201
  16.4 2.1 %collective-permute-start.7 = (bf16[64,2048]{1,0:T(8,128)(2,1)S(1)}, bf16[64,2048]{1,0:T(8,128)(2,1)S(1)}, u32[]{:S(2)}, u32[]{:S(2)}) collective-permute-start(bf16[64,2048]{1,0:T(8,128)(2,1)S(1)} %shard_map.49.rest_0_), channel_id=1, source_target_pairs={{0,6},{1,7},{2,0},{3,1},{4,2},{5,3},{6,4},{7,5},{8,14},{9,15},{10,... | collective-permute-start | bytes 786440 | tf_op jit(solution)/shard_map/ppermute | solution.py:201
  18.5 1.7 %collective-permute-start.5 = (bf16[64,2048]{1,0:T(8,128)(2,1)S(1)}, bf16[64,2048]{1,0:T(8,128)(2,1)S(1)}, u32[]{:S(2)}, u32[]{:S(2)}) collective-permute-start(bf16[64,2048]{1,0:T(8,128)(2,1)S(1)} %shard_map.49.rest_0_), channel_id=1, source_target_pairs={{0,1},{1,0},{2,3},{3,2},{4,5},{5,4},{6,7},{7,6},{8,9},{9,8},{10,11... | collective-permute-start | bytes 786440 | tf_op jit(solution)/shard_map/ppermute | solution.py:198
  20.2 0.0 collective-permute-done.3.got_ref
  20.2 0.1 shard_map.50.rest_2_.refs_1_
  20.3 0.0 collective-permute-done.2.rest_1_
  20.3 5.6 %shard_map.51 = (f32[1536,2048]{1,0:T(8,128)S(1)}, f32[8,128]{1,0:T(8,128)S(1)}) custom-call(bf16[1536,2048]{1,0:T(8,128)(2,1)S(1)} %get-tuple-element.31.rows_ref, f32[1536,1]{1,0:T(8,128)S(1)} %get-tuple-element.32.row_energy_ref, f32[1,128]{1,0:T(1,128)S(1)} %get-tuple-element.36.block_energy_ref, bf16[64,2048]{1,0:T(8,128)(2,1)S(1)} %shard_map.49.rest_0_, ...), custom_call_target="tpu_custom_call" | custom-call | tf_op jit(solution)/shard_map/pallas_call | solution.py:17
  25.9 0.0 collective-permute-done.9.refs_1_
  25.9 0.1 collective-permute-start.10
  26.0 4.4 %collective-permute-done.7.refs_1_ = bf16[64,2048]{1,0:T(8,128)(2,1)S(1)} collective-permute-done((bf16[64,2048]{1,0:T(8,128)(2,1)S(1)}, bf16[64,2048]{1,0:T(8,128)(2,1)S(1)}, u32[]{:S(2)}, u32[]{:S(2)}) %collective-permute-start.7) | collective-permute-done | bytes 262176 | tf_op jit(solution)/shard_map/ppermute | solution.py:201
  30.4 0.0 collective-permute-start.8
  30.4 0.0 collective-permute-done.5.refs_1_
  30.4 0.5 collective-permute-start.6
  30.9 0.1 collective-permute-start.4
  31.0 1.5 %collective-permute-start.17 = (bf16[64,2048]{1,0:T(8,128)(2,1)S(1)}, bf16[64,2048]{1,0:T(8,128)(2,1)S(1)}, u32[]{:S(2)}, u32[]{:S(2)}) collective-permute-start(bf16[64,2048]{1,0:T(8,128)(2,1)S(1)} %shard_map.55.rest_6_), channel_id=1, source_target_pairs={{0,1},{1,0},{2,3},{3,2},{4,5},{5,4},{6,7},{7,6},{8,9},{9,8},{10,11... | collective-permute-start | bytes 786440 | tf_op jit(solution)/shard_map/ppermute | solution.py:198
  32.5 1.5 %collective-permute-start.15 = (bf16[64,2048]{1,0:T(8,128)(2,1)S(1)}, bf16[64,2048]{1,0:T(8,128)(2,1)S(1)}, u32[]{:S(2)}, u32[]{:S(2)}) collective-permute-start(bf16[64,2048]{1,0:T(8,128)(2,1)S(1)} %shard_map.55.rest_6_), channel_id=1, source_target_pairs={{0,16},{8,24},{16,0},{24,8},{1,17},{9,25},{17,1},{25,9},{2,18},{10... | collective-permute-start | bytes 786440 | tf_op jit(solution)/shard_map/ppermute | solution.py:195
  34.0 0.5 collective-permute-start.13
  34.6 0.0 collective-permute-done.6.rest_3_
  34.6 2.7 %collective-permute-start.11 = (bf16[64,2048]{1,0:T(8,128)(2,1)S(1)}, bf16[64,2048]{1,0:T(8,128)(2,1)S(1)}, u32[]{:S(2)}, u32[]{:S(2)}) collective-permute-start(bf16[64,2048]{1,0:T(8,128)(2,1)S(1)} %shard_map.54.rest_4_), channel_id=1, source_target_pairs={{0,6},{1,7},{2,0},{3,1},{4,2},{5,3},{6,4},{7,5},{8,14},{9,15},{10,... | collective-permute-start | bytes 786440 | tf_op jit(solution)/shard_map/ppermute | solution.py:201
  37.3 0.5 collective-permute-start.19
  37.8 7.4 %shard_map.56 = (f32[1536,2048]{1,0:T(8,128)S(1)}, f32[8,128]{1,0:T(8,128)S(1)}) custom-call(bf16[1536,2048]{1,0:T(8,128)(2,1)S(1)} %get-tuple-element.31.rows_ref, f32[1536,1]{1,0:T(8,128)S(1)} %get-tuple-element.32.row_energy_ref, f32[1,512]{1,0:T(1,128)S(1)} %get-tuple-element.35.block_energy_ref, ...), custom_call_target="tpu_custom_call", output_to_operand_aliasing={{0}: (11, {})} | custom-call | tf_op jit(solution)/shard_map/pallas_call | solution.py:17
  45.2 0.0 collective-permute-done.17.refs_1_
  45.2 0.1 collective-permute-start.18
  45.3 0.0 collective-permute-done.15.refs_1_
  45.3 0.5 collective-permute-start.16
  45.8 0.7 collective-permute-done.13.refs_1_
  46.5 0.0 collective-permute-start.14
  46.5 0.5 collective-permute-start.12
  47.0 0.0 collective-permute-done.19.refs_1_
  47.0 2.4 %collective-permute-start.28 = (bf16[64,2048]{1,0:T(8,128)(2,1)S(1)}, bf16[64,2048]{1,0:T(8,128)(2,1)S(1)}, u32[]{:S(2)}, u32[]{:S(2)}) collective-permute-start(bf16[64,2048]{1,0:T(8,128)(2,1)S(1)} %shard_map.53.rest_2_), channel_id=1, source_target_pairs={{0,6},{1,7},{2,0},{3,1},{4,2},{5,3},{6,4},{7,5},{8,14},{9,15},{10,... | collective-permute-start | bytes 786440 | tf_op jit(solution)/shard_map/ppermute | solution.py:201
  49.4 0.0 collective-permute-done.18.rest_7_
  49.4 0.8 collective-permute-start.26
  50.3 1.5 %collective-permute-start.24 = (bf16[64,2048]{1,0:T(8,128)(2,1)S(1)}, bf16[64,2048]{1,0:T(8,128)(2,1)S(1)}, u32[]{:S(2)}, u32[]{:S(2)}) collective-permute-start(bf16[64,2048]{1,0:T(8,128)(2,1)S(1)} %shard_map.57.rest_0_), channel_id=1, source_target_pairs={{0,16},{8,24},{16,0},{24,8},{1,17},{9,25},{17,1},{25,9},{2,18},{10... | collective-permute-start | bytes 786440 | tf_op jit(solution)/shard_map/ppermute | solution.py:195
  51.8 0.5 collective-permute-start.22
  52.3 1.2 %collective-permute-start.20 = (bf16[64,2048]{1,0:T(8,128)(2,1)S(1)}, bf16[64,2048]{1,0:T(8,128)(2,1)S(1)}, u32[]{:S(2)}, u32[]{:S(2)}) collective-permute-start(bf16[64,2048]{1,0:T(8,128)(2,1)S(1)} %shard_map.58.rest_2_), channel_id=1, source_target_pairs={{0,1},{1,0},{2,3},{3,2},{4,5},{5,4},{6,7},{7,6},{8,9},{9,8},{10,11... | collective-permute-start | bytes 786440 | tf_op jit(solution)/shard_map/ppermute | solution.py:198
  53.5 7.4 %shard_map.62 = (f32[1536,2048]{1,0:T(8,128)S(1)}, f32[8,128]{1,0:T(8,128)S(1)}) custom-call(bf16[1536,2048]{1,0:T(8,128)(2,1)S(1)} %get-tuple-element.31.rows_ref, f32[1536,1]{1,0:T(8,128)S(1)} %get-tuple-element.32.row_energy_ref, f32[1,512]{1,0:T(1,128)S(1)} %get-tuple-element.34.block_energy_ref, ...), custom_call_target="tpu_custom_call", output_to_operand_aliasing={{0}: (12, {})} | custom-call | tf_op jit(solution)/shard_map/pallas_call | solution.py:17
  60.9 0.1 collective-permute-start.30
  61.0 0.5 collective-permute-start.29
  61.5 0.1 collective-permute-start.27
  61.6 2.2 %collective-permute-done.22.refs_1_ = bf16[64,2048]{1,0:T(8,128)(2,1)S(1)} collective-permute-done((bf16[64,2048]{1,0:T(8,128)(2,1)S(1)}, bf16[64,2048]{1,0:T(8,128)(2,1)S(1)}, u32[]{:S(2)}, u32[]{:S(2)}) %collective-permute-start.22) | collective-permute-done | bytes 262176 | tf_op jit(solution)/shard_map/ppermute | solution.py:195
  63.8 1.2 %collective-permute-start.31 = (bf16[64,2048]{1,0:T(8,128)(2,1)S(1)}, bf16[64,2048]{1,0:T(8,128)(2,1)S(1)}, u32[]{:S(2)}, u32[]{:S(2)}) collective-permute-start(bf16[64,2048]{1,0:T(8,128)(2,1)S(1)} %shard_map.65.rest_0_), channel_id=1, source_target_pairs={{0,1},{1,0},{2,3},{3,2},{4,5},{5,4},{6,7},{7,6},{8,9},{9,8},{10,11... | collective-permute-start | bytes 786440 | tf_op jit(solution)/shard_map/ppermute | solution.py:198
  65.0 0.2 collective-permute-start.23
  65.2 0.3 collective-permute-start.21
  65.5 7.4 %shard_map.68 = (f32[1536,2048]{1,0:T(8,128)S(1)}, f32[8,128]{1,0:T(8,128)S(1)}) custom-call(bf16[1536,2048]{1,0:T(8,128)(2,1)S(1)} %get-tuple-element.31.rows_ref, f32[1536,1]{1,0:T(8,128)S(1)} %get-tuple-element.32.row_energy_ref, f32[1,512]{1,0:T(1,128)S(1)} %get-tuple-element.44.block_energy_ref, ...), custom_call_target="tpu_custom_call", output_to_operand_aliasing={{0}: (13, {})} | custom-call | tf_op jit(solution)/shard_map/pallas_call | solution.py:17
  72.9 0.3 collective-permute-start.32
  73.2 1.3 %collective-permute-done.32.rest_5_ = bf16[64,2048]{1,0:T(8,128)(2,1)S(1)} collective-permute-done((bf16[64,2048]{1,0:T(8,128)(2,1)S(1)}, bf16[64,2048]{1,0:T(8,128)(2,1)S(1)}, u32[]{:S(2)}, u32[]{:S(2)}) %collective-permute-start.32) | collective-permute-done | bytes 262176 | tf_op jit(solution)/shard_map/ppermute | solution.py:195
  74.5 9.3 %shard_map.70 = (bf16[1536,2048]{1,0:T(8,128)(2,1)}, f32[8,128]{1,0:T(8,128)}) custom-call(bf16[1536,2048]{1,0:T(8,128)(2,1)S(1)} %get-tuple-element.31.rows_ref, f32[1536,1]{1,0:T(8,128)S(1)} %get-tuple-element.32.row_energy_ref, f32[1,384]{1,0:T(1,128)S(1)} %get-tuple-element.33.block_energy_ref, bf16[64,2048]{1,0:T(8,128)(2,1)S(1)} %shard_map.63.rest_8_.rest_0_, ...), custom_call_target="tpu_custom_call" | custom-call | tf_op jit(solution)/shard_map/pallas_call | solution.py:17
  (37 shorter events, 0.1 us)
Async XLA Ops:
  1.9 2.1 %collective-permute-start = (bf16[128,2048]{1,0:T(8,128)(2,1)S(1)}, bf16[128,2048]{1,0:T(8,128)(2,1)S(1)}, u32[]{:S(2)}, u32[]{:S(2)}) collective-permute-start(bf16[128,2048]{1,0:T(8,128)(2,1)S(1)} %get-tuple-element.29), channel_id=1, source_target_pairs={{0,8},{8,0},{16,24},{24,16},{1,9},{9,1},{17,25},{25,17},{2,10},{10... | collective-permute-start | bytes 1572872 | tf_op jit(solution)/shard_map/ppermute | solution.py:195
  4.1 10.0 %collective-permute-start.1 = (bf16[64,2048]{1,0:T(8,128)(2,1)S(1)}, bf16[64,2048]{1,0:T(8,128)(2,1)S(1)}, u32[]{:S(2)}, u32[]{:S(2)}) collective-permute-start(bf16[64,2048]{1,0:T(8,128)(2,1)S(1)} %get-tuple-element.37.own_ref), channel_id=1, source_target_pairs={{0,16},{8,24},{16,0},{24,8},{1,17},{9,25},{17,1},{25,9},{2,18},{10... | collective-permute-start | bytes 786440 | tf_op jit(solution)/shard_map/ppermute | solution.py:195
  8.7 11.5 %collective-permute-start.3 = (bf16[64,2048]{1,0:T(8,128)(2,1)S(1)}, bf16[64,2048]{1,0:T(8,128)(2,1)S(1)}, u32[]{:S(2)}, u32[]{:S(2)}) collective-permute-start(bf16[64,2048]{1,0:T(8,128)(2,1)S(1)} %get-tuple-element.30.rest_0_.own_ref), channel_id=1, source_target_pairs={{0,16},{8,24},{16,0},{24,8},{1,17},{9,25},{17,1},{25,9},{2,18},{10... | collective-permute-start | bytes 786440 | tf_op jit(solution)/shard_map/ppermute | solution.py:195
  8.7 2.8 %copy-start = (bf16[12,128,2048]{2,1,0:T(8,128)(2,1)S(1)}, bf16[12,128,2048]{2,1,0:T(8,128)(2,1)}, u32[]{:S(2)}) copy-start(bf16[12,128,2048]{2,1,0:T(8,128)(2,1)} %integrals_ref.1) | copy-start | bytes 18874372
  11.5 0.7 copy-start.1
  12.2 0.7 copy-start.2
  14.1 6.1 %collective-permute-start.2 = (bf16[64,2048]{1,0:T(8,128)(2,1)S(1)}, bf16[64,2048]{1,0:T(8,128)(2,1)S(1)}, u32[]{:S(2)}, u32[]{:S(2)}) collective-permute-start(bf16[64,2048]{1,0:T(8,128)(2,1)S(1)} %shard_map.49.rest_0_), channel_id=1, source_target_pairs={{0,8},{8,0},{16,24},{24,16},{1,9},{9,1},{17,25},{25,17},{2,10},{10... | collective-permute-start | bytes 786440 | tf_op jit(solution)/shard_map/ppermute | solution.py:195
  14.2 11.7 %collective-permute-start.9 = (bf16[64,2048]{1,0:T(8,128)(2,1)S(1)}, bf16[64,2048]{1,0:T(8,128)(2,1)S(1)}, u32[]{:S(2)}, u32[]{:S(2)}) collective-permute-start(bf16[64,2048]{1,0:T(8,128)(2,1)S(1)} %shard_map.49.rest_0_), channel_id=1, source_target_pairs={{0,2},{1,3},{2,4},{3,5},{4,6},{5,7},{6,0},{7,1},{8,10},{9,11},{10,... | collective-permute-start | bytes 786440 | tf_op jit(solution)/shard_map/ppermute | solution.py:201
  16.4 14.0 %collective-permute-start.7 = (bf16[64,2048]{1,0:T(8,128)(2,1)S(1)}, bf16[64,2048]{1,0:T(8,128)(2,1)S(1)}, u32[]{:S(2)}, u32[]{:S(2)}) collective-permute-start(bf16[64,2048]{1,0:T(8,128)(2,1)S(1)} %shard_map.49.rest_0_), channel_id=1, source_target_pairs={{0,6},{1,7},{2,0},{3,1},{4,2},{5,3},{6,4},{7,5},{8,14},{9,15},{10,... | collective-permute-start | bytes 786440 | tf_op jit(solution)/shard_map/ppermute | solution.py:201
  18.5 11.9 %collective-permute-start.5 = (bf16[64,2048]{1,0:T(8,128)(2,1)S(1)}, bf16[64,2048]{1,0:T(8,128)(2,1)S(1)}, u32[]{:S(2)}, u32[]{:S(2)}) collective-permute-start(bf16[64,2048]{1,0:T(8,128)(2,1)S(1)} %shard_map.49.rest_0_), channel_id=1, source_target_pairs={{0,1},{1,0},{2,3},{3,2},{4,5},{5,4},{6,7},{7,6},{8,9},{9,8},{10,11... | collective-permute-start | bytes 786440 | tf_op jit(solution)/shard_map/ppermute | solution.py:198
  25.9 6.6 %collective-permute-start.10 = (bf16[64,2048]{1,0:T(8,128)(2,1)S(1)}, bf16[64,2048]{1,0:T(8,128)(2,1)S(1)}, u32[]{:S(2)}, u32[]{:S(2)}) collective-permute-start(bf16[64,2048]{1,0:T(8,128)(2,1)S(1)} %shard_map.55.rest_6_), channel_id=1, source_target_pairs={{0,8},{8,0},{16,24},{24,16},{1,9},{9,1},{17,25},{25,17},{2,10},{10... | collective-permute-start | bytes 786440 | tf_op jit(solution)/shard_map/ppermute | solution.py:195
  30.4 3.6 %collective-permute-start.8 = (bf16[64,2048]{1,0:T(8,128)(2,1)S(1)}, bf16[64,2048]{1,0:T(8,128)(2,1)S(1)}, u32[]{:S(2)}, u32[]{:S(2)}) collective-permute-start(bf16[64,2048]{1,0:T(8,128)(2,1)S(1)} %shard_map.54.rest_4_), channel_id=1, source_target_pairs={{0,8},{8,0},{16,24},{24,16},{1,9},{9,1},{17,25},{25,17},{2,10},{10... | collective-permute-start | bytes 786440 | tf_op jit(solution)/shard_map/ppermute | solution.py:195
  30.4 4.1 %collective-permute-start.6 = (bf16[64,2048]{1,0:T(8,128)(2,1)S(1)}, bf16[64,2048]{1,0:T(8,128)(2,1)S(1)}, u32[]{:S(2)}, u32[]{:S(2)}) collective-permute-start(bf16[64,2048]{1,0:T(8,128)(2,1)S(1)} %shard_map.53.rest_2_), channel_id=1, source_target_pairs={{0,8},{8,0},{16,24},{24,16},{1,9},{9,1},{17,25},{25,17},{2,10},{10... | collective-permute-start | bytes 786440 | tf_op jit(solution)/shard_map/ppermute | solution.py:195
  30.9 6.4 %collective-permute-start.4 = (bf16[64,2048]{1,0:T(8,128)(2,1)S(1)}, bf16[64,2048]{1,0:T(8,128)(2,1)S(1)}, u32[]{:S(2)}, u32[]{:S(2)}) collective-permute-start(bf16[64,2048]{1,0:T(8,128)(2,1)S(1)} %shard_map.52.rest_0_), channel_id=1, source_target_pairs={{0,8},{8,0},{16,24},{24,16},{1,9},{9,1},{17,25},{25,17},{2,10},{10... | collective-permute-start | bytes 786440 | tf_op jit(solution)/shard_map/ppermute | solution.py:195
  31.0 14.2 %collective-permute-start.17 = (bf16[64,2048]{1,0:T(8,128)(2,1)S(1)}, bf16[64,2048]{1,0:T(8,128)(2,1)S(1)}, u32[]{:S(2)}, u32[]{:S(2)}) collective-permute-start(bf16[64,2048]{1,0:T(8,128)(2,1)S(1)} %shard_map.55.rest_6_), channel_id=1, source_target_pairs={{0,1},{1,0},{2,3},{3,2},{4,5},{5,4},{6,7},{7,6},{8,9},{9,8},{10,11... | collective-permute-start | bytes 786440 | tf_op jit(solution)/shard_map/ppermute | solution.py:198
  32.5 12.8 %collective-permute-start.15 = (bf16[64,2048]{1,0:T(8,128)(2,1)S(1)}, bf16[64,2048]{1,0:T(8,128)(2,1)S(1)}, u32[]{:S(2)}, u32[]{:S(2)}) collective-permute-start(bf16[64,2048]{1,0:T(8,128)(2,1)S(1)} %shard_map.55.rest_6_), channel_id=1, source_target_pairs={{0,16},{8,24},{16,0},{24,8},{1,17},{9,25},{17,1},{25,9},{2,18},{10... | collective-permute-start | bytes 786440 | tf_op jit(solution)/shard_map/ppermute | solution.py:195
  34.0 12.5 %collective-permute-start.13 = (bf16[64,2048]{1,0:T(8,128)(2,1)S(1)}, bf16[64,2048]{1,0:T(8,128)(2,1)S(1)}, u32[]{:S(2)}, u32[]{:S(2)}) collective-permute-start(bf16[64,2048]{1,0:T(8,128)(2,1)S(1)} %shard_map.54.rest_4_), channel_id=1, source_target_pairs={{0,16},{8,24},{16,0},{24,8},{1,17},{9,25},{17,1},{25,9},{2,18},{10... | collective-permute-start | bytes 786440 | tf_op jit(solution)/shard_map/ppermute | solution.py:195
  34.6 12.0 %collective-permute-start.11 = (bf16[64,2048]{1,0:T(8,128)(2,1)S(1)}, bf16[64,2048]{1,0:T(8,128)(2,1)S(1)}, u32[]{:S(2)}, u32[]{:S(2)}) collective-permute-start(bf16[64,2048]{1,0:T(8,128)(2,1)S(1)} %shard_map.54.rest_4_), channel_id=1, source_target_pairs={{0,6},{1,7},{2,0},{3,1},{4,2},{5,3},{6,4},{7,5},{8,14},{9,15},{10,... | collective-permute-start | bytes 786440 | tf_op jit(solution)/shard_map/ppermute | solution.py:201
  37.3 9.7 %collective-permute-start.19 = (bf16[64,2048]{1,0:T(8,128)(2,1)S(1)}, bf16[64,2048]{1,0:T(8,128)(2,1)S(1)}, u32[]{:S(2)}, u32[]{:S(2)}) collective-permute-start(bf16[64,2048]{1,0:T(8,128)(2,1)S(1)} %shard_map.52.rest_0_), channel_id=1, source_target_pairs={{0,1},{1,0},{2,3},{3,2},{4,5},{5,4},{6,7},{7,6},{8,9},{9,8},{10,11... | collective-permute-start | bytes 786440 | tf_op jit(solution)/shard_map/ppermute | solution.py:198
  45.2 4.2 %collective-permute-start.18 = (bf16[64,2048]{1,0:T(8,128)(2,1)S(1)}, bf16[64,2048]{1,0:T(8,128)(2,1)S(1)}, u32[]{:S(2)}, u32[]{:S(2)}) collective-permute-start(bf16[64,2048]{1,0:T(8,128)(2,1)S(1)} %shard_map.60.rest_6_), channel_id=1, source_target_pairs={{0,8},{8,0},{16,24},{24,16},{1,9},{9,1},{17,25},{25,17},{2,10},{10... | collective-permute-start | bytes 786440 | tf_op jit(solution)/shard_map/ppermute | solution.py:195
  45.3 4.9 %collective-permute-start.16 = (bf16[64,2048]{1,0:T(8,128)(2,1)S(1)}, bf16[64,2048]{1,0:T(8,128)(2,1)S(1)}, u32[]{:S(2)}, u32[]{:S(2)}) collective-permute-start(bf16[64,2048]{1,0:T(8,128)(2,1)S(1)} %shard_map.59.rest_4_), channel_id=1, source_target_pairs={{0,8},{8,0},{16,24},{24,16},{1,9},{9,1},{17,25},{25,17},{2,10},{10... | collective-permute-start | bytes 786440 | tf_op jit(solution)/shard_map/ppermute | solution.py:195
  46.5 5.2 %collective-permute-start.14 = (bf16[64,2048]{1,0:T(8,128)(2,1)S(1)}, bf16[64,2048]{1,0:T(8,128)(2,1)S(1)}, u32[]{:S(2)}, u32[]{:S(2)}) collective-permute-start(bf16[64,2048]{1,0:T(8,128)(2,1)S(1)} %shard_map.58.rest_2_), channel_id=1, source_target_pairs={{0,8},{8,0},{16,24},{24,16},{1,9},{9,1},{17,25},{25,17},{2,10},{10... | collective-permute-start | bytes 786440 | tf_op jit(solution)/shard_map/ppermute | solution.py:195
  46.5 5.8 %collective-permute-start.12 = (bf16[64,2048]{1,0:T(8,128)(2,1)S(1)}, bf16[64,2048]{1,0:T(8,128)(2,1)S(1)}, u32[]{:S(2)}, u32[]{:S(2)}) collective-permute-start(bf16[64,2048]{1,0:T(8,128)(2,1)S(1)} %shard_map.57.rest_0_), channel_id=1, source_target_pairs={{0,8},{8,0},{16,24},{24,16},{1,9},{9,1},{17,25},{25,17},{2,10},{10... | collective-permute-start | bytes 786440 | tf_op jit(solution)/shard_map/ppermute | solution.py:195
  47.0 13.9 %collective-permute-start.28 = (bf16[64,2048]{1,0:T(8,128)(2,1)S(1)}, bf16[64,2048]{1,0:T(8,128)(2,1)S(1)}, u32[]{:S(2)}, u32[]{:S(2)}) collective-permute-start(bf16[64,2048]{1,0:T(8,128)(2,1)S(1)} %shard_map.53.rest_2_), channel_id=1, source_target_pairs={{0,6},{1,7},{2,0},{3,1},{4,2},{5,3},{6,4},{7,5},{8,14},{9,15},{10,... | collective-permute-start | bytes 786440 | tf_op jit(solution)/shard_map/ppermute | solution.py:201
  49.4 11.6 %collective-permute-start.26 = (bf16[64,2048]{1,0:T(8,128)(2,1)S(1)}, bf16[64,2048]{1,0:T(8,128)(2,1)S(1)}, u32[]{:S(2)}, u32[]{:S(2)}) collective-permute-start(bf16[64,2048]{1,0:T(8,128)(2,1)S(1)} %shard_map.57.rest_0_), channel_id=1, source_target_pairs={{0,1},{1,0},{2,3},{3,2},{4,5},{5,4},{6,7},{7,6},{8,9},{9,8},{10,11... | collective-permute-start | bytes 786440 | tf_op jit(solution)/shard_map/ppermute | solution.py:198
  50.3 11.2 %collective-permute-start.24 = (bf16[64,2048]{1,0:T(8,128)(2,1)S(1)}, bf16[64,2048]{1,0:T(8,128)(2,1)S(1)}, u32[]{:S(2)}, u32[]{:S(2)}) collective-permute-start(bf16[64,2048]{1,0:T(8,128)(2,1)S(1)} %shard_map.57.rest_0_), channel_id=1, source_target_pairs={{0,16},{8,24},{16,0},{24,8},{1,17},{9,25},{17,1},{25,9},{2,18},{10... | collective-permute-start | bytes 786440 | tf_op jit(solution)/shard_map/ppermute | solution.py:195
  51.8 12.0 %collective-permute-start.22 = (bf16[64,2048]{1,0:T(8,128)(2,1)S(1)}, bf16[64,2048]{1,0:T(8,128)(2,1)S(1)}, u32[]{:S(2)}, u32[]{:S(2)}) collective-permute-start(bf16[64,2048]{1,0:T(8,128)(2,1)S(1)} %shard_map.60.rest_6_), channel_id=1, source_target_pairs={{0,16},{8,24},{16,0},{24,8},{1,17},{9,25},{17,1},{25,9},{2,18},{10... | collective-permute-start | bytes 786440 | tf_op jit(solution)/shard_map/ppermute | solution.py:195
  52.3 11.5 %collective-permute-start.20 = (bf16[64,2048]{1,0:T(8,128)(2,1)S(1)}, bf16[64,2048]{1,0:T(8,128)(2,1)S(1)}, u32[]{:S(2)}, u32[]{:S(2)}) collective-permute-start(bf16[64,2048]{1,0:T(8,128)(2,1)S(1)} %shard_map.58.rest_2_), channel_id=1, source_target_pairs={{0,1},{1,0},{2,3},{3,2},{4,5},{5,4},{6,7},{7,6},{8,9},{9,8},{10,11... | collective-permute-start | bytes 786440 | tf_op jit(solution)/shard_map/ppermute | solution.py:198
  60.9 4.1 %collective-permute-start.30 = (bf16[64,2048]{1,0:T(8,128)(2,1)S(1)}, bf16[64,2048]{1,0:T(8,128)(2,1)S(1)}, u32[]{:S(2)}, u32[]{:S(2)}) collective-permute-start(bf16[64,2048]{1,0:T(8,128)(2,1)S(1)} %shard_map.61.rest_8_.rest_6_), channel_id=1, source_target_pairs={{0,8},{8,0},{16,24},{24,16},{1,9},{9,1},{17,25},{25,17},{2,10},{10... | collective-permute-start | bytes 786440 | tf_op jit(solution)/shard_map/ppermute | solution.py:195
  61.0 4.2 %collective-permute-start.29 = (bf16[64,2048]{1,0:T(8,128)(2,1)S(1)}, bf16[64,2048]{1,0:T(8,128)(2,1)S(1)}, u32[]{:S(2)}, u32[]{:S(2)}) collective-permute-start(bf16[64,2048]{1,0:T(8,128)(2,1)S(1)} %shard_map.67.rest_4_), channel_id=1, source_target_pairs={{0,8},{8,0},{16,24},{24,16},{1,9},{9,1},{17,25},{25,17},{2,10},{10... | collective-permute-start | bytes 786440 | tf_op jit(solution)/shard_map/ppermute | solution.py:195
  61.5 4.0 %collective-permute-start.27 = (bf16[64,2048]{1,0:T(8,128)(2,1)S(1)}, bf16[64,2048]{1,0:T(8,128)(2,1)S(1)}, u32[]{:S(2)}, u32[]{:S(2)}) collective-permute-start(bf16[64,2048]{1,0:T(8,128)(2,1)S(1)} %shard_map.66.rest_2_), channel_id=1, source_target_pairs={{0,8},{8,0},{16,24},{24,16},{1,9},{9,1},{17,25},{25,17},{2,10},{10... | collective-permute-start | bytes 786440 | tf_op jit(solution)/shard_map/ppermute | solution.py:195
  63.8 1.7 %collective-permute-start.25 = (bf16[64,2048]{1,0:T(8,128)(2,1)S(1)}, bf16[64,2048]{1,0:T(8,128)(2,1)S(1)}, u32[]{:S(2)}, u32[]{:S(2)}) collective-permute-start(bf16[64,2048]{1,0:T(8,128)(2,1)S(1)} %shard_map.65.rest_0_), channel_id=1, source_target_pairs={{0,8},{8,0},{16,24},{24,16},{1,9},{9,1},{17,25},{25,17},{2,10},{10... | collective-permute-start | bytes 786440 | tf_op jit(solution)/shard_map/ppermute | solution.py:195
  63.8 9.1 %collective-permute-start.31 = (bf16[64,2048]{1,0:T(8,128)(2,1)S(1)}, bf16[64,2048]{1,0:T(8,128)(2,1)S(1)}, u32[]{:S(2)}, u32[]{:S(2)}) collective-permute-start(bf16[64,2048]{1,0:T(8,128)(2,1)S(1)} %shard_map.65.rest_0_), channel_id=1, source_target_pairs={{0,1},{1,0},{2,3},{3,2},{4,5},{5,4},{6,7},{7,6},{8,9},{9,8},{10,11... | collective-permute-start | bytes 786440 | tf_op jit(solution)/shard_map/ppermute | solution.py:198
  65.0 8.2 %collective-permute-start.23 = (bf16[64,2048]{1,0:T(8,128)(2,1)S(1)}, bf16[64,2048]{1,0:T(8,128)(2,1)S(1)}, u32[]{:S(2)}, u32[]{:S(2)}) collective-permute-start(bf16[64,2048]{1,0:T(8,128)(2,1)S(1)} %shard_map.64.rest_9_.rest_2_), channel_id=1, source_target_pairs={{0,8},{8,0},{16,24},{24,16},{1,9},{9,1},{17,25},{25,17},{2,10},{10... | collective-permute-start | bytes 786440 | tf_op jit(solution)/shard_map/ppermute | solution.py:195
  65.2 8.0 %collective-permute-start.21 = (bf16[64,2048]{1,0:T(8,128)(2,1)S(1)}, bf16[64,2048]{1,0:T(8,128)(2,1)S(1)}, u32[]{:S(2)}, u32[]{:S(2)}) collective-permute-start(bf16[64,2048]{1,0:T(8,128)(2,1)S(1)} %shard_map.63.rest_8_.rest_0_), channel_id=1, source_target_pairs={{0,8},{8,0},{16,24},{24,16},{1,9},{9,1},{17,25},{25,17},{2,10},{10... | collective-permute-start | bytes 786440 | tf_op jit(solution)/shard_map/ppermute | solution.py:195
  72.9 1.6 %collective-permute-start.32 = (bf16[64,2048]{1,0:T(8,128)(2,1)S(1)}, bf16[64,2048]{1,0:T(8,128)(2,1)S(1)}, u32[]{:S(2)}, u32[]{:S(2)}) collective-permute-start(bf16[64,2048]{1,0:T(8,128)(2,1)S(1)} %shard_map.69.rest_4_), channel_id=1, source_target_pairs={{0,8},{8,0},{16,24},{24,16},{1,9},{9,1},{17,25},{25,17},{2,10},{10... | collective-permute-start | bytes 786440 | tf_op jit(solution)/shard_map/ppermute | solution.py:195

commit v5 on v4

--- a/solution.py
+++ b/solution.py
@@ -24,6 +24,10 @@
         compiler_params=pltpu.CompilerParams(vmem_limit_bytes=vmem << 20),
         cost_estimate=pl.CostEstimate(flops=0, bytes_accessed=0, transcendentals=0),
     )(*operands)
+
+
+def padded(depth):
+    return depth if depth <= 256 else -(-depth // 256) * 256
 
 
 def extract(bits, partners, integrals):
@@ -77,11 +81,21 @@
     return call(kernel, operands, specs, [(VMEM, pltpu.VMEM((depth, width), own.dtype))] * halves)
 
 
+def pick(first, second):
+    def kernel(first_ref, second_ref, out_ref):
+        core = lax.rem(lax.axis_index("occ"), 2)
+        flag = jnp.full((1, 1), core, jnp.int32) == 0
+        out_ref[...] = jnp.where(flag, first_ref[...], second_ref[...])
+
+    outs = [(VMEM, pltpu.VMEM(first.shape, first.dtype))]
+    return call(kernel, [first, second], [VMEM, VMEM], outs)[0]
+
+
 def prepare(where, partners, occ_energy, column, virt_halves, rows, groups, ready):
     height = rows.shape[0]
     local_virt, half = column.shape[0], virt_halves.shape[1]
     occ_dev, virt_size = height // local_virt, virt_halves.shape[0] // 2
-    widths = [half * len(places) for places in groups]
+    widths = [padded(half * len(places)) for places in groups]
 
     def kernel(where_ref, partners_ref, occ_energy_ref, column_ref, virt_ref, rows_ref, *rest):
         rest = rest[1:]
@@ -96,6 +110,7 @@
             own = occ_energy_ref[occ_index * occ_dev + i]
             row_energy_ref[pl.ds(i * local_virt, local_virt), :] = column_ref[...] - own
         for places, energy_ref in zip(groups, energy_refs):
+            energy_ref[...] = jnp.ones_like(energy_ref)
             for k, (ring_step, side, which, step) in enumerate(places):
                 position = lax.rem(virt_index + 2 * ring_step, virt_size)
                 position = position + side * (1 - 2 * lax.rem(position, 2))
@@ -120,7 +135,7 @@
 def contract(rows, row_energy, block_energy, blocks, waits, total, last):
     height, width = rows.shape
     count, depths = len(blocks), [block.shape[0] for block in blocks]
-    starts, depth = [sum(depths[:k]) for k in range(count)], sum(depths)
+    starts, depth = [sum(depths[:k]) for k in range(count)], padded(sum(depths))
     tile = max(t for t in range(16, 513, 16) if height % t == 0)
     tiles = height // tile
 
@@ -135,6 +150,8 @@
         for copy in copies:
             copy.start()
         token_ref[...] = jnp.zeros_like(token_ref)
+        if sum(depths) < depth:
+            held[sum(depths) :, :] = jnp.zeros((depth - sum(depths), width), held.dtype)
         for copy in copies:
             copy.wait()
         writes = []
@@ -200,18 +217,37 @@
     def shift_ring(value, k):
         return lax.ppermute(value, "virt", [(v, (v - 2 * k) % virt_size) for v in range(virt_size)])
 
+    def mix(value):
+        to = [(o ^ 2, v) if o % 2 == 0 else (o, v ^ 1) for o in range(occ_size) for v in range(virt_size)]
+        moves = [(n, o * virt_size + v) for n, (o, v) in enumerate(to)]
+        return lax.ppermute(value, ("occ", "virt"), moves)
+
     shifts = sorted(range(1, ring), key=lambda k: min(k, ring - k))
     early, late = shifts[: ring // 2], shifts[ring // 2 :]
-    even, odd, reach = early[0::2], early[1::2], (len(early) + 1) // 2
-    groups = [
-        [(0, 0, FIRST)],
-        [(0, 0, SECOND), (0, 1, FIRST)] + [(k, 0, FIRST) for k in early],
-        [(k, 0, FIRST) for k in late] + [(k, 0, SECOND) for k in early] + [(k, 1, FIRST) for k in odd],
-        [(k, 0, SECOND) for k in late] + [(k, 1, FIRST) for k in late + even] + [(0, 1, SECOND)],
-        [(k, 1, SECOND) for k in early + late],
-    ]
-    awaited = [[(0, 0, SECOND)], [], [(0, 1, SECOND)], [(k, 1, SECOND) for k in early], []]
-    places = [[(*place, step) for place in group for step in range(2)] for group in groups]
+    kinds = {"O": [0], "A": early[0::2], "B": early[1::2], "C": late}
+    reach = (len(early) + 1) // 2
+    plan = {
+        ("C", 0, SECOND): ("plane", 3, 3),
+        ("A", 1, SECOND): ("both", 4, 4),
+        ("A", 0, FIRST): ("ring", 1, 1),
+        ("O", 0, FIRST): ("own", 0, 1),
+        ("O", 1, SECOND): ("both", 2, 3),
+        ("B", 1, FIRST): ("shift", 3, 3),
+        ("B", 1, SECOND): ("both", 4, 4),
+        ("B", 0, SECOND): ("plane", 3, 4),
+        ("C", 0, FIRST): ("ring", 2, 2),
+        ("C", 1, FIRST): ("pair", 3, 3),
+        ("A", 0, SECOND): ("plane", 2, 2),
+        ("A", 1, FIRST): ("pair", 2, 2),
+        ("B", 0, FIRST): ("ring", 2, 2),
+        ("O", 0, SECOND): ("own", 1, 1),
+        ("O", 1, FIRST): ("pair", 1, 1),
+        ("C", 1, SECOND): ("both", 4, 4),
+    }
+    listed = [((k, side, half), *plan[kind, side, half]) for kind, side, half in plan for k in kinds[kind]]
+    stages = 1 + max(group for *_, group in listed)
+    groups = [[name for name, _, _, group in listed if group == n] for n in range(stages)]
+    places = [[(*name, step) for name in group for step in range(2)] for group in groups]
 
     where = jnp.stack([virt_index, occ_index]).astype(jnp.int32)
     column = lax.dynamic_slice_in_dim(virt_energy, virt_index * local_virt, local_virt)[:, None]
@@ -220,49 +256,47 @@
     own, sent, held = extract(bits, partners, integrals)
     first, second = choose(held, 0, own, swap_occ(sent, 1))
     rows, row_energy, token, energies = prepare(
-        where, partners, occ_energy, column, virt_halves, integrals.reshape(-1, aux_width), places, first
+        where, partners, occ_energy, column, virt_halves, integrals.reshape(-1, aux_width), [group for group in places if group], first
     )
     sent = [second, first]
     for n, bit in list(enumerate(bits))[1:]:
         (first,) = choose(held, n, first, swap_occ(sent[0] if bit == 2 else first, bit), token)
-    blocks = {(0, 0, FIRST): first, (0, 1, FIRST): swap_pair(first)}
-    for k in early:
-        blocks[k, 0, FIRST] = shift_ring(first, k)
     for n, bit in list(enumerate(bits))[1:]:
         got = swap_occ(sent[1] if bit == 2 else second, bit)
         (second,) = choose(held, n, second, got, token)
-    blocks[0, 0, SECOND] = second
-    total = None
-    for n, group in enumerate(groups):
-        if n > 0:
-            for name in [*group, *awaited[n]]:
-                if n == 1 or name not in awaited[n - 1]:
-                    (blocks[name],) = gate([token], [blocks[name]])
-        if n == 1:
-            for k in late:
-                near, step = (k - reach, reach) if k - reach in early else (k + reach, -reach)
-                blocks[k, 0, FIRST] = shift_ring(blocks[near, 0, FIRST], step)
-            for k in early:
-                blocks[k, 0, SECOND] = swap_occ(blocks[k, 0, FIRST], 2)
-            for k in odd:
-                blocks[k, 1, FIRST] = swap_pair(blocks[k, 0, FIRST])
-            for k in even:
-                blocks[k, 1, FIRST] = shift_ring(blocks[0, 1, FIRST], k)
-            blocks[0, 1, SECOND] = swap_pair(blocks[0, 0, SECOND])
-        if n == 2:
-            for k in late:
-                blocks[k, 0, SECOND] = swap_occ(blocks[k, 0, FIRST], 2)
-                blocks[k, 1, FIRST] = swap_pair(blocks[k, 0, FIRST])
-            for k in even:
-                blocks[k, 1, SECOND] = swap_pair(blocks[k, 0, SECOND])
-            for k in odd:
-                blocks[k, 1, SECOND] = swap_occ(blocks[k, 1, FIRST], 2)
-        if n == 3:
-            for k in late:
-                blocks[k, 1, SECOND] = swap_pair(blocks[k, 0, SECOND])
-        pairs = [block for name in group for block in (blocks[name], swap_occ(blocks[name], 1))]
-        waits = [blocks[name] for name in awaited[n]]
-        total, token = contract(rows, row_energy, energies[n], pairs, waits, total, n == len(groups) - 1)
+
+    blocks = {(0, 0, FIRST): first}
+
+    def fetch(name, move):
+        k, side, half = name
+        if move == "own":
+            return second
+        if move == "ring":
+            near = k - reach if (k - reach, 0, FIRST) in blocks else 0
+            return shift_ring(blocks[near, 0, FIRST], k - near)
+        if move == "plane":
+            return swap_occ(blocks[k, side, FIRST], 2)
+        if move == "pair":
+            return swap_pair(blocks[k, 0, half])
+        if move == "both":
+            return mix(pick(blocks[k, 1, FIRST], blocks[k, 0, SECOND]))
+        return shift_ring(blocks[0, side, half], k)
+
+    fetched, total = {}, None
+    for n in range(stages):
+        for name, move, stage, _ in listed:
+            if stage == n == 0 and name != (0, 0, FIRST):
+                blocks[name] = fetch(name, move)
+            if stage == n > 0:
+                (blocks[name],) = gate([token], [fetched[name]])
+        for name, move, stage, _ in listed:
+            if stage == n + 1:
+                fetched[name] = fetch(name, move)
+        if not groups[n]:
+            continue
+        pairs = [block for name in groups[n] for block in (blocks[name], swap_occ(blocks[name], 1))]
+        waits = [second] if n == 0 else [blocks[name] for name, _, stage, _ in listed if stage == n and name not in groups[n]]
+        total, token = contract(rows, row_energy, energies.pop(0), pairs, waits, total, n == stages - 1)
     return total.reshape(integrals.shape)
 
 

time: 84.3 us -> 78.5 us (0.931)
  Pallas kernels: 40.4 us -> 34.8 us
    pallas_call x25 -> x28, Pallas kernels: 40.4 us -> 34.8 us  [call(): pl.pallas_call(kernel, in_specs=in_specs, out_specs=[spec for spec, _ in...]
    ppermute x0 -> x4, starting transfers between devices: none -> 4.14 us  [mix(): return lax.ppermute(value, ('occ', 'virt'), moves)]
    ppermute x6 -> x3, starting transfers between devices: 6.9 us -> 4.56 us  [swap_pair(): return lax.ppermute(value, 'virt', [(v, v ^ 1) for v in range(virt_size)])]
    ppermute x23 -> x22, waiting for transfers between devices: 5.88 us -> 3.56 us  [swap_occ(): return lax.ppermute(value, 'occ', [(o, o ^ bit) for o in range(occ_size)])]
    ppermute x6 -> x3, waiting for transfers between devices: 0.02 us -> 2.2 us  [swap_pair(): return lax.ppermute(value, 'virt', [(v, v ^ 1) for v in range(virt_size)])]
    ppermute x23 -> x22, starting transfers between devices: 10.7 us -> 10.1 us  [swap_occ(): return lax.ppermute(value, 'occ', [(o, o ^ bit) for o in range(occ_size)])]
  transfers between devices with their start and end apart: 33 -> 33, of which waited for: 6 -> 10; matrix products, arithmetic and copies ran while one was open for 2% -> 2% of each run, Pallas kernels for 35% -> 30%
where the time goes in v5:
time: 78.5 us; the launch traced here: 78.2 us
  Pallas kernels  34.8 us (44%)
  starting transfers between devices  27.4 us (35%)
  waiting for transfers between devices  9.8 us (12%)
  local copies, waits for them, and re-layouts  5.72 us (7%)
    pallas_call x28, Pallas kernels, call(): pl.pallas_call(kernel, in_specs=in_specs, out_specs=[spec for spec, _ in...  34.8 us
    ppermute x22, starting transfers between devices, swap_occ(): return lax.ppermute(value, 'occ', [(o, o ^ bit) for o in range(occ_size)])  10.1 us
    ppermute x4, starting transfers between devices, shift_ring(): lax.ppermute(value, 'virt', [(v, (v - 2 * k) % virt_size) for v in range(...  8.6 us
    ppermute x3, starting transfers between devices, swap_pair(): return lax.ppermute(value, 'virt', [(v, v ^ 1) for v in range(virt_size)])  4.56 us
    ppermute x4, starting transfers between devices, mix(): return lax.ppermute(value, ('occ', 'virt'), moves)  4.14 us
    unnamed x6, local copies, waits for them, and re-layouts  4.09 us
    ppermute x4, waiting for transfers between devices, shift_ring(): lax.ppermute(value, 'virt', [(v, (v - 2 * k) % virt_size) for v in range(...  3.78 us
    ppermute x22, waiting for transfers between devices, swap_occ(): return lax.ppermute(value, 'occ', [(o, o ^ bit) for o in range(occ_size)])  3.56 us
  transfers between devices with their start and end apart: 33, of which 10 were waited for; matrix products, arithmetic and copies ran while one was open for 2% of the time, Pallas kernels for 30%

profile of v5, /device:TPU:0, one launch (start us, length us, event | category | flops | bytes accessed | tf_op | source)
XLA Modules:
  0.0 78.2 jit_solution(10648537768682275626)
XLA Ops:
  0.0 1.9 %shard_map.46 = (bf16[128,2048]{1,0:T(8,128)(2,1)S(1)}, bf16[128,2048]{1,0:T(8,128)(2,1)S(1)}, s32[16,128]{1,0:T(8,128)S(1)}) custom-call(s32[2]{0:T(128)} %partners_ref.3, bf16[12,128,2048]{2,1,0:T(8,128)(2,1)} %integrals_ref.1), custom_call_target="tpu_custom_call" | custom-call | tf_op jit(solution)/shard_map/pallas_call | solution.py:17
  1.9 0.5 collective-permute-start
  2.4 1.5 %collective-permute-done.got_ref = bf16[128,2048]{1,0:T(8,128)(2,1)S(1)} collective-permute-done((bf16[128,2048]{1,0:T(8,128)(2,1)S(1)}, bf16[128,2048]{1,0:T(8,128)(2,1)S(1)}, u32[]{:S(2)}, u32[]{:S(2)}) %collective-permute-start) | collective-permute-done | bytes 524320 | tf_op jit(solution)/shard_map/ppermute | solution.py:212
  4.0 0.1 shard_map.47
  4.1 2.9 %collective-permute-start.1 = (bf16[64,2048]{1,0:T(8,128)(2,1)S(1)}, bf16[64,2048]{1,0:T(8,128)(2,1)S(1)}, u32[]{:S(2)}, u32[]{:S(2)}) collective-permute-start(bf16[64,2048]{1,0:T(8,128)(2,1)S(1)} %get-tuple-element.35.own_ref), channel_id=1, source_target_pairs={{0,16},{8,24},{16,0},{24,8},{1,17},{9,25},{17,1},{25,9},{2,18},{10... | collective-permute-start | bytes 786440 | tf_op jit(solution)/shard_map/ppermute | solution.py:212
  7.0 0.8 reshape.9.virt_ref
  7.7 0.8 dynamic-slice_bitcast_fusion
  8.5 0.1 copy.22.column_ref
  8.6 0.1 pad_add_fusion.where_ref
  8.7 0.0 collective-permute-start.5
  8.7 2.8 %copy-done = bf16[12,128,2048]{2,1,0:T(8,128)(2,1)S(1)} copy-done((bf16[12,128,2048]{2,1,0:T(8,128)(2,1)S(1)}, bf16[12,128,2048]{2,1,0:T(8,128)(2,1)}, u32[]{:S(2)}) %copy-start) | copy-done | bytes 6291480
  11.5 0.7 copy-done.1
  12.2 0.7 copy-done.2
  12.8 1.1 %shard_map.48 = (bf16[1536,2048]{1,0:T(8,128)(2,1)S(1)}, f32[1536,1]{1,0:T(8,128)S(1)}, f32[8,128]{1,0:T(8,128)S(1)}, f32[1,512]{1,0:T(1,128)S(1)}, f32[1,512]{1...) custom-call(s32[2]{0:T(128)S(1)} %pad_add_fusion.where_ref, s32[2]{0:T(128)S(1)} %copy-done.1, ...), custom_call_target="tpu_custom_call" | custom-call | tf_op jit(solution)/shard_map/pallas_call | solution.py:17
  14.0 0.1 collective-permute-done.1.got_ref
  14.1 0.1 shard_map.49.rest_2_
  14.1 4.2 %collective-permute-start.2 = (bf16[64,2048]{1,0:T(8,128)(2,1)S(1)}, bf16[64,2048]{1,0:T(8,128)(2,1)S(1)}, u32[]{:S(2)}, u32[]{:S(2)}) collective-permute-start(bf16[64,2048]{1,0:T(8,128)(2,1)S(1)} %shard_map.49.rest_2_), channel_id=1, source_target_pairs={{0,6},{1,7},{2,0},{3,1},{4,2},{5,3},{6,4},{7,5},{8,14},{9,15},{10,... | collective-permute-start | bytes 786440 | tf_op jit(solution)/shard_map/ppermute | solution.py:218
  18.4 1.5 %collective-permute-start.7 = (bf16[64,2048]{1,0:T(8,128)(2,1)S(1)}, bf16[64,2048]{1,0:T(8,128)(2,1)S(1)}, u32[]{:S(2)}, u32[]{:S(2)}) collective-permute-start(bf16[64,2048]{1,0:T(8,128)(2,1)S(1)} %shard_map.49.rest_2_), channel_id=1, source_target_pairs={{0,1},{1,0},{2,3},{3,2},{4,5},{5,4},{6,7},{7,6},{8,9},{9,8},{10,11... | collective-permute-start | bytes 786440 | tf_op jit(solution)/shard_map/ppermute | solution.py:215
  19.9 0.0 collective-permute-done.5.got_ref
  19.9 0.1 shard_map.51.refs_1_
  20.0 0.6 collective-permute-start.6
  20.5 3.0 %collective-permute-done.2.refs_1_ = bf16[64,2048]{1,0:T(8,128)(2,1)S(1)} collective-permute-done((bf16[64,2048]{1,0:T(8,128)(2,1)S(1)}, bf16[64,2048]{1,0:T(8,128)(2,1)S(1)}, u32[]{:S(2)}, u32[]{:S(2)}) %collective-permute-start.2) | collective-permute-done | bytes 262176 | tf_op jit(solution)/shard_map/ppermute | solution.py:218
  23.5 0.0 collective-permute-start.3
  23.5 2.2 %collective-permute-done.7.refs_1_ = bf16[64,2048]{1,0:T(8,128)(2,1)S(1)} collective-permute-done((bf16[64,2048]{1,0:T(8,128)(2,1)S(1)}, bf16[64,2048]{1,0:T(8,128)(2,1)S(1)}, u32[]{:S(2)}, u32[]{:S(2)}) %collective-permute-start.7) | collective-permute-done | bytes 262176 | tf_op jit(solution)/shard_map/ppermute | solution.py:215
  25.7 0.0 collective-permute-start.8
  25.7 2.6 %collective-permute-start.9 = (bf16[64,2048]{1,0:T(8,128)(2,1)S(1)}, bf16[64,2048]{1,0:T(8,128)(2,1)S(1)}, u32[]{:S(2)}, u32[]{:S(2)}) collective-permute-start(bf16[64,2048]{1,0:T(8,128)(2,1)S(1)} %shard_map.50.rest_0_), channel_id=1, source_target_pairs={{0,6},{1,7},{2,0},{3,1},{4,2},{5,3},{6,4},{7,5},{8,14},{9,15},{10,... | collective-permute-start | bytes 786440 | tf_op jit(solution)/shard_map/ppermute | solution.py:218
  28.3 0.0 collective-permute-done.4.rest_3_
  28.3 1.5 %collective-permute-start.11 = (bf16[64,2048]{1,0:T(8,128)(2,1)S(1)}, bf16[64,2048]{1,0:T(8,128)(2,1)S(1)}, u32[]{:S(2)}, u32[]{:S(2)}) collective-permute-start(bf16[64,2048]{1,0:T(8,128)(2,1)S(1)} %shard_map.50.rest_0_), channel_id=1, source_target_pairs={{0,16},{8,24},{16,0},{24,8},{1,17},{9,25},{17,1},{25,9},{2,18},{10... | collective-permute-start | bytes 786440 | tf_op jit(solution)/shard_map/ppermute | solution.py:212
  29.8 0.0 collective-permute-done.6.rest_5_
  29.8 1.5 %collective-permute-start.13 = (bf16[64,2048]{1,0:T(8,128)(2,1)S(1)}, bf16[64,2048]{1,0:T(8,128)(2,1)S(1)}, u32[]{:S(2)}, u32[]{:S(2)}) collective-permute-start(bf16[64,2048]{1,0:T(8,128)(2,1)S(1)} %shard_map.50.rest_0_), channel_id=1, source_target_pairs={{0,1},{1,0},{2,3},{3,2},{4,5},{5,4},{6,7},{7,6},{8,9},{9,8},{10,11... | collective-permute-start | bytes 786440 | tf_op jit(solution)/shard_map/ppermute | solution.py:215
  31.3 0.0 collective-permute-start.15
  31.4 0.0 collective-permute-done.8.rest_7_
  31.4 0.6 collective-permute-start.17
  32.0 7.1 %shard_map.54 = (f32[1536,2048]{1,0:T(8,128)S(1)}, f32[8,128]{1,0:T(8,128)S(1)}) custom-call(bf16[1536,2048]{1,0:T(8,128)(2,1)S(1)} %get-tuple-element.28.rows_ref, f32[1536,1]{1,0:T(8,128)S(1)} %get-tuple-element.29.row_energy_ref, f32[1,512]{1,0:T(1,128)S(1)} %get-tuple-element.33.block_energy_ref, bf16[64,2048]{1,0:T(8,128)(2,1)S(1)} %shard_map.50.rest_0_, ...), custom_call_target="tpu_custom_call" | custom-call | tf_op jit(solution)/shard_map/pallas_call | solution.py:17
  39.1 0.1 collective-permute-start.10
  39.2 0.0 collective-permute-done.11.refs_1_
  39.2 0.5 collective-permute-start.12
  39.7 0.1 collective-permute-start.14
  39.8 0.8 %collective-permute-done.15.refs_1_ = bf16[64,2048]{1,0:T(8,128)(2,1)S(1)} collective-permute-done((bf16[64,2048]{1,0:T(8,128)(2,1)S(1)}, bf16[64,2048]{1,0:T(8,128)(2,1)S(1)}, u32[]{:S(2)}, u32[]{:S(2)}) %collective-permute-start.15) | collective-permute-done | bytes 262176 | tf_op jit(solution)/shard_map/ppermute | solution.py:218
  40.6 0.0 collective-permute-start.16
  40.6 0.0 collective-permute-done.17.refs_1_
  40.6 1.4 %collective-permute-start.18 = (bf16[64,2048]{1,0:T(8,128)(2,1)S(1)}, bf16[64,2048]{1,0:T(8,128)(2,1)S(1)}, u32[]{:S(2)}, u32[]{:S(2)}) collective-permute-start(bf16[64,2048]{1,0:T(8,128)(2,1)S(1)} %shard_map.55.rest_0_), channel_id=1, source_target_pairs={{0,16},{8,24},{16,0},{24,8},{1,17},{9,25},{17,1},{25,9},{2,18},{10... | collective-permute-start | bytes 786440 | tf_op jit(solution)/shard_map/ppermute | solution.py:212
  42.0 1.8 %collective-permute-start.21 = (bf16[64,2048]{1,0:T(8,128)(2,1)S(1)}, bf16[64,2048]{1,0:T(8,128)(2,1)S(1)}, u32[]{:S(2)}, u32[]{:S(2)}) collective-permute-start(bf16[64,2048]{1,0:T(8,128)(2,1)S(1)} %shard_map.53.rest_6_.first_ref), channel_id=1, source_target_pairs={{0,2},{1,3},{2,4},{3,5},{4,6},{5,7},{6,0},{7,1},{8,10},{9,11},{10,... | collective-permute-start | bytes 786440 | tf_op jit(solution)/shard_map/ppermute | solution.py:218
  43.8 1.5 %collective-permute-start.23 = (bf16[64,2048]{1,0:T(8,128)(2,1)S(1)}, bf16[64,2048]{1,0:T(8,128)(2,1)S(1)}, u32[]{:S(2)}, u32[]{:S(2)}) collective-permute-start(bf16[64,2048]{1,0:T(8,128)(2,1)S(1)} %shard_map.55.rest_0_), channel_id=1, source_target_pairs={{0,1},{1,0},{2,3},{3,2},{4,5},{5,4},{6,7},{7,6},{8,9},{9,8},{10,11... | collective-permute-start | bytes 786440 | tf_op jit(solution)/shard_map/ppermute | solution.py:215
  45.3 0.0 collective-permute-done.14.rest_5_
  45.3 0.5 collective-permute-start.25
  45.9 0.0 collective-permute-done.16.rest_7_
  45.9 7.4 %shard_map.61 = (f32[1536,2048]{1,0:T(8,128)S(1)}, f32[8,128]{1,0:T(8,128)S(1)}) custom-call(bf16[1536,2048]{1,0:T(8,128)(2,1)S(1)} %get-tuple-element.28.rows_ref, f32[1536,1]{1,0:T(8,128)S(1)} %get-tuple-element.29.row_energy_ref, f32[1,512]{1,0:T(1,128)S(1)} %get-tuple-element.32.block_energy_ref, ...), custom_call_target="tpu_custom_call", output_to_operand_aliasing={{0}: (12, {})} | custom-call | tf_op jit(solution)/shard_map/pallas_call | solution.py:17
  53.3 0.6 collective-permute-start.19
  53.9 0.1 collective-permute-start.22
  54.0 0.4 collective-permute-start.24
  54.4 0.5 collective-permute-done.25.refs_1_
  54.9 1.4 %collective-permute-start.26 = (bf16[64,2048]{1,0:T(8,128)(2,1)S(1)}, bf16[64,2048]{1,0:T(8,128)(2,1)S(1)}, u32[]{:S(2)}, u32[]{:S(2)}) collective-permute-start(bf16[64,2048]{1,0:T(8,128)(2,1)S(1)} %shard_map.67), channel_id=1, source_target_pairs={{0,16},{1,17},{2,18},{3,19},{4,20},{5,21},{6,22},{7,23},{8,9},{9,8... | collective-permute-start | bytes 786440 | tf_op jit(solution)/shard_map/ppermute | solution.py:223
  56.3 0.7 collective-permute-start.28
  57.1 1.4 %collective-permute-start.31 = (bf16[64,2048]{1,0:T(8,128)(2,1)S(1)}, bf16[64,2048]{1,0:T(8,128)(2,1)S(1)}, u32[]{:S(2)}, u32[]{:S(2)}) collective-permute-start(bf16[64,2048]{1,0:T(8,128)(2,1)S(1)} %shard_map.71), channel_id=1, source_target_pairs={{0,16},{1,17},{2,18},{3,19},{4,20},{5,21},{6,22},{7,23},{8,9},{9,8... | collective-permute-start | bytes 786440 | tf_op jit(solution)/shard_map/ppermute | solution.py:223
  58.6 7.4 %shard_map.66 = (f32[1536,2048]{1,0:T(8,128)S(1)}, f32[8,128]{1,0:T(8,128)S(1)}) custom-call(bf16[1536,2048]{1,0:T(8,128)(2,1)S(1)} %get-tuple-element.28.rows_ref, f32[1536,1]{1,0:T(8,128)S(1)} %get-tuple-element.29.row_energy_ref, f32[1,512]{1,0:T(1,128)S(1)} %get-tuple-element.31.block_energy_ref, ...), custom_call_target="tpu_custom_call", output_to_operand_aliasing={{0}: (12, {})} | custom-call | tf_op jit(solution)/shard_map/pallas_call | solution.py:17
  66.0 0.6 collective-permute-start.27
  66.6 0.1 collective-permute-start.29
  66.7 0.2 collective-permute-done.31.refs_1_
  66.9 0.2 collective-permute-start.32
  67.1 0.6 collective-permute-done.27.rest_1_
  67.7 0.4 collective-permute-done.29.rest_3_
  68.1 0.4 collective-permute-done.32.rest_7_
  68.5 9.6 %shard_map.73 = (bf16[1536,2048]{1,0:T(8,128)(2,1)}, f32[8,128]{1,0:T(8,128)}) custom-call(bf16[1536,2048]{1,0:T(8,128)(2,1)S(1)} %get-tuple-element.28.rows_ref, f32[1536,1]{1,0:T(8,128)S(1)} %get-tuple-element.29.row_energy_ref, f32[1,512]{1,0:T(1,128)S(1)} %get-tuple-element.30.block_energy_ref, bf16[64,2048]{1,0:T(8,128)(2,1)S(1)} %shard_map.68.rest_0_, ...), custom_call_target="tpu_custom_call" | custom-call | tf_op jit(solution)/shard_map/pallas_call | solution.py:17
  (40 shorter events, 0.2 us)
Async XLA Ops:
  1.9 2.1 %collective-permute-start = (bf16[128,2048]{1,0:T(8,128)(2,1)S(1)}, bf16[128,2048]{1,0:T(8,128)(2,1)S(1)}, u32[]{:S(2)}, u32[]{:S(2)}) collective-permute-start(bf16[128,2048]{1,0:T(8,128)(2,1)S(1)} %get-tuple-element.26), channel_id=1, source_target_pairs={{0,8},{8,0},{16,24},{24,16},{1,9},{9,1},{17,25},{25,17},{2,10},{10... | collective-permute-start | bytes 1572872 | tf_op jit(solution)/shard_map/ppermute | solution.py:212
  4.1 10.0 %collective-permute-start.1 = (bf16[64,2048]{1,0:T(8,128)(2,1)S(1)}, bf16[64,2048]{1,0:T(8,128)(2,1)S(1)}, u32[]{:S(2)}, u32[]{:S(2)}) collective-permute-start(bf16[64,2048]{1,0:T(8,128)(2,1)S(1)} %get-tuple-element.35.own_ref), channel_id=1, source_target_pairs={{0,16},{8,24},{16,0},{24,8},{1,17},{9,25},{17,1},{25,9},{2,18},{10... | collective-permute-start | bytes 786440 | tf_op jit(solution)/shard_map/ppermute | solution.py:212
  8.7 11.2 %collective-permute-start.5 = (bf16[64,2048]{1,0:T(8,128)(2,1)S(1)}, bf16[64,2048]{1,0:T(8,128)(2,1)S(1)}, u32[]{:S(2)}, u32[]{:S(2)}) collective-permute-start(bf16[64,2048]{1,0:T(8,128)(2,1)S(1)} %get-tuple-element.27.rest_0_.own_ref), channel_id=1, source_target_pairs={{0,16},{8,24},{16,0},{24,8},{1,17},{9,25},{17,1},{25,9},{2,18},{10... | collective-permute-start | bytes 786440 | tf_op jit(solution)/shard_map/ppermute | solution.py:212
  8.7 2.8 %copy-start = (bf16[12,128,2048]{2,1,0:T(8,128)(2,1)S(1)}, bf16[12,128,2048]{2,1,0:T(8,128)(2,1)}, u32[]{:S(2)}) copy-start(bf16[12,128,2048]{2,1,0:T(8,128)(2,1)} %integrals_ref.1) | copy-start | bytes 18874372
  11.5 0.7 copy-start.1
  12.2 0.7 copy-start.2
  14.1 9.4 %collective-permute-start.2 = (bf16[64,2048]{1,0:T(8,128)(2,1)S(1)}, bf16[64,2048]{1,0:T(8,128)(2,1)S(1)}, u32[]{:S(2)}, u32[]{:S(2)}) collective-permute-start(bf16[64,2048]{1,0:T(8,128)(2,1)S(1)} %shard_map.49.rest_2_), channel_id=1, source_target_pairs={{0,6},{1,7},{2,0},{3,1},{4,2},{5,3},{6,4},{7,5},{8,14},{9,15},{10,... | collective-permute-start | bytes 786440 | tf_op jit(solution)/shard_map/ppermute | solution.py:218
  18.4 7.3 %collective-permute-start.7 = (bf16[64,2048]{1,0:T(8,128)(2,1)S(1)}, bf16[64,2048]{1,0:T(8,128)(2,1)S(1)}, u32[]{:S(2)}, u32[]{:S(2)}) collective-permute-start(bf16[64,2048]{1,0:T(8,128)(2,1)S(1)} %shard_map.49.rest_2_), channel_id=1, source_target_pairs={{0,1},{1,0},{2,3},{3,2},{4,5},{5,4},{6,7},{7,6},{8,9},{9,8},{10,11... | collective-permute-start | bytes 786440 | tf_op jit(solution)/shard_map/ppermute | solution.py:215
  19.9 8.4 %collective-permute-start.4 = (bf16[64,2048]{1,0:T(8,128)(2,1)S(1)}, bf16[64,2048]{1,0:T(8,128)(2,1)S(1)}, u32[]{:S(2)}, u32[]{:S(2)}) collective-permute-start(bf16[64,2048]{1,0:T(8,128)(2,1)S(1)} %shard_map.49.rest_2_), channel_id=1, source_target_pairs={{0,8},{8,0},{16,24},{24,16},{1,9},{9,1},{17,25},{25,17},{2,10},{10... | collective-permute-start | bytes 786440 | tf_op jit(solution)/shard_map/ppermute | solution.py:212
  20.0 9.8 %collective-permute-start.6 = (bf16[64,2048]{1,0:T(8,128)(2,1)S(1)}, bf16[64,2048]{1,0:T(8,128)(2,1)S(1)}, u32[]{:S(2)}, u32[]{:S(2)}) collective-permute-start(bf16[64,2048]{1,0:T(8,128)(2,1)S(1)} %shard_map.52.rest_4_.second_ref), channel_id=1, source_target_pairs={{0,8},{8,0},{16,24},{24,16},{1,9},{9,1},{17,25},{25,17},{2,10},{10... | collective-permute-start | bytes 786440 | tf_op jit(solution)/shard_map/ppermute | solution.py:212
  23.5 7.8 %collective-permute-start.3 = (bf16[64,2048]{1,0:T(8,128)(2,1)S(1)}, bf16[64,2048]{1,0:T(8,128)(2,1)S(1)}, u32[]{:S(2)}, u32[]{:S(2)}) collective-permute-start(bf16[64,2048]{1,0:T(8,128)(2,1)S(1)} %shard_map.50.rest_0_), channel_id=1, source_target_pairs={{0,8},{8,0},{16,24},{24,16},{1,9},{9,1},{17,25},{25,17},{2,10},{10... | collective-permute-start | bytes 786440 | tf_op jit(solution)/shard_map/ppermute | solution.py:212
  25.7 5.7 %collective-permute-start.8 = (bf16[64,2048]{1,0:T(8,128)(2,1)S(1)}, bf16[64,2048]{1,0:T(8,128)(2,1)S(1)}, u32[]{:S(2)}, u32[]{:S(2)}) collective-permute-start(bf16[64,2048]{1,0:T(8,128)(2,1)S(1)} %shard_map.53.rest_6_.first_ref), channel_id=1, source_target_pairs={{0,8},{8,0},{16,24},{24,16},{1,9},{9,1},{17,25},{25,17},{2,10},{10... | collective-permute-start | bytes 786440 | tf_op jit(solution)/shard_map/ppermute | solution.py:212
  25.7 13.3 %collective-permute-start.9 = (bf16[64,2048]{1,0:T(8,128)(2,1)S(1)}, bf16[64,2048]{1,0:T(8,128)(2,1)S(1)}, u32[]{:S(2)}, u32[]{:S(2)}) collective-permute-start(bf16[64,2048]{1,0:T(8,128)(2,1)S(1)} %shard_map.50.rest_0_), channel_id=1, source_target_pairs={{0,6},{1,7},{2,0},{3,1},{4,2},{5,3},{6,4},{7,5},{8,14},{9,15},{10,... | collective-permute-start | bytes 786440 | tf_op jit(solution)/shard_map/ppermute | solution.py:218
  28.3 10.9 %collective-permute-start.11 = (bf16[64,2048]{1,0:T(8,128)(2,1)S(1)}, bf16[64,2048]{1,0:T(8,128)(2,1)S(1)}, u32[]{:S(2)}, u32[]{:S(2)}) collective-permute-start(bf16[64,2048]{1,0:T(8,128)(2,1)S(1)} %shard_map.50.rest_0_), channel_id=1, source_target_pairs={{0,16},{8,24},{16,0},{24,8},{1,17},{9,25},{17,1},{25,9},{2,18},{10... | collective-permute-start | bytes 786440 | tf_op jit(solution)/shard_map/ppermute | solution.py:212
  29.8 9.9 %collective-permute-start.13 = (bf16[64,2048]{1,0:T(8,128)(2,1)S(1)}, bf16[64,2048]{1,0:T(8,128)(2,1)S(1)}, u32[]{:S(2)}, u32[]{:S(2)}) collective-permute-start(bf16[64,2048]{1,0:T(8,128)(2,1)S(1)} %shard_map.50.rest_0_), channel_id=1, source_target_pairs={{0,1},{1,0},{2,3},{3,2},{4,5},{5,4},{6,7},{7,6},{8,9},{9,8},{10,11... | collective-permute-start | bytes 786440 | tf_op jit(solution)/shard_map/ppermute | solution.py:215
  31.3 9.2 %collective-permute-start.15 = (bf16[64,2048]{1,0:T(8,128)(2,1)S(1)}, bf16[64,2048]{1,0:T(8,128)(2,1)S(1)}, u32[]{:S(2)}, u32[]{:S(2)}) collective-permute-start(bf16[64,2048]{1,0:T(8,128)(2,1)S(1)} %shard_map.49.rest_2_), channel_id=1, source_target_pairs={{0,2},{1,3},{2,4},{3,5},{4,6},{5,7},{6,0},{7,1},{8,10},{9,11},{10,... | collective-permute-start | bytes 786440 | tf_op jit(solution)/shard_map/ppermute | solution.py:218
  31.4 9.2 %collective-permute-start.17 = (bf16[64,2048]{1,0:T(8,128)(2,1)S(1)}, bf16[64,2048]{1,0:T(8,128)(2,1)S(1)}, u32[]{:S(2)}, u32[]{:S(2)}) collective-permute-start(bf16[64,2048]{1,0:T(8,128)(2,1)S(1)} %shard_map.59), channel_id=1, source_target_pairs={{0,16},{1,17},{2,18},{3,19},{4,20},{5,21},{6,22},{7,23},{8,9},{9,8... | collective-permute-start | bytes 786440 | tf_op jit(solution)/shard_map/ppermute | solution.py:223
  39.1 2.9 %collective-permute-start.10 = (bf16[64,2048]{1,0:T(8,128)(2,1)S(1)}, bf16[64,2048]{1,0:T(8,128)(2,1)S(1)}, u32[]{:S(2)}, u32[]{:S(2)}) collective-permute-start(bf16[64,2048]{1,0:T(8,128)(2,1)S(1)} %shard_map.55.rest_0_), channel_id=1, source_target_pairs={{0,8},{8,0},{16,24},{24,16},{1,9},{9,1},{17,25},{25,17},{2,10},{10... | collective-permute-start | bytes 786440 | tf_op jit(solution)/shard_map/ppermute | solution.py:212
  39.2 4.6 %collective-permute-start.12 = (bf16[64,2048]{1,0:T(8,128)(2,1)S(1)}, bf16[64,2048]{1,0:T(8,128)(2,1)S(1)}, u32[]{:S(2)}, u32[]{:S(2)}) collective-permute-start(bf16[64,2048]{1,0:T(8,128)(2,1)S(1)} %shard_map.56.rest_2_.second_ref), channel_id=1, source_target_pairs={{0,8},{8,0},{16,24},{24,16},{1,9},{9,1},{17,25},{25,17},{2,10},{10... | collective-permute-start | bytes 786440 | tf_op jit(solution)/shard_map/ppermute | solution.py:212
  39.7 5.7 %collective-permute-start.14 = (bf16[64,2048]{1,0:T(8,128)(2,1)S(1)}, bf16[64,2048]{1,0:T(8,128)(2,1)S(1)}, u32[]{:S(2)}, u32[]{:S(2)}) collective-permute-start(bf16[64,2048]{1,0:T(8,128)(2,1)S(1)} %shard_map.57.rest_4_.first_ref), channel_id=1, source_target_pairs={{0,8},{8,0},{16,24},{24,16},{1,9},{9,1},{17,25},{25,17},{2,10},{10... | collective-permute-start | bytes 786440 | tf_op jit(solution)/shard_map/ppermute | solution.py:212
  40.6 5.3 %collective-permute-start.16 = (bf16[64,2048]{1,0:T(8,128)(2,1)S(1)}, bf16[64,2048]{1,0:T(8,128)(2,1)S(1)}, u32[]{:S(2)}, u32[]{:S(2)}) collective-permute-start(bf16[64,2048]{1,0:T(8,128)(2,1)S(1)} %shard_map.58.rest_6_), channel_id=1, source_target_pairs={{0,8},{8,0},{16,24},{24,16},{1,9},{9,1},{17,25},{25,17},{2,10},{10... | collective-permute-start | bytes 786440 | tf_op jit(solution)/shard_map/ppermute | solution.py:212
  40.6 12.7 %collective-permute-start.18 = (bf16[64,2048]{1,0:T(8,128)(2,1)S(1)}, bf16[64,2048]{1,0:T(8,128)(2,1)S(1)}, u32[]{:S(2)}, u32[]{:S(2)}) collective-permute-start(bf16[64,2048]{1,0:T(8,128)(2,1)S(1)} %shard_map.55.rest_0_), channel_id=1, source_target_pairs={{0,16},{8,24},{16,0},{24,8},{1,17},{9,25},{17,1},{25,9},{2,18},{10... | collective-permute-start | bytes 786440 | tf_op jit(solution)/shard_map/ppermute | solution.py:212
  42.0 11.9 %collective-permute-start.21 = (bf16[64,2048]{1,0:T(8,128)(2,1)S(1)}, bf16[64,2048]{1,0:T(8,128)(2,1)S(1)}, u32[]{:S(2)}, u32[]{:S(2)}) collective-permute-start(bf16[64,2048]{1,0:T(8,128)(2,1)S(1)} %shard_map.53.rest_6_.first_ref), channel_id=1, source_target_pairs={{0,2},{1,3},{2,4},{3,5},{4,6},{5,7},{6,0},{7,1},{8,10},{9,11},{10,... | collective-permute-start | bytes 786440 | tf_op jit(solution)/shard_map/ppermute | solution.py:218
  43.8 10.2 %collective-permute-start.23 = (bf16[64,2048]{1,0:T(8,128)(2,1)S(1)}, bf16[64,2048]{1,0:T(8,128)(2,1)S(1)}, u32[]{:S(2)}, u32[]{:S(2)}) collective-permute-start(bf16[64,2048]{1,0:T(8,128)(2,1)S(1)} %shard_map.55.rest_0_), channel_id=1, source_target_pairs={{0,1},{1,0},{2,3},{3,2},{4,5},{5,4},{6,7},{7,6},{8,9},{9,8},{10,11... | collective-permute-start | bytes 786440 | tf_op jit(solution)/shard_map/ppermute | solution.py:215
  45.3 9.6 %collective-permute-start.25 = (bf16[64,2048]{1,0:T(8,128)(2,1)S(1)}, bf16[64,2048]{1,0:T(8,128)(2,1)S(1)}, u32[]{:S(2)}, u32[]{:S(2)}) collective-permute-start(bf16[64,2048]{1,0:T(8,128)(2,1)S(1)} %shard_map.58.rest_6_), channel_id=1, source_target_pairs={{0,16},{8,24},{16,0},{24,8},{1,17},{9,25},{17,1},{25,9},{2,18},{10... | collective-permute-start | bytes 786440 | tf_op jit(solution)/shard_map/ppermute | solution.py:212
  45.9 10.5 %collective-permute-start.20 = (bf16[64,2048]{1,0:T(8,128)(2,1)S(1)}, bf16[64,2048]{1,0:T(8,128)(2,1)S(1)}, u32[]{:S(2)}, u32[]{:S(2)}) collective-permute-start(bf16[64,2048]{1,0:T(8,128)(2,1)S(1)} %shard_map.60.rest_8_.rest_2_), channel_id=1, source_target_pairs={{0,8},{8,0},{16,24},{24,16},{1,9},{9,1},{17,25},{25,17},{2,10},{10... | collective-permute-start | bytes 786440 | tf_op jit(solution)/shard_map/ppermute | solution.py:212
  53.3 3.8 %collective-permute-start.19 = (bf16[64,2048]{1,0:T(8,128)(2,1)S(1)}, bf16[64,2048]{1,0:T(8,128)(2,1)S(1)}, u32[]{:S(2)}, u32[]{:S(2)}) collective-permute-start(bf16[64,2048]{1,0:T(8,128)(2,1)S(1)} %shard_map.62.rest_0_.second_ref), channel_id=1, source_target_pairs={{0,8},{8,0},{16,24},{24,16},{1,9},{9,1},{17,25},{25,17},{2,10},{10... | collective-permute-start | bytes 786440 | tf_op jit(solution)/shard_map/ppermute | solution.py:212
  53.9 4.7 %collective-permute-start.22 = (bf16[64,2048]{1,0:T(8,128)(2,1)S(1)}, bf16[64,2048]{1,0:T(8,128)(2,1)S(1)}, u32[]{:S(2)}, u32[]{:S(2)}) collective-permute-start(bf16[64,2048]{1,0:T(8,128)(2,1)S(1)} %shard_map.63.rest_4_.first_ref), channel_id=1, source_target_pairs={{0,8},{8,0},{16,24},{24,16},{1,9},{9,1},{17,25},{25,17},{2,10},{10... | collective-permute-start | bytes 786440 | tf_op jit(solution)/shard_map/ppermute | solution.py:212
  54.0 4.6 %collective-permute-start.24 = (bf16[64,2048]{1,0:T(8,128)(2,1)S(1)}, bf16[64,2048]{1,0:T(8,128)(2,1)S(1)}, u32[]{:S(2)}, u32[]{:S(2)}) collective-permute-start(bf16[64,2048]{1,0:T(8,128)(2,1)S(1)} %shard_map.64.rest_6_.first_ref), channel_id=1, source_target_pairs={{0,8},{8,0},{16,24},{24,16},{1,9},{9,1},{17,25},{25,17},{2,10},{10... | collective-permute-start | bytes 786440 | tf_op jit(solution)/shard_map/ppermute | solution.py:212
  54.9 11.1 %collective-permute-start.26 = (bf16[64,2048]{1,0:T(8,128)(2,1)S(1)}, bf16[64,2048]{1,0:T(8,128)(2,1)S(1)}, u32[]{:S(2)}, u32[]{:S(2)}) collective-permute-start(bf16[64,2048]{1,0:T(8,128)(2,1)S(1)} %shard_map.67), channel_id=1, source_target_pairs={{0,16},{1,17},{2,18},{3,19},{4,20},{5,21},{6,22},{7,23},{8,9},{9,8... | collective-permute-start | bytes 786440 | tf_op jit(solution)/shard_map/ppermute | solution.py:223
  56.3 10.2 %collective-permute-start.28 = (bf16[64,2048]{1,0:T(8,128)(2,1)S(1)}, bf16[64,2048]{1,0:T(8,128)(2,1)S(1)}, u32[]{:S(2)}, u32[]{:S(2)}) collective-permute-start(bf16[64,2048]{1,0:T(8,128)(2,1)S(1)} %shard_map.69), channel_id=1, source_target_pairs={{0,16},{1,17},{2,18},{3,19},{4,20},{5,21},{6,22},{7,23},{8,9},{9,8... | collective-permute-start | bytes 786440 | tf_op jit(solution)/shard_map/ppermute | solution.py:223
  57.1 9.8 %collective-permute-start.31 = (bf16[64,2048]{1,0:T(8,128)(2,1)S(1)}, bf16[64,2048]{1,0:T(8,128)(2,1)S(1)}, u32[]{:S(2)}, u32[]{:S(2)}) collective-permute-start(bf16[64,2048]{1,0:T(8,128)(2,1)S(1)} %shard_map.71), channel_id=1, source_target_pairs={{0,16},{1,17},{2,18},{3,19},{4,20},{5,21},{6,22},{7,23},{8,9},{9,8... | collective-permute-start | bytes 786440 | tf_op jit(solution)/shard_map/ppermute | solution.py:223
  58.5 8.5 %collective-permute-start.30 = (bf16[64,2048]{1,0:T(8,128)(2,1)S(1)}, bf16[64,2048]{1,0:T(8,128)(2,1)S(1)}, u32[]{:S(2)}, u32[]{:S(2)}) collective-permute-start(bf16[64,2048]{1,0:T(8,128)(2,1)S(1)} %shard_map.65.rest_8_.second_ref.rest_4_), channel_id=1, source_target_pairs={{0,8},{8,0},{16,24},{24,16},{1,9},{9,1},{17,25},{25,17},{2,10},{10... | collective-permute-start | bytes 786440 | tf_op jit(solution)/shard_map/ppermute | solution.py:212
  66.0 1.7 %collective-permute-start.27 = (bf16[64,2048]{1,0:T(8,128)(2,1)S(1)}, bf16[64,2048]{1,0:T(8,128)(2,1)S(1)}, u32[]{:S(2)}, u32[]{:S(2)}) collective-permute-start(bf16[64,2048]{1,0:T(8,128)(2,1)S(1)} %shard_map.68.rest_0_), channel_id=1, source_target_pairs={{0,8},{8,0},{16,24},{24,16},{1,9},{9,1},{17,25},{25,17},{2,10},{10... | collective-permute-start | bytes 786440 | tf_op jit(solution)/shard_map/ppermute | solution.py:212
  66.6 1.5 %collective-permute-start.29 = (bf16[64,2048]{1,0:T(8,128)(2,1)S(1)}, bf16[64,2048]{1,0:T(8,128)(2,1)S(1)}, u32[]{:S(2)}, u32[]{:S(2)}) collective-permute-start(bf16[64,2048]{1,0:T(8,128)(2,1)S(1)} %shard_map.70.rest_2_), channel_id=1, source_target_pairs={{0,8},{8,0},{16,24},{24,16},{1,9},{9,1},{17,25},{25,17},{2,10},{10... | collective-permute-start | bytes 786440 | tf_op jit(solution)/shard_map/ppermute | solution.py:212
  66.9 1.6 %collective-permute-start.32 = (bf16[64,2048]{1,0:T(8,128)(2,1)S(1)}, bf16[64,2048]{1,0:T(8,128)(2,1)S(1)}, u32[]{:S(2)}, u32[]{:S(2)}) collective-permute-start(bf16[64,2048]{1,0:T(8,128)(2,1)S(1)} %shard_map.72.rest_6_), channel_id=1, source_target_pairs={{0,8},{8,0},{16,24},{24,16},{1,9},{9,1},{17,25},{25,17},{2,10},{10... | collective-permute-start | bytes 786440 | tf_op jit(solution)/shard_map/ppermute | solution.py:212

commit v6 on v5

--- a/solution.py
+++ b/solution.py
@@ -227,22 +227,22 @@
     kinds = {"O": [0], "A": early[0::2], "B": early[1::2], "C": late}
     reach = (len(early) + 1) // 2
     plan = {
+        ("O", 0, FIRST): ("own", 0, 1),
+        ("B", 1, SECOND): ("shift", 4, 4),
+        ("A", 0, FIRST): ("ring", 1, 1),
         ("C", 0, SECOND): ("plane", 3, 3),
+        ("B", 0, FIRST): ("ring", 2, 2),
+        ("B", 1, FIRST): ("shift", 3, 3),
         ("A", 1, SECOND): ("both", 4, 4),
-        ("A", 0, FIRST): ("ring", 1, 1),
-        ("O", 0, FIRST): ("own", 0, 1),
-        ("O", 1, SECOND): ("both", 2, 3),
-        ("B", 1, FIRST): ("shift", 3, 3),
-        ("B", 1, SECOND): ("both", 4, 4),
         ("B", 0, SECOND): ("plane", 3, 4),
         ("C", 0, FIRST): ("ring", 2, 2),
         ("C", 1, FIRST): ("pair", 3, 3),
         ("A", 0, SECOND): ("plane", 2, 2),
         ("A", 1, FIRST): ("pair", 2, 2),
-        ("B", 0, FIRST): ("ring", 2, 2),
+        ("C", 1, SECOND): ("both", 4, 4),
         ("O", 0, SECOND): ("own", 1, 1),
         ("O", 1, FIRST): ("pair", 1, 1),
-        ("C", 1, SECOND): ("both", 4, 4),
+        ("O", 1, SECOND): ("both", 2, 3),
     }
     listed = [((k, side, half), *plan[kind, side, half]) for kind, side, half in plan for k in kinds[kind]]
     stages = 1 + max(group for *_, group in listed)

time: 78.5 us -> 77.7 us (0.990)
  waiting for transfers between devices: 9.8 us -> 8.28 us
  starting transfers between devices: 27.4 us -> 28.4 us
    ppermute x4 -> x5, starting transfers between devices: 8.6 us -> 10.3 us  [shift_ring(): lax.ppermute(value, 'virt', [(v, (v - 2 * k) % virt_size) for v in range(...]
    ppermute x4 -> x3, starting transfers between devices: 4.14 us -> 2.76 us  [mix(): return lax.ppermute(value, ('occ', 'virt'), moves)]
    ppermute x4 -> x5, waiting for transfers between devices: 3.78 us -> 2.98 us  [shift_ring(): lax.ppermute(value, 'virt', [(v, (v - 2 * k) % virt_size) for v in range(...]
    pallas_call x28 -> x27, Pallas kernels: 34.8 us -> 34.6 us  [call(): pl.pallas_call(kernel, in_specs=in_specs, out_specs=[spec for spec, _ in...]
  transfers between devices with their start and end apart: 33 -> 33, of which waited for: 10 -> 7; matrix products, arithmetic and copies ran while one was open for 2% -> 2% of each run, Pallas kernels for 30% -> 30%
where the time goes in v6:
time: 77.7 us; the launch traced here: 77.4 us
  Pallas kernels  34.6 us (45%)
  starting transfers between devices  28.4 us (37%)
  waiting for transfers between devices  8.28 us (11%)
  local copies, waits for them, and re-layouts  5.72 us (7%)
    pallas_call x27, Pallas kernels, call(): pl.pallas_call(kernel, in_specs=in_specs, out_specs=[spec for spec, _ in...  34.6 us
    ppermute x22, starting transfers between devices, swap_occ(): return lax.ppermute(value, 'occ', [(o, o ^ bit) for o in range(occ_size)])  10.8 us
    ppermute x5, starting transfers between devices, shift_ring(): lax.ppermute(value, 'virt', [(v, (v - 2 * k) % virt_size) for v in range(...  10.3 us
    ppermute x3, starting transfers between devices, swap_pair(): return lax.ppermute(value, 'virt', [(v, v ^ 1) for v in range(virt_size)])  4.56 us
    unnamed x6, local copies, waits for them, and re-layouts  4.09 us
    ppermute x22, waiting for transfers between devices, swap_occ(): return lax.ppermute(value, 'occ', [(o, o ^ bit) for o in range(occ_size)])  3.09 us
    ppermute x5, waiting for transfers between devices, shift_ring(): lax.ppermute(value, 'virt', [(v, (v - 2 * k) % virt_size) for v in range(...  2.98 us
    ppermute x3, starting transfers between devices, mix(): return lax.ppermute(value, ('occ', 'virt'), moves)  2.76 us
  transfers between devices with their start and end apart: 33, of which 7 were waited for; matrix products, arithmetic and copies ran while one was open for 2% of the time, Pallas kernels for 30%

profile of v6, /device:TPU:0, one launch (start us, length us, event | category | flops | bytes accessed | tf_op | source)
XLA Modules:
  0.0 77.4 jit_solution(2012516112259381864)
XLA Ops:
  0.0 1.9 %shard_map.46 = (bf16[128,2048]{1,0:T(8,128)(2,1)S(1)}, bf16[128,2048]{1,0:T(8,128)(2,1)S(1)}, s32[16,128]{1,0:T(8,128)S(1)}) custom-call(s32[2]{0:T(128)} %partners_ref.3, bf16[12,128,2048]{2,1,0:T(8,128)(2,1)} %integrals_ref.1), custom_call_target="tpu_custom_call" | custom-call | tf_op jit(solution)/shard_map/pallas_call | solution.py:17
  1.9 0.5 collective-permute-start
  2.4 1.5 %collective-permute-done.got_ref = bf16[128,2048]{1,0:T(8,128)(2,1)S(1)} collective-permute-done((bf16[128,2048]{1,0:T(8,128)(2,1)S(1)}, bf16[128,2048]{1,0:T(8,128)(2,1)S(1)}, u32[]{:S(2)}, u32[]{:S(2)}) %collective-permute-start) | collective-permute-done | bytes 524320 | tf_op jit(solution)/shard_map/ppermute | solution.py:212
  4.0 0.1 shard_map.47
  4.1 2.9 %collective-permute-start.1 = (bf16[64,2048]{1,0:T(8,128)(2,1)S(1)}, bf16[64,2048]{1,0:T(8,128)(2,1)S(1)}, u32[]{:S(2)}, u32[]{:S(2)}) collective-permute-start(bf16[64,2048]{1,0:T(8,128)(2,1)S(1)} %get-tuple-element.34.own_ref), channel_id=1, source_target_pairs={{0,16},{8,24},{16,0},{24,8},{1,17},{9,25},{17,1},{25,9},{2,18},{10... | collective-permute-start | bytes 786440 | tf_op jit(solution)/shard_map/ppermute | solution.py:212
  7.0 0.8 reshape.9.virt_ref
  7.7 0.8 dynamic-slice_bitcast_fusion
  8.5 0.1 copy.22.column_ref
  8.6 0.1 pad_add_fusion.where_ref
  8.7 0.0 collective-permute-start.5
  8.7 2.8 %copy-done = bf16[12,128,2048]{2,1,0:T(8,128)(2,1)S(1)} copy-done((bf16[12,128,2048]{2,1,0:T(8,128)(2,1)S(1)}, bf16[12,128,2048]{2,1,0:T(8,128)(2,1)}, u32[]{:S(2)}) %copy-start) | copy-done | bytes 6291480
  11.5 0.7 copy-done.1
  12.2 0.7 copy-done.2
  12.8 1.1 %shard_map.48 = (bf16[1536,2048]{1,0:T(8,128)(2,1)S(1)}, f32[1536,1]{1,0:T(8,128)S(1)}, f32[8,128]{1,0:T(8,128)S(1)}, f32[1,512]{1,0:T(1,128)S(1)}, f32[1,512]{1...) custom-call(s32[2]{0:T(128)S(1)} %pad_add_fusion.where_ref, s32[2]{0:T(128)S(1)} %copy-done.1, ...), custom_call_target="tpu_custom_call" | custom-call | tf_op jit(solution)/shard_map/pallas_call | solution.py:17
  14.0 0.1 collective-permute-done.1.got_ref
  14.1 0.1 shard_map.49.rest_0_
  14.1 4.2 %collective-permute-start.3 = (bf16[64,2048]{1,0:T(8,128)(2,1)S(1)}, bf16[64,2048]{1,0:T(8,128)(2,1)S(1)}, u32[]{:S(2)}, u32[]{:S(2)}) collective-permute-start(bf16[64,2048]{1,0:T(8,128)(2,1)S(1)} %shard_map.49.rest_0_), channel_id=1, source_target_pairs={{0,6},{1,7},{2,0},{3,1},{4,2},{5,3},{6,4},{7,5},{8,14},{9,15},{10,... | collective-permute-start | bytes 786440 | tf_op jit(solution)/shard_map/ppermute | solution.py:218
  18.4 1.5 %collective-permute-start.7 = (bf16[64,2048]{1,0:T(8,128)(2,1)S(1)}, bf16[64,2048]{1,0:T(8,128)(2,1)S(1)}, u32[]{:S(2)}, u32[]{:S(2)}) collective-permute-start(bf16[64,2048]{1,0:T(8,128)(2,1)S(1)} %shard_map.49.rest_0_), channel_id=1, source_target_pairs={{0,1},{1,0},{2,3},{3,2},{4,5},{5,4},{6,7},{7,6},{8,9},{9,8},{10,11... | collective-permute-start | bytes 786440 | tf_op jit(solution)/shard_map/ppermute | solution.py:215
  19.9 0.0 collective-permute-start.2
  19.9 0.1 shard_map.51.refs_1_
  20.0 0.6 collective-permute-start.6
  20.5 3.0 %collective-permute-done.3.refs_1_ = bf16[64,2048]{1,0:T(8,128)(2,1)S(1)} collective-permute-done((bf16[64,2048]{1,0:T(8,128)(2,1)S(1)}, bf16[64,2048]{1,0:T(8,128)(2,1)S(1)}, u32[]{:S(2)}, u32[]{:S(2)}) %collective-permute-start.3) | collective-permute-done | bytes 262176 | tf_op jit(solution)/shard_map/ppermute | solution.py:218
  23.5 0.0 collective-permute-start.4
  23.5 2.2 %collective-permute-done.7.refs_1_ = bf16[64,2048]{1,0:T(8,128)(2,1)S(1)} collective-permute-done((bf16[64,2048]{1,0:T(8,128)(2,1)S(1)}, bf16[64,2048]{1,0:T(8,128)(2,1)S(1)}, u32[]{:S(2)}, u32[]{:S(2)}) %collective-permute-start.7) | collective-permute-done | bytes 262176 | tf_op jit(solution)/shard_map/ppermute | solution.py:215
  25.7 0.0 collective-permute-start.8
  25.7 0.0 collective-permute-start.9
  25.7 0.0 collective-permute-done.2.rest_1_
  25.7 3.8 %collective-permute-start.11 = (bf16[64,2048]{1,0:T(8,128)(2,1)S(1)}, bf16[64,2048]{1,0:T(8,128)(2,1)S(1)}, u32[]{:S(2)}, u32[]{:S(2)}) collective-permute-start(bf16[64,2048]{1,0:T(8,128)(2,1)S(1)} %shard_map.50.rest_2_), channel_id=1, source_target_pairs={{0,6},{1,7},{2,0},{3,1},{4,2},{5,3},{6,4},{7,5},{8,14},{9,15},{10,... | collective-permute-start | bytes 786440 | tf_op jit(solution)/shard_map/ppermute | solution.py:218
  29.5 1.5 %collective-permute-start.13 = (bf16[64,2048]{1,0:T(8,128)(2,1)S(1)}, bf16[64,2048]{1,0:T(8,128)(2,1)S(1)}, u32[]{:S(2)}, u32[]{:S(2)}) collective-permute-start(bf16[64,2048]{1,0:T(8,128)(2,1)S(1)} %shard_map.50.rest_2_), channel_id=1, source_target_pairs={{0,16},{8,24},{16,0},{24,8},{1,17},{9,25},{17,1},{25,9},{2,18},{10... | collective-permute-start | bytes 786440 | tf_op jit(solution)/shard_map/ppermute | solution.py:212
  31.0 1.5 %collective-permute-start.15 = (bf16[64,2048]{1,0:T(8,128)(2,1)S(1)}, bf16[64,2048]{1,0:T(8,128)(2,1)S(1)}, u32[]{:S(2)}, u32[]{:S(2)}) collective-permute-start(bf16[64,2048]{1,0:T(8,128)(2,1)S(1)} %shard_map.50.rest_2_), channel_id=1, source_target_pairs={{0,1},{1,0},{2,3},{3,2},{4,5},{5,4},{6,7},{7,6},{8,9},{9,8},{10,11... | collective-permute-start | bytes 786440 | tf_op jit(solution)/shard_map/ppermute | solution.py:215
  32.6 0.6 collective-permute-start.17
  33.2 7.1 %shard_map.54 = (f32[1536,2048]{1,0:T(8,128)S(1)}, f32[8,128]{1,0:T(8,128)S(1)}) custom-call(bf16[1536,2048]{1,0:T(8,128)(2,1)S(1)} %get-tuple-element.28.rows_ref, f32[1536,1]{1,0:T(8,128)S(1)} %get-tuple-element.29.row_energy_ref, f32[1,512]{1,0:T(1,128)S(1)} %get-tuple-element.33.block_energy_ref, bf16[64,2048]{1,0:T(8,128)(2,1)S(1)} %shard_map.49.rest_0_, ...), custom_call_target="tpu_custom_call" | custom-call | tf_op jit(solution)/shard_map/pallas_call | solution.py:17
  40.3 0.0 collective-permute-done.9.refs_1_
  40.3 0.1 collective-permute-start.10
  40.4 0.5 collective-permute-start.12
  40.9 0.0 collective-permute-done.13.refs_1_
  40.9 0.1 collective-permute-start.14
  41.0 0.4 collective-permute-start.16
  41.4 0.0 collective-permute-done.17.refs_1_
  41.4 1.5 %collective-permute-start.18 = (bf16[64,2048]{1,0:T(8,128)(2,1)S(1)}, bf16[64,2048]{1,0:T(8,128)(2,1)S(1)}, u32[]{:S(2)}, u32[]{:S(2)}) collective-permute-start(bf16[64,2048]{1,0:T(8,128)(2,1)S(1)} %shard_map.56.rest_2_), channel_id=1, source_target_pairs={{0,16},{8,24},{16,0},{24,8},{1,17},{9,25},{17,1},{25,9},{2,18},{10... | collective-permute-start | bytes 786440 | tf_op jit(solution)/shard_map/ppermute | solution.py:212
  42.9 0.5 collective-permute-start.20
  43.4 1.5 %collective-permute-start.22 = (bf16[64,2048]{1,0:T(8,128)(2,1)S(1)}, bf16[64,2048]{1,0:T(8,128)(2,1)S(1)}, u32[]{:S(2)}, u32[]{:S(2)}) collective-permute-start(bf16[64,2048]{1,0:T(8,128)(2,1)S(1)} %shard_map.56.rest_2_), channel_id=1, source_target_pairs={{0,1},{1,0},{2,3},{3,2},{4,5},{5,4},{6,7},{7,6},{8,9},{9,8},{10,11... | collective-permute-start | bytes 786440 | tf_op jit(solution)/shard_map/ppermute | solution.py:215
  44.9 0.5 collective-permute-start.25
  45.5 0.0 collective-permute-done.16.rest_7_
  45.5 7.4 %shard_map.61 = (f32[1536,2048]{1,0:T(8,128)S(1)}, f32[8,128]{1,0:T(8,128)S(1)}) custom-call(bf16[1536,2048]{1,0:T(8,128)(2,1)S(1)} %get-tuple-element.28.rows_ref, f32[1536,1]{1,0:T(8,128)S(1)} %get-tuple-element.29.row_energy_ref, f32[1,512]{1,0:T(1,128)S(1)} %get-tuple-element.32.block_energy_ref, ...), custom_call_target="tpu_custom_call", output_to_operand_aliasing={{0}: (12, {})} | custom-call | tf_op jit(solution)/shard_map/pallas_call | solution.py:17
  52.9 0.0 collective-permute-done.18.refs_1_
  52.9 0.6 collective-permute-start.19
  53.5 0.1 collective-permute-start.21
  53.6 0.4 collective-permute-start.23
  54.0 0.0 collective-permute-done.24.rest_7_
  54.0 1.7 %collective-permute-start.26 = (bf16[64,2048]{1,0:T(8,128)(2,1)S(1)}, bf16[64,2048]{1,0:T(8,128)(2,1)S(1)}, u32[]{:S(2)}, u32[]{:S(2)}) collective-permute-start(bf16[64,2048]{1,0:T(8,128)(2,1)S(1)} %shard_map.60.rest_8_.rest_6_), channel_id=1, source_target_pairs={{0,2},{1,3},{2,4},{3,5},{4,6},{5,7},{6,0},{7,1},{8,10},{9,11},{10,... | collective-permute-start | bytes 786440 | tf_op jit(solution)/shard_map/ppermute | solution.py:218
  55.8 1.6 %collective-permute-start.28 = (bf16[64,2048]{1,0:T(8,128)(2,1)S(1)}, bf16[64,2048]{1,0:T(8,128)(2,1)S(1)}, u32[]{:S(2)}, u32[]{:S(2)}) collective-permute-start(bf16[64,2048]{1,0:T(8,128)(2,1)S(1)} %shard_map.68), channel_id=1, source_target_pairs={{0,16},{1,17},{2,18},{3,19},{4,20},{5,21},{6,22},{7,23},{8,9},{9,8... | collective-permute-start | bytes 786440 | tf_op jit(solution)/shard_map/ppermute | solution.py:223
  57.4 0.0 collective-permute-done.19.rest_1_
  57.4 0.6 collective-permute-start.31
  58.0 0.0 collective-permute-done.21.rest_3_
  58.0 7.4 %shard_map.66 = (f32[1536,2048]{1,0:T(8,128)S(1)}, f32[8,128]{1,0:T(8,128)S(1)}) custom-call(bf16[1536,2048]{1,0:T(8,128)(2,1)S(1)} %get-tuple-element.28.rows_ref, f32[1536,1]{1,0:T(8,128)S(1)} %get-tuple-element.29.row_energy_ref, f32[1,512]{1,0:T(1,128)S(1)} %get-tuple-element.31.block_energy_ref, ...), custom_call_target="tpu_custom_call", output_to_operand_aliasing={{0}: (12, {})} | custom-call | tf_op jit(solution)/shard_map/pallas_call | solution.py:17
  65.4 0.0 collective-permute-done.26.refs_1_
  65.4 0.6 collective-permute-start.27
  66.0 0.1 collective-permute-start.29
  66.1 0.4 collective-permute-start.32
  66.5 0.6 collective-permute-done.27.rest_1_
  67.1 0.4 collective-permute-done.29.rest_3_
  67.5 0.4 collective-permute-done.32.rest_7_
  67.9 9.3 %shard_map.72 = (bf16[1536,2048]{1,0:T(8,128)(2,1)}, f32[8,128]{1,0:T(8,128)}) custom-call(bf16[1536,2048]{1,0:T(8,128)(2,1)S(1)} %get-tuple-element.28.rows_ref, f32[1536,1]{1,0:T(8,128)S(1)} %get-tuple-element.29.row_energy_ref, f32[1,512]{1,0:T(1,128)S(1)} %get-tuple-element.30.block_energy_ref, bf16[64,2048]{1,0:T(8,128)(2,1)S(1)} %shard_map.67.rest_0_, ...), custom_call_target="tpu_custom_call" | custom-call | tf_op jit(solution)/shard_map/pallas_call | solution.py:17
  (39 shorter events, 0.2 us)
Async XLA Ops:
  1.9 2.1 %collective-permute-start = (bf16[128,2048]{1,0:T(8,128)(2,1)S(1)}, bf16[128,2048]{1,0:T(8,128)(2,1)S(1)}, u32[]{:S(2)}, u32[]{:S(2)}) collective-permute-start(bf16[128,2048]{1,0:T(8,128)(2,1)S(1)} %get-tuple-element.26), channel_id=1, source_target_pairs={{0,8},{8,0},{16,24},{24,16},{1,9},{9,1},{17,25},{25,17},{2,10},{10... | collective-permute-start | bytes 1572872 | tf_op jit(solution)/shard_map/ppermute | solution.py:212
  4.1 10.0 %collective-permute-start.1 = (bf16[64,2048]{1,0:T(8,128)(2,1)S(1)}, bf16[64,2048]{1,0:T(8,128)(2,1)S(1)}, u32[]{:S(2)}, u32[]{:S(2)}) collective-permute-start(bf16[64,2048]{1,0:T(8,128)(2,1)S(1)} %get-tuple-element.34.own_ref), channel_id=1, source_target_pairs={{0,16},{8,24},{16,0},{24,8},{1,17},{9,25},{17,1},{25,9},{2,18},{10... | collective-permute-start | bytes 786440 | tf_op jit(solution)/shard_map/ppermute | solution.py:212
  8.7 11.2 %collective-permute-start.5 = (bf16[64,2048]{1,0:T(8,128)(2,1)S(1)}, bf16[64,2048]{1,0:T(8,128)(2,1)S(1)}, u32[]{:S(2)}, u32[]{:S(2)}) collective-permute-start(bf16[64,2048]{1,0:T(8,128)(2,1)S(1)} %get-tuple-element.27.rest_0_.own_ref), channel_id=1, source_target_pairs={{0,16},{8,24},{16,0},{24,8},{1,17},{9,25},{17,1},{25,9},{2,18},{10... | collective-permute-start | bytes 786440 | tf_op jit(solution)/shard_map/ppermute | solution.py:212
  8.7 2.8 %copy-start = (bf16[12,128,2048]{2,1,0:T(8,128)(2,1)S(1)}, bf16[12,128,2048]{2,1,0:T(8,128)(2,1)}, u32[]{:S(2)}) copy-start(bf16[12,128,2048]{2,1,0:T(8,128)(2,1)} %integrals_ref.1) | copy-start | bytes 18874372
  11.5 0.7 copy-start.1
  12.2 0.7 copy-start.2
  14.1 9.4 %collective-permute-start.3 = (bf16[64,2048]{1,0:T(8,128)(2,1)S(1)}, bf16[64,2048]{1,0:T(8,128)(2,1)S(1)}, u32[]{:S(2)}, u32[]{:S(2)}) collective-permute-start(bf16[64,2048]{1,0:T(8,128)(2,1)S(1)} %shard_map.49.rest_0_), channel_id=1, source_target_pairs={{0,6},{1,7},{2,0},{3,1},{4,2},{5,3},{6,4},{7,5},{8,14},{9,15},{10,... | collective-permute-start | bytes 786440 | tf_op jit(solution)/shard_map/ppermute | solution.py:218
  18.4 7.4 %collective-permute-start.7 = (bf16[64,2048]{1,0:T(8,128)(2,1)S(1)}, bf16[64,2048]{1,0:T(8,128)(2,1)S(1)}, u32[]{:S(2)}, u32[]{:S(2)}) collective-permute-start(bf16[64,2048]{1,0:T(8,128)(2,1)S(1)} %shard_map.49.rest_0_), channel_id=1, source_target_pairs={{0,1},{1,0},{2,3},{3,2},{4,5},{5,4},{6,7},{7,6},{8,9},{9,8},{10,11... | collective-permute-start | bytes 786440 | tf_op jit(solution)/shard_map/ppermute | solution.py:215
  19.9 5.8 %collective-permute-start.2 = (bf16[64,2048]{1,0:T(8,128)(2,1)S(1)}, bf16[64,2048]{1,0:T(8,128)(2,1)S(1)}, u32[]{:S(2)}, u32[]{:S(2)}) collective-permute-start(bf16[64,2048]{1,0:T(8,128)(2,1)S(1)} %shard_map.49.rest_0_), channel_id=1, source_target_pairs={{0,8},{8,0},{16,24},{24,16},{1,9},{9,1},{17,25},{25,17},{2,10},{10... | collective-permute-start | bytes 786440 | tf_op jit(solution)/shard_map/ppermute | solution.py:212
  20.0 9.6 %collective-permute-start.6 = (bf16[64,2048]{1,0:T(8,128)(2,1)S(1)}, bf16[64,2048]{1,0:T(8,128)(2,1)S(1)}, u32[]{:S(2)}, u32[]{:S(2)}) collective-permute-start(bf16[64,2048]{1,0:T(8,128)(2,1)S(1)} %shard_map.52.rest_4_.second_ref), channel_id=1, source_target_pairs={{0,8},{8,0},{16,24},{24,16},{1,9},{9,1},{17,25},{25,17},{2,10},{10... | collective-permute-start | bytes 786440 | tf_op jit(solution)/shard_map/ppermute | solution.py:212
  23.5 7.5 %collective-permute-start.4 = (bf16[64,2048]{1,0:T(8,128)(2,1)S(1)}, bf16[64,2048]{1,0:T(8,128)(2,1)S(1)}, u32[]{:S(2)}, u32[]{:S(2)}) collective-permute-start(bf16[64,2048]{1,0:T(8,128)(2,1)S(1)} %shard_map.50.rest_2_), channel_id=1, source_target_pairs={{0,8},{8,0},{16,24},{24,16},{1,9},{9,1},{17,25},{25,17},{2,10},{10... | collective-permute-start | bytes 786440 | tf_op jit(solution)/shard_map/ppermute | solution.py:212
  25.7 6.9 %collective-permute-start.8 = (bf16[64,2048]{1,0:T(8,128)(2,1)S(1)}, bf16[64,2048]{1,0:T(8,128)(2,1)S(1)}, u32[]{:S(2)}, u32[]{:S(2)}) collective-permute-start(bf16[64,2048]{1,0:T(8,128)(2,1)S(1)} %shard_map.53.rest_6_.first_ref), channel_id=1, source_target_pairs={{0,8},{8,0},{16,24},{24,16},{1,9},{9,1},{17,25},{25,17},{2,10},{10... | collective-permute-start | bytes 786440 | tf_op jit(solution)/shard_map/ppermute | solution.py:212
  25.7 14.6 %collective-permute-start.9 = (bf16[64,2048]{1,0:T(8,128)(2,1)S(1)}, bf16[64,2048]{1,0:T(8,128)(2,1)S(1)}, u32[]{:S(2)}, u32[]{:S(2)}) collective-permute-start(bf16[64,2048]{1,0:T(8,128)(2,1)S(1)} %shard_map.49.rest_0_), channel_id=1, source_target_pairs={{0,2},{1,3},{2,4},{3,5},{4,6},{5,7},{6,0},{7,1},{8,10},{9,11},{10,... | collective-permute-start | bytes 786440 | tf_op jit(solution)/shard_map/ppermute | solution.py:218
  25.7 14.7 %collective-permute-start.11 = (bf16[64,2048]{1,0:T(8,128)(2,1)S(1)}, bf16[64,2048]{1,0:T(8,128)(2,1)S(1)}, u32[]{:S(2)}, u32[]{:S(2)}) collective-permute-start(bf16[64,2048]{1,0:T(8,128)(2,1)S(1)} %shard_map.50.rest_2_), channel_id=1, source_target_pairs={{0,6},{1,7},{2,0},{3,1},{4,2},{5,3},{6,4},{7,5},{8,14},{9,15},{10,... | collective-permute-start | bytes 786440 | tf_op jit(solution)/shard_map/ppermute | solution.py:218
  29.5 11.3 %collective-permute-start.13 = (bf16[64,2048]{1,0:T(8,128)(2,1)S(1)}, bf16[64,2048]{1,0:T(8,128)(2,1)S(1)}, u32[]{:S(2)}, u32[]{:S(2)}) collective-permute-start(bf16[64,2048]{1,0:T(8,128)(2,1)S(1)} %shard_map.50.rest_2_), channel_id=1, source_target_pairs={{0,16},{8,24},{16,0},{24,8},{1,17},{9,25},{17,1},{25,9},{2,18},{10... | collective-permute-start | bytes 786440 | tf_op jit(solution)/shard_map/ppermute | solution.py:212
  31.0 9.9 %collective-permute-start.15 = (bf16[64,2048]{1,0:T(8,128)(2,1)S(1)}, bf16[64,2048]{1,0:T(8,128)(2,1)S(1)}, u32[]{:S(2)}, u32[]{:S(2)}) collective-permute-start(bf16[64,2048]{1,0:T(8,128)(2,1)S(1)} %shard_map.50.rest_2_), channel_id=1, source_target_pairs={{0,1},{1,0},{2,3},{3,2},{4,5},{5,4},{6,7},{7,6},{8,9},{9,8},{10,11... | collective-permute-start | bytes 786440 | tf_op jit(solution)/shard_map/ppermute | solution.py:215
  32.6 8.8 %collective-permute-start.17 = (bf16[64,2048]{1,0:T(8,128)(2,1)S(1)}, bf16[64,2048]{1,0:T(8,128)(2,1)S(1)}, u32[]{:S(2)}, u32[]{:S(2)}) collective-permute-start(bf16[64,2048]{1,0:T(8,128)(2,1)S(1)} %shard_map.59), channel_id=1, source_target_pairs={{0,16},{1,17},{2,18},{3,19},{4,20},{5,21},{6,22},{7,23},{8,9},{9,8... | collective-permute-start | bytes 786440 | tf_op jit(solution)/shard_map/ppermute | solution.py:223
  40.3 2.6 %collective-permute-start.10 = (bf16[64,2048]{1,0:T(8,128)(2,1)S(1)}, bf16[64,2048]{1,0:T(8,128)(2,1)S(1)}, u32[]{:S(2)}, u32[]{:S(2)}) collective-permute-start(bf16[64,2048]{1,0:T(8,128)(2,1)S(1)} %shard_map.55.rest_0_), channel_id=1, source_target_pairs={{0,8},{8,0},{16,24},{24,16},{1,9},{9,1},{17,25},{25,17},{2,10},{10... | collective-permute-start | bytes 786440 | tf_op jit(solution)/shard_map/ppermute | solution.py:212
  40.4 3.0 %collective-permute-start.12 = (bf16[64,2048]{1,0:T(8,128)(2,1)S(1)}, bf16[64,2048]{1,0:T(8,128)(2,1)S(1)}, u32[]{:S(2)}, u32[]{:S(2)}) collective-permute-start(bf16[64,2048]{1,0:T(8,128)(2,1)S(1)} %shard_map.56.rest_2_), channel_id=1, source_target_pairs={{0,8},{8,0},{16,24},{24,16},{1,9},{9,1},{17,25},{25,17},{2,10},{10... | collective-permute-start | bytes 786440 | tf_op jit(solution)/shard_map/ppermute | solution.py:212
  40.9 4.0 %collective-permute-start.14 = (bf16[64,2048]{1,0:T(8,128)(2,1)S(1)}, bf16[64,2048]{1,0:T(8,128)(2,1)S(1)}, u32[]{:S(2)}, u32[]{:S(2)}) collective-permute-start(bf16[64,2048]{1,0:T(8,128)(2,1)S(1)} %shard_map.57.rest_4_.second_ref), channel_id=1, source_target_pairs={{0,8},{8,0},{16,24},{24,16},{1,9},{9,1},{17,25},{25,17},{2,10},{10... | collective-permute-start | bytes 786440 | tf_op jit(solution)/shard_map/ppermute | solution.py:212
  41.0 4.5 %collective-permute-start.16 = (bf16[64,2048]{1,0:T(8,128)(2,1)S(1)}, bf16[64,2048]{1,0:T(8,128)(2,1)S(1)}, u32[]{:S(2)}, u32[]{:S(2)}) collective-permute-start(bf16[64,2048]{1,0:T(8,128)(2,1)S(1)} %shard_map.58.rest_6_.first_ref), channel_id=1, source_target_pairs={{0,8},{8,0},{16,24},{24,16},{1,9},{9,1},{17,25},{25,17},{2,10},{10... | collective-permute-start | bytes 786440 | tf_op jit(solution)/shard_map/ppermute | solution.py:212
  41.4 11.5 %collective-permute-start.18 = (bf16[64,2048]{1,0:T(8,128)(2,1)S(1)}, bf16[64,2048]{1,0:T(8,128)(2,1)S(1)}, u32[]{:S(2)}, u32[]{:S(2)}) collective-permute-start(bf16[64,2048]{1,0:T(8,128)(2,1)S(1)} %shard_map.56.rest_2_), channel_id=1, source_target_pairs={{0,16},{8,24},{16,0},{24,8},{1,17},{9,25},{17,1},{25,9},{2,18},{10... | collective-permute-start | bytes 786440 | tf_op jit(solution)/shard_map/ppermute | solution.py:212
  42.9 10.6 %collective-permute-start.20 = (bf16[64,2048]{1,0:T(8,128)(2,1)S(1)}, bf16[64,2048]{1,0:T(8,128)(2,1)S(1)}, u32[]{:S(2)}, u32[]{:S(2)}) collective-permute-start(bf16[64,2048]{1,0:T(8,128)(2,1)S(1)} %shard_map.53.rest_6_.first_ref), channel_id=1, source_target_pairs={{0,2},{1,3},{2,4},{3,5},{4,6},{5,7},{6,0},{7,1},{8,10},{9,11},{10,... | collective-permute-start | bytes 786440 | tf_op jit(solution)/shard_map/ppermute | solution.py:218
  43.4 10.2 %collective-permute-start.22 = (bf16[64,2048]{1,0:T(8,128)(2,1)S(1)}, bf16[64,2048]{1,0:T(8,128)(2,1)S(1)}, u32[]{:S(2)}, u32[]{:S(2)}) collective-permute-start(bf16[64,2048]{1,0:T(8,128)(2,1)S(1)} %shard_map.56.rest_2_), channel_id=1, source_target_pairs={{0,1},{1,0},{2,3},{3,2},{4,5},{5,4},{6,7},{7,6},{8,9},{9,8},{10,11... | collective-permute-start | bytes 786440 | tf_op jit(solution)/shard_map/ppermute | solution.py:215
  44.9 10.8 %collective-permute-start.25 = (bf16[64,2048]{1,0:T(8,128)(2,1)S(1)}, bf16[64,2048]{1,0:T(8,128)(2,1)S(1)}, u32[]{:S(2)}, u32[]{:S(2)}) collective-permute-start(bf16[64,2048]{1,0:T(8,128)(2,1)S(1)} %shard_map.55.rest_0_), channel_id=1, source_target_pairs={{0,16},{8,24},{16,0},{24,8},{1,17},{9,25},{17,1},{25,9},{2,18},{10... | collective-permute-start | bytes 786440 | tf_op jit(solution)/shard_map/ppermute | solution.py:212
  45.5 8.5 %collective-permute-start.24 = (bf16[64,2048]{1,0:T(8,128)(2,1)S(1)}, bf16[64,2048]{1,0:T(8,128)(2,1)S(1)}, u32[]{:S(2)}, u32[]{:S(2)}) collective-permute-start(bf16[64,2048]{1,0:T(8,128)(2,1)S(1)} %shard_map.60.rest_8_.rest_6_), channel_id=1, source_target_pairs={{0,8},{8,0},{16,24},{24,16},{1,9},{9,1},{17,25},{25,17},{2,10},{10... | collective-permute-start | bytes 786440 | tf_op jit(solution)/shard_map/ppermute | solution.py:212
  52.9 4.4 %collective-permute-start.19 = (bf16[64,2048]{1,0:T(8,128)(2,1)S(1)}, bf16[64,2048]{1,0:T(8,128)(2,1)S(1)}, u32[]{:S(2)}, u32[]{:S(2)}) collective-permute-start(bf16[64,2048]{1,0:T(8,128)(2,1)S(1)} %shard_map.62.rest_0_.second_ref), channel_id=1, source_target_pairs={{0,8},{8,0},{16,24},{24,16},{1,9},{9,1},{17,25},{25,17},{2,10},{10... | collective-permute-start | bytes 786440 | tf_op jit(solution)/shard_map/ppermute | solution.py:212
  53.5 4.5 %collective-permute-start.21 = (bf16[64,2048]{1,0:T(8,128)(2,1)S(1)}, bf16[64,2048]{1,0:T(8,128)(2,1)S(1)}, u32[]{:S(2)}, u32[]{:S(2)}) collective-permute-start(bf16[64,2048]{1,0:T(8,128)(2,1)S(1)} %shard_map.63.rest_2_), channel_id=1, source_target_pairs={{0,8},{8,0},{16,24},{24,16},{1,9},{9,1},{17,25},{25,17},{2,10},{10... | collective-permute-start | bytes 786440 | tf_op jit(solution)/shard_map/ppermute | solution.py:212
  53.6 4.4 %collective-permute-start.23 = (bf16[64,2048]{1,0:T(8,128)(2,1)S(1)}, bf16[64,2048]{1,0:T(8,128)(2,1)S(1)}, u32[]{:S(2)}, u32[]{:S(2)}) collective-permute-start(bf16[64,2048]{1,0:T(8,128)(2,1)S(1)} %shard_map.64.rest_4_.first_ref), channel_id=1, source_target_pairs={{0,8},{8,0},{16,24},{24,16},{1,9},{9,1},{17,25},{25,17},{2,10},{10... | collective-permute-start | bytes 786440 | tf_op jit(solution)/shard_map/ppermute | solution.py:212
  54.0 11.4 %collective-permute-start.26 = (bf16[64,2048]{1,0:T(8,128)(2,1)S(1)}, bf16[64,2048]{1,0:T(8,128)(2,1)S(1)}, u32[]{:S(2)}, u32[]{:S(2)}) collective-permute-start(bf16[64,2048]{1,0:T(8,128)(2,1)S(1)} %shard_map.60.rest_8_.rest_6_), channel_id=1, source_target_pairs={{0,2},{1,3},{2,4},{3,5},{4,6},{5,7},{6,0},{7,1},{8,10},{9,11},{10,... | collective-permute-start | bytes 786440 | tf_op jit(solution)/shard_map/ppermute | solution.py:218
  55.8 10.2 %collective-permute-start.28 = (bf16[64,2048]{1,0:T(8,128)(2,1)S(1)}, bf16[64,2048]{1,0:T(8,128)(2,1)S(1)}, u32[]{:S(2)}, u32[]{:S(2)}) collective-permute-start(bf16[64,2048]{1,0:T(8,128)(2,1)S(1)} %shard_map.68), channel_id=1, source_target_pairs={{0,16},{1,17},{2,18},{3,19},{4,20},{5,21},{6,22},{7,23},{8,9},{9,8... | collective-permute-start | bytes 786440 | tf_op jit(solution)/shard_map/ppermute | solution.py:223
  57.4 8.7 %collective-permute-start.31 = (bf16[64,2048]{1,0:T(8,128)(2,1)S(1)}, bf16[64,2048]{1,0:T(8,128)(2,1)S(1)}, u32[]{:S(2)}, u32[]{:S(2)}) collective-permute-start(bf16[64,2048]{1,0:T(8,128)(2,1)S(1)} %shard_map.70), channel_id=1, source_target_pairs={{0,16},{1,17},{2,18},{3,19},{4,20},{5,21},{6,22},{7,23},{8,9},{9,8... | collective-permute-start | bytes 786440 | tf_op jit(solution)/shard_map/ppermute | solution.py:223
  58.0 8.5 %collective-permute-start.30 = (bf16[64,2048]{1,0:T(8,128)(2,1)S(1)}, bf16[64,2048]{1,0:T(8,128)(2,1)S(1)}, u32[]{:S(2)}, u32[]{:S(2)}) collective-permute-start(bf16[64,2048]{1,0:T(8,128)(2,1)S(1)} %shard_map.65.rest_8_.rest_4_), channel_id=1, source_target_pairs={{0,8},{8,0},{16,24},{24,16},{1,9},{9,1},{17,25},{25,17},{2,10},{10... | collective-permute-start | bytes 786440 | tf_op jit(solution)/shard_map/ppermute | solution.py:212
  65.4 1.7 %collective-permute-start.27 = (bf16[64,2048]{1,0:T(8,128)(2,1)S(1)}, bf16[64,2048]{1,0:T(8,128)(2,1)S(1)}, u32[]{:S(2)}, u32[]{:S(2)}) collective-permute-start(bf16[64,2048]{1,0:T(8,128)(2,1)S(1)} %shard_map.67.rest_0_), channel_id=1, source_target_pairs={{0,8},{8,0},{16,24},{24,16},{1,9},{9,1},{17,25},{25,17},{2,10},{10... | collective-permute-start | bytes 786440 | tf_op jit(solution)/shard_map/ppermute | solution.py:212
  66.0 1.5 %collective-permute-start.29 = (bf16[64,2048]{1,0:T(8,128)(2,1)S(1)}, bf16[64,2048]{1,0:T(8,128)(2,1)S(1)}, u32[]{:S(2)}, u32[]{:S(2)}) collective-permute-start(bf16[64,2048]{1,0:T(8,128)(2,1)S(1)} %shard_map.69.rest_2_), channel_id=1, source_target_pairs={{0,8},{8,0},{16,24},{24,16},{1,9},{9,1},{17,25},{25,17},{2,10},{10... | collective-permute-start | bytes 786440 | tf_op jit(solution)/shard_map/ppermute | solution.py:212
  66.1 1.8 %collective-permute-start.32 = (bf16[64,2048]{1,0:T(8,128)(2,1)S(1)}, bf16[64,2048]{1,0:T(8,128)(2,1)S(1)}, u32[]{:S(2)}, u32[]{:S(2)}) collective-permute-start(bf16[64,2048]{1,0:T(8,128)(2,1)S(1)} %shard_map.71.rest_6_), channel_id=1, source_target_pairs={{0,8},{8,0},{16,24},{24,16},{1,9},{9,1},{17,25},{25,17},{2,10},{10... | collective-permute-start | bytes 786440 | tf_op jit(solution)/shard_map/ppermute | solution.py:212

commit v7 on v6

--- a/solution.py
+++ b/solution.py
@@ -91,13 +91,14 @@
     return call(kernel, [first, second], [VMEM, VMEM], outs)[0]
 
 
-def prepare(where, partners, occ_energy, column, virt_halves, rows, groups, ready):
+def prepare(where, partners, occ_energy, virt_halves, rows, groups, ready):
     height = rows.shape[0]
-    local_virt, half = column.shape[0], virt_halves.shape[1]
+    half = virt_halves.shape[1]
+    local_virt = 2 * half
     occ_dev, virt_size = height // local_virt, virt_halves.shape[0] // 2
     widths = [padded(half * len(places)) for places in groups]
 
-    def kernel(where_ref, partners_ref, occ_energy_ref, column_ref, virt_ref, rows_ref, *rest):
+    def kernel(where_ref, partners_ref, occ_energy_ref, virt_ref, rows_ref, *rest):
         rest = rest[1:]
         out_ref, row_energy_ref, token_ref = rest[:3]
         energy_refs, sem = rest[3:-1], rest[-1]
@@ -106,9 +107,13 @@
         virt_index, occ_index = where_ref[0], where_ref[1]
         plane = lax.rem(lax.div(occ_index, 2), 2)
         token_ref[...] = jnp.zeros_like(token_ref)
-        for i in range(occ_dev):
-            own = occ_energy_ref[occ_index * occ_dev + i]
-            row_energy_ref[pl.ds(i * local_virt, local_virt), :] = column_ref[...] - own
+        square = [lax.broadcasted_iota(jnp.int32, (half, half), axis) for axis in (0, 1)]
+        for part in range(2):
+            line = virt_ref[pl.ds(2 * virt_index + part, 1), :]
+            column = jnp.sum(jnp.where(square[0] == square[1], line, 0.0), axis=1, keepdims=True)
+            for i in range(occ_dev):
+                own = occ_energy_ref[occ_index * occ_dev + i]
+                row_energy_ref[pl.ds(i * local_virt + part * half, half), :] = column - own
         for places, energy_ref in zip(groups, energy_refs):
             energy_ref[...] = jnp.ones_like(energy_ref)
             for k, (ring_step, side, which, step) in enumerate(places):
@@ -123,8 +128,8 @@
     outs += [(VMEM, pltpu.VMEM((1, width), jnp.float32)) for width in widths]
     rows, row_energy, token, *energies = call(
         kernel,
-        [where, partners, occ_energy, column, virt_halves, rows, ready],
-        [SMEM] * 3 + [VMEM] * 2 + [ANY] * 2,
+        [where, partners, occ_energy, virt_halves, rows, ready],
+        [SMEM] * 3 + [VMEM] + [ANY] * 2,
         outs,
         [pltpu.SemaphoreType.DMA],
         vmem=16,
@@ -250,13 +255,12 @@
     places = [[(*name, step) for name in group for step in range(2)] for group in groups]
 
     where = jnp.stack([virt_index, occ_index]).astype(jnp.int32)
-    column = lax.dynamic_slice_in_dim(virt_energy, virt_index * local_virt, local_virt)[:, None]
     virt_halves = virt_energy.reshape(2 * virt_size, half)
     bits = [1 << n for n in range(occ_size.bit_length() - 1)]
     own, sent, held = extract(bits, partners, integrals)
     first, second = choose(held, 0, own, swap_occ(sent, 1))
     rows, row_energy, token, energies = prepare(
-        where, partners, occ_energy, column, virt_halves, integrals.reshape(-1, aux_width), [group for group in places if group], first
+        where, partners, occ_energy, virt_halves, integrals.reshape(-1, aux_width), [group for group in places if group], first
     )
     sent = [second, first]
     for n, bit in list(enumerate(bits))[1:]:

time: 77.7 us -> 76.8 us (0.988)
  local copies, waits for them, and re-layouts: 5.72 us -> 4.85 us
    broadcast_in_dim x2 -> x0, local copies, waits for them, and re-layouts: 0.87 us -> none  [per_device(): lax.dynamic_slice_in_dim(virt_energy, virt_index * local_virt, local_virt)]
    ppermute x22, waiting for transfers between devices: 3.09 us -> 3.95 us  [swap_occ(): return lax.ppermute(value, 'occ', [(o, o ^ bit) for o in range(occ_size)])]
    ppermute x5, waiting for transfers between devices: 2.98 us -> 2.12 us  [shift_ring(): lax.ppermute(value, 'virt', [(v, (v - 2 * k) % virt_size) for v in range(...]
  transfers between devices with their start and end apart: 33 -> 33, of which waited for: 7 -> 7; matrix products, arithmetic and copies ran while one was open for 2% -> 1% of each run, Pallas kernels for 30% -> 30%
where the time goes in v7:
time: 76.8 us; the launch traced here: 76.5 us
  Pallas kernels  34.6 us (45%)
  starting transfers between devices  28.4 us (37%)
  waiting for transfers between devices  8.28 us (11%)
  local copies, waits for them, and re-layouts  4.85 us (6%)
    pallas_call x27, Pallas kernels, call(): pl.pallas_call(kernel, in_specs=in_specs, out_specs=[spec for spec, _ in...  34.6 us
    ppermute x22, starting transfers between devices, swap_occ(): return lax.ppermute(value, 'occ', [(o, o ^ bit) for o in range(occ_size)])  10.8 us
    ppermute x5, starting transfers between devices, shift_ring(): lax.ppermute(value, 'virt', [(v, (v - 2 * k) % virt_size) for v in range(...  10.3 us
    ppermute x3, starting transfers between devices, swap_pair(): return lax.ppermute(value, 'virt', [(v, v ^ 1) for v in range(virt_size)])  4.56 us
    unnamed x6, local copies, waits for them, and re-layouts  4.09 us
    ppermute x22, waiting for transfers between devices, swap_occ(): return lax.ppermute(value, 'occ', [(o, o ^ bit) for o in range(occ_size)])  3.95 us
    ppermute x3, starting transfers between devices, mix(): return lax.ppermute(value, ('occ', 'virt'), moves)  2.76 us
    ppermute x3, waiting for transfers between devices, swap_pair(): return lax.ppermute(value, 'virt', [(v, v ^ 1) for v in range(virt_size)])  2.2 us
  transfers between devices with their start and end apart: 33, of which 7 were waited for; matrix products, arithmetic and copies ran while one was open for 1% of the time, Pallas kernels for 30%

profile of v7, /device:TPU:0, one launch (start us, length us, event | category | flops | bytes accessed | tf_op | source)
XLA Modules:
  0.0 76.5 jit_solution(6156842076334749934)
XLA Ops:
  0.0 1.9 %shard_map.46 = (bf16[128,2048]{1,0:T(8,128)(2,1)S(1)}, bf16[128,2048]{1,0:T(8,128)(2,1)S(1)}, s32[16,128]{1,0:T(8,128)S(1)}) custom-call(s32[2]{0:T(128)} %partners_ref.3, bf16[12,128,2048]{2,1,0:T(8,128)(2,1)} %integrals_ref.1), custom_call_target="tpu_custom_call" | custom-call | tf_op jit(solution)/shard_map/pallas_call | solution.py:17
  1.9 0.5 collective-permute-start
  2.4 1.5 %collective-permute-done.got_ref = bf16[128,2048]{1,0:T(8,128)(2,1)S(1)} collective-permute-done((bf16[128,2048]{1,0:T(8,128)(2,1)S(1)}, bf16[128,2048]{1,0:T(8,128)(2,1)S(1)}, u32[]{:S(2)}, u32[]{:S(2)}) %collective-permute-start) | collective-permute-done | bytes 524320 | tf_op jit(solution)/shard_map/ppermute | solution.py:217
  4.0 0.1 shard_map.47
  4.1 2.9 %collective-permute-start.1 = (bf16[64,2048]{1,0:T(8,128)(2,1)S(1)}, bf16[64,2048]{1,0:T(8,128)(2,1)S(1)}, u32[]{:S(2)}, u32[]{:S(2)}) collective-permute-start(bf16[64,2048]{1,0:T(8,128)(2,1)S(1)} %get-tuple-element.34.own_ref), channel_id=1, source_target_pairs={{0,16},{8,24},{16,0},{24,8},{1,17},{9,25},{17,1},{25,9},{2,18},{10... | collective-permute-start | bytes 786440 | tf_op jit(solution)/shard_map/ppermute | solution.py:217
  7.0 0.8 reshape.9.virt_ref
  7.7 0.1 pad_add_fusion.where_ref
  7.8 0.0 collective-permute-start.5
  7.8 2.8 %copy-done = bf16[12,128,2048]{2,1,0:T(8,128)(2,1)S(1)} copy-done((bf16[12,128,2048]{2,1,0:T(8,128)(2,1)S(1)}, bf16[12,128,2048]{2,1,0:T(8,128)(2,1)}, u32[]{:S(2)}) %copy-start) | copy-done | bytes 6291480
  10.6 0.7 copy-done.1
  11.3 0.7 copy-done.2
  11.9 1.2 %shard_map.48 = (bf16[1536,2048]{1,0:T(8,128)(2,1)S(1)}, f32[1536,1]{1,0:T(8,128)S(1)}, f32[8,128]{1,0:T(8,128)S(1)}, f32[1,512]{1,0:T(1,128)S(1)}, f32[1,512]{1...) custom-call(s32[2]{0:T(128)S(1)} %pad_add_fusion.where_ref, s32[2]{0:T(128)S(1)} %copy-done.1, ...), custom_call_target="tpu_custom_call" | custom-call | tf_op jit(solution)/shard_map/pallas_call | solution.py:17
  13.1 1.0 %collective-permute-done.1.got_ref = bf16[64,2048]{1,0:T(8,128)(2,1)S(1)} collective-permute-done((bf16[64,2048]{1,0:T(8,128)(2,1)S(1)}, bf16[64,2048]{1,0:T(8,128)(2,1)S(1)}, u32[]{:S(2)}, u32[]{:S(2)}) %collective-permute-start.1) | collective-permute-done | bytes 262176 | tf_op jit(solution)/shard_map/ppermute | solution.py:217
  14.1 0.1 shard_map.49.rest_0_
  14.1 4.2 %collective-permute-start.3 = (bf16[64,2048]{1,0:T(8,128)(2,1)S(1)}, bf16[64,2048]{1,0:T(8,128)(2,1)S(1)}, u32[]{:S(2)}, u32[]{:S(2)}) collective-permute-start(bf16[64,2048]{1,0:T(8,128)(2,1)S(1)} %shard_map.49.rest_0_), channel_id=1, source_target_pairs={{0,6},{1,7},{2,0},{3,1},{4,2},{5,3},{6,4},{7,5},{8,14},{9,15},{10,... | collective-permute-start | bytes 786440 | tf_op jit(solution)/shard_map/ppermute | solution.py:223
  18.4 1.5 %collective-permute-start.7 = (bf16[64,2048]{1,0:T(8,128)(2,1)S(1)}, bf16[64,2048]{1,0:T(8,128)(2,1)S(1)}, u32[]{:S(2)}, u32[]{:S(2)}) collective-permute-start(bf16[64,2048]{1,0:T(8,128)(2,1)S(1)} %shard_map.49.rest_0_), channel_id=1, source_target_pairs={{0,1},{1,0},{2,3},{3,2},{4,5},{5,4},{6,7},{7,6},{8,9},{9,8},{10,11... | collective-permute-start | bytes 786440 | tf_op jit(solution)/shard_map/ppermute | solution.py:220
  19.9 0.1 shard_map.51.refs_1_
  20.0 0.6 collective-permute-start.6
  20.5 2.1 %collective-permute-done.3.refs_1_ = bf16[64,2048]{1,0:T(8,128)(2,1)S(1)} collective-permute-done((bf16[64,2048]{1,0:T(8,128)(2,1)S(1)}, bf16[64,2048]{1,0:T(8,128)(2,1)S(1)}, u32[]{:S(2)}, u32[]{:S(2)}) %collective-permute-start.3) | collective-permute-done | bytes 262176 | tf_op jit(solution)/shard_map/ppermute | solution.py:223
  22.6 0.0 collective-permute-start.4
  22.6 2.2 %collective-permute-done.7.refs_1_ = bf16[64,2048]{1,0:T(8,128)(2,1)S(1)} collective-permute-done((bf16[64,2048]{1,0:T(8,128)(2,1)S(1)}, bf16[64,2048]{1,0:T(8,128)(2,1)S(1)}, u32[]{:S(2)}, u32[]{:S(2)}) %collective-permute-start.7) | collective-permute-done | bytes 262176 | tf_op jit(solution)/shard_map/ppermute | solution.py:220
  24.8 0.0 collective-permute-start.8
  24.9 0.0 collective-permute-start.9
  24.9 0.0 collective-permute-done.2.rest_1_
  24.9 3.8 %collective-permute-start.11 = (bf16[64,2048]{1,0:T(8,128)(2,1)S(1)}, bf16[64,2048]{1,0:T(8,128)(2,1)S(1)}, u32[]{:S(2)}, u32[]{:S(2)}) collective-permute-start(bf16[64,2048]{1,0:T(8,128)(2,1)S(1)} %shard_map.50.rest_2_), channel_id=1, source_target_pairs={{0,6},{1,7},{2,0},{3,1},{4,2},{5,3},{6,4},{7,5},{8,14},{9,15},{10,... | collective-permute-start | bytes 786440 | tf_op jit(solution)/shard_map/ppermute | solution.py:223
  28.7 0.0 collective-permute-done.6.rest_5_
  28.7 1.5 %collective-permute-start.13 = (bf16[64,2048]{1,0:T(8,128)(2,1)S(1)}, bf16[64,2048]{1,0:T(8,128)(2,1)S(1)}, u32[]{:S(2)}, u32[]{:S(2)}) collective-permute-start(bf16[64,2048]{1,0:T(8,128)(2,1)S(1)} %shard_map.50.rest_2_), channel_id=1, source_target_pairs={{0,16},{8,24},{16,0},{24,8},{1,17},{9,25},{17,1},{25,9},{2,18},{10... | collective-permute-start | bytes 786440 | tf_op jit(solution)/shard_map/ppermute | solution.py:217
  30.2 1.5 %collective-permute-start.15 = (bf16[64,2048]{1,0:T(8,128)(2,1)S(1)}, bf16[64,2048]{1,0:T(8,128)(2,1)S(1)}, u32[]{:S(2)}, u32[]{:S(2)}) collective-permute-start(bf16[64,2048]{1,0:T(8,128)(2,1)S(1)} %shard_map.50.rest_2_), channel_id=1, source_target_pairs={{0,1},{1,0},{2,3},{3,2},{4,5},{5,4},{6,7},{7,6},{8,9},{9,8},{10,11... | collective-permute-start | bytes 786440 | tf_op jit(solution)/shard_map/ppermute | solution.py:220
  31.7 0.6 collective-permute-start.17
  32.3 7.1 %shard_map.54 = (f32[1536,2048]{1,0:T(8,128)S(1)}, f32[8,128]{1,0:T(8,128)S(1)}) custom-call(bf16[1536,2048]{1,0:T(8,128)(2,1)S(1)} %get-tuple-element.28.rows_ref, f32[1536,1]{1,0:T(8,128)S(1)} %get-tuple-element.29.row_energy_ref, f32[1,512]{1,0:T(1,128)S(1)} %get-tuple-element.33.block_energy_ref, bf16[64,2048]{1,0:T(8,128)(2,1)S(1)} %shard_map.49.rest_0_, ...), custom_call_target="tpu_custom_call" | custom-call | tf_op jit(solution)/shard_map/pallas_call | solution.py:17
  39.4 0.0 collective-permute-done.9.refs_1_
  39.4 0.1 collective-permute-start.10
  39.5 0.0 collective-permute-done.11.refs_1_
  39.5 0.5 collective-permute-start.12
  40.0 0.0 collective-permute-done.13.refs_1_
  40.0 0.1 collective-permute-start.14
  40.1 0.0 collective-permute-done.15.refs_1_
  40.1 0.4 collective-permute-start.16
  40.5 1.5 %collective-permute-start.18 = (bf16[64,2048]{1,0:T(8,128)(2,1)S(1)}, bf16[64,2048]{1,0:T(8,128)(2,1)S(1)}, u32[]{:S(2)}, u32[]{:S(2)}) collective-permute-start(bf16[64,2048]{1,0:T(8,128)(2,1)S(1)} %shard_map.56.rest_2_), channel_id=1, source_target_pairs={{0,16},{8,24},{16,0},{24,8},{1,17},{9,25},{17,1},{25,9},{2,18},{10... | collective-permute-start | bytes 786440 | tf_op jit(solution)/shard_map/ppermute | solution.py:217
  42.0 0.0 collective-permute-done.10.rest_1_
  42.0 0.5 collective-permute-start.20
  42.6 1.5 %collective-permute-start.22 = (bf16[64,2048]{1,0:T(8,128)(2,1)S(1)}, bf16[64,2048]{1,0:T(8,128)(2,1)S(1)}, u32[]{:S(2)}, u32[]{:S(2)}) collective-permute-start(bf16[64,2048]{1,0:T(8,128)(2,1)S(1)} %shard_map.56.rest_2_), channel_id=1, source_target_pairs={{0,1},{1,0},{2,3},{3,2},{4,5},{5,4},{6,7},{7,6},{8,9},{9,8},{10,11... | collective-permute-start | bytes 786440 | tf_op jit(solution)/shard_map/ppermute | solution.py:220
  44.1 0.5 collective-permute-start.25
  44.6 7.4 %shard_map.61 = (f32[1536,2048]{1,0:T(8,128)S(1)}, f32[8,128]{1,0:T(8,128)S(1)}) custom-call(bf16[1536,2048]{1,0:T(8,128)(2,1)S(1)} %get-tuple-element.28.rows_ref, f32[1536,1]{1,0:T(8,128)S(1)} %get-tuple-element.29.row_energy_ref, f32[1,512]{1,0:T(1,128)S(1)} %get-tuple-element.32.block_energy_ref, ...), custom_call_target="tpu_custom_call", output_to_operand_aliasing={{0}: (12, {})} | custom-call | tf_op jit(solution)/shard_map/pallas_call | solution.py:17
  52.0 0.6 collective-permute-start.19
  52.6 0.0 collective-permute-done.20.refs_1_
  52.6 0.1 collective-permute-start.21
  52.7 0.0 collective-permute-done.22.refs_1_
  52.7 0.4 collective-permute-start.23
  53.1 1.7 %collective-permute-start.26 = (bf16[64,2048]{1,0:T(8,128)(2,1)S(1)}, bf16[64,2048]{1,0:T(8,128)(2,1)S(1)}, u32[]{:S(2)}, u32[]{:S(2)}) collective-permute-start(bf16[64,2048]{1,0:T(8,128)(2,1)S(1)} %shard_map.60.rest_8_.rest_6_), channel_id=1, source_target_pairs={{0,2},{1,3},{2,4},{3,5},{4,6},{5,7},{6,0},{7,1},{8,10},{9,11},{10,... | collective-permute-start | bytes 786440 | tf_op jit(solution)/shard_map/ppermute | solution.py:223
  54.9 0.0 collective-permute-done.25.refs_1_
  54.9 1.6 %collective-permute-start.28 = (bf16[64,2048]{1,0:T(8,128)(2,1)S(1)}, bf16[64,2048]{1,0:T(8,128)(2,1)S(1)}, u32[]{:S(2)}, u32[]{:S(2)}) collective-permute-start(bf16[64,2048]{1,0:T(8,128)(2,1)S(1)} %shard_map.68), channel_id=1, source_target_pairs={{0,16},{1,17},{2,18},{3,19},{4,20},{5,21},{6,22},{7,23},{8,9},{9,8... | collective-permute-start | bytes 786440 | tf_op jit(solution)/shard_map/ppermute | solution.py:228
  56.5 0.6 collective-permute-start.31
  57.1 0.0 collective-permute-done.21.rest_3_
  57.1 0.0 collective-permute-start.30
  57.1 0.0 collective-permute-done.23.rest_5_
  57.1 7.4 %shard_map.66 = (f32[1536,2048]{1,0:T(8,128)S(1)}, f32[8,128]{1,0:T(8,128)S(1)}) custom-call(bf16[1536,2048]{1,0:T(8,128)(2,1)S(1)} %get-tuple-element.28.rows_ref, f32[1536,1]{1,0:T(8,128)S(1)} %get-tuple-element.29.row_energy_ref, f32[1,512]{1,0:T(1,128)S(1)} %get-tuple-element.31.block_energy_ref, ...), custom_call_target="tpu_custom_call", output_to_operand_aliasing={{0}: (12, {})} | custom-call | tf_op jit(solution)/shard_map/pallas_call | solution.py:17
  64.5 0.6 collective-permute-start.27
  65.1 0.1 collective-permute-start.29
  65.2 0.4 collective-permute-start.32
  65.6 0.6 collective-permute-done.27.rest_1_
  66.3 0.4 collective-permute-done.29.rest_3_
  66.6 0.4 collective-permute-done.32.rest_7_
  67.0 9.3 %shard_map.72 = (bf16[1536,2048]{1,0:T(8,128)(2,1)}, f32[8,128]{1,0:T(8,128)}) custom-call(bf16[1536,2048]{1,0:T(8,128)(2,1)S(1)} %get-tuple-element.28.rows_ref, f32[1536,1]{1,0:T(8,128)S(1)} %get-tuple-element.29.row_energy_ref, f32[1,512]{1,0:T(1,128)S(1)} %get-tuple-element.30.block_energy_ref, bf16[64,2048]{1,0:T(8,128)(2,1)S(1)} %shard_map.67.rest_0_, ...), custom_call_target="tpu_custom_call" | custom-call | tf_op jit(solution)/shard_map/pallas_call | solution.py:17
  (37 shorter events, 0.2 us)
Async XLA Ops:
  1.9 2.1 %collective-permute-start = (bf16[128,2048]{1,0:T(8,128)(2,1)S(1)}, bf16[128,2048]{1,0:T(8,128)(2,1)S(1)}, u32[]{:S(2)}, u32[]{:S(2)}) collective-permute-start(bf16[128,2048]{1,0:T(8,128)(2,1)S(1)} %get-tuple-element.26), channel_id=1, source_target_pairs={{0,8},{8,0},{16,24},{24,16},{1,9},{9,1},{17,25},{25,17},{2,10},{10... | collective-permute-start | bytes 1572872 | tf_op jit(solution)/shard_map/ppermute | solution.py:217
  4.1 10.0 %collective-permute-start.1 = (bf16[64,2048]{1,0:T(8,128)(2,1)S(1)}, bf16[64,2048]{1,0:T(8,128)(2,1)S(1)}, u32[]{:S(2)}, u32[]{:S(2)}) collective-permute-start(bf16[64,2048]{1,0:T(8,128)(2,1)S(1)} %get-tuple-element.34.own_ref), channel_id=1, source_target_pairs={{0,16},{8,24},{16,0},{24,8},{1,17},{9,25},{17,1},{25,9},{2,18},{10... | collective-permute-start | bytes 786440 | tf_op jit(solution)/shard_map/ppermute | solution.py:217
  7.8 12.1 %collective-permute-start.5 = (bf16[64,2048]{1,0:T(8,128)(2,1)S(1)}, bf16[64,2048]{1,0:T(8,128)(2,1)S(1)}, u32[]{:S(2)}, u32[]{:S(2)}) collective-permute-start(bf16[64,2048]{1,0:T(8,128)(2,1)S(1)} %get-tuple-element.27.rest_0_.own_ref), channel_id=1, source_target_pairs={{0,16},{8,24},{16,0},{24,8},{1,17},{9,25},{17,1},{25,9},{2,18},{10... | collective-permute-start | bytes 786440 | tf_op jit(solution)/shard_map/ppermute | solution.py:217
  7.8 2.8 %copy-start = (bf16[12,128,2048]{2,1,0:T(8,128)(2,1)S(1)}, bf16[12,128,2048]{2,1,0:T(8,128)(2,1)}, u32[]{:S(2)}) copy-start(bf16[12,128,2048]{2,1,0:T(8,128)(2,1)} %integrals_ref.1) | copy-start | bytes 18874372
  10.6 0.7 copy-start.1
  11.3 0.7 copy-start.2
  14.1 8.5 %collective-permute-start.3 = (bf16[64,2048]{1,0:T(8,128)(2,1)S(1)}, bf16[64,2048]{1,0:T(8,128)(2,1)S(1)}, u32[]{:S(2)}, u32[]{:S(2)}) collective-permute-start(bf16[64,2048]{1,0:T(8,128)(2,1)S(1)} %shard_map.49.rest_0_), channel_id=1, source_target_pairs={{0,6},{1,7},{2,0},{3,1},{4,2},{5,3},{6,4},{7,5},{8,14},{9,15},{10,... | collective-permute-start | bytes 786440 | tf_op jit(solution)/shard_map/ppermute | solution.py:223
  18.4 6.5 %collective-permute-start.7 = (bf16[64,2048]{1,0:T(8,128)(2,1)S(1)}, bf16[64,2048]{1,0:T(8,128)(2,1)S(1)}, u32[]{:S(2)}, u32[]{:S(2)}) collective-permute-start(bf16[64,2048]{1,0:T(8,128)(2,1)S(1)} %shard_map.49.rest_0_), channel_id=1, source_target_pairs={{0,1},{1,0},{2,3},{3,2},{4,5},{5,4},{6,7},{7,6},{8,9},{9,8},{10,11... | collective-permute-start | bytes 786440 | tf_op jit(solution)/shard_map/ppermute | solution.py:220
  19.9 5.0 %collective-permute-start.2 = (bf16[64,2048]{1,0:T(8,128)(2,1)S(1)}, bf16[64,2048]{1,0:T(8,128)(2,1)S(1)}, u32[]{:S(2)}, u32[]{:S(2)}) collective-permute-start(bf16[64,2048]{1,0:T(8,128)(2,1)S(1)} %shard_map.49.rest_0_), channel_id=1, source_target_pairs={{0,8},{8,0},{16,24},{24,16},{1,9},{9,1},{17,25},{25,17},{2,10},{10... | collective-permute-start | bytes 786440 | tf_op jit(solution)/shard_map/ppermute | solution.py:217
  20.0 8.7 %collective-permute-start.6 = (bf16[64,2048]{1,0:T(8,128)(2,1)S(1)}, bf16[64,2048]{1,0:T(8,128)(2,1)S(1)}, u32[]{:S(2)}, u32[]{:S(2)}) collective-permute-start(bf16[64,2048]{1,0:T(8,128)(2,1)S(1)} %shard_map.52.rest_4_.second_ref), channel_id=1, source_target_pairs={{0,8},{8,0},{16,24},{24,16},{1,9},{9,1},{17,25},{25,17},{2,10},{10... | collective-permute-start | bytes 786440 | tf_op jit(solution)/shard_map/ppermute | solution.py:217
  22.6 7.5 %collective-permute-start.4 = (bf16[64,2048]{1,0:T(8,128)(2,1)S(1)}, bf16[64,2048]{1,0:T(8,128)(2,1)S(1)}, u32[]{:S(2)}, u32[]{:S(2)}) collective-permute-start(bf16[64,2048]{1,0:T(8,128)(2,1)S(1)} %shard_map.50.rest_2_), channel_id=1, source_target_pairs={{0,8},{8,0},{16,24},{24,16},{1,9},{9,1},{17,25},{25,17},{2,10},{10... | collective-permute-start | bytes 786440 | tf_op jit(solution)/shard_map/ppermute | solution.py:217
  24.8 6.9 %collective-permute-start.8 = (bf16[64,2048]{1,0:T(8,128)(2,1)S(1)}, bf16[64,2048]{1,0:T(8,128)(2,1)S(1)}, u32[]{:S(2)}, u32[]{:S(2)}) collective-permute-start(bf16[64,2048]{1,0:T(8,128)(2,1)S(1)} %shard_map.53.rest_6_.first_ref), channel_id=1, source_target_pairs={{0,8},{8,0},{16,24},{24,16},{1,9},{9,1},{17,25},{25,17},{2,10},{10... | collective-permute-start | bytes 786440 | tf_op jit(solution)/shard_map/ppermute | solution.py:217
  24.9 14.6 %collective-permute-start.9 = (bf16[64,2048]{1,0:T(8,128)(2,1)S(1)}, bf16[64,2048]{1,0:T(8,128)(2,1)S(1)}, u32[]{:S(2)}, u32[]{:S(2)}) collective-permute-start(bf16[64,2048]{1,0:T(8,128)(2,1)S(1)} %shard_map.49.rest_0_), channel_id=1, source_target_pairs={{0,2},{1,3},{2,4},{3,5},{4,6},{5,7},{6,0},{7,1},{8,10},{9,11},{10,... | collective-permute-start | bytes 786440 | tf_op jit(solution)/shard_map/ppermute | solution.py:223
  24.9 14.7 %collective-permute-start.11 = (bf16[64,2048]{1,0:T(8,128)(2,1)S(1)}, bf16[64,2048]{1,0:T(8,128)(2,1)S(1)}, u32[]{:S(2)}, u32[]{:S(2)}) collective-permute-start(bf16[64,2048]{1,0:T(8,128)(2,1)S(1)} %shard_map.50.rest_2_), channel_id=1, source_target_pairs={{0,6},{1,7},{2,0},{3,1},{4,2},{5,3},{6,4},{7,5},{8,14},{9,15},{10,... | collective-permute-start | bytes 786440 | tf_op jit(solution)/shard_map/ppermute | solution.py:223
  28.7 11.3 %collective-permute-start.13 = (bf16[64,2048]{1,0:T(8,128)(2,1)S(1)}, bf16[64,2048]{1,0:T(8,128)(2,1)S(1)}, u32[]{:S(2)}, u32[]{:S(2)}) collective-permute-start(bf16[64,2048]{1,0:T(8,128)(2,1)S(1)} %shard_map.50.rest_2_), channel_id=1, source_target_pairs={{0,16},{8,24},{16,0},{24,8},{1,17},{9,25},{17,1},{25,9},{2,18},{10... | collective-permute-start | bytes 786440 | tf_op jit(solution)/shard_map/ppermute | solution.py:217
  30.2 9.9 %collective-permute-start.15 = (bf16[64,2048]{1,0:T(8,128)(2,1)S(1)}, bf16[64,2048]{1,0:T(8,128)(2,1)S(1)}, u32[]{:S(2)}, u32[]{:S(2)}) collective-permute-start(bf16[64,2048]{1,0:T(8,128)(2,1)S(1)} %shard_map.50.rest_2_), channel_id=1, source_target_pairs={{0,1},{1,0},{2,3},{3,2},{4,5},{5,4},{6,7},{7,6},{8,9},{9,8},{10,11... | collective-permute-start | bytes 786440 | tf_op jit(solution)/shard_map/ppermute | solution.py:220
  31.7 8.8 %collective-permute-start.17 = (bf16[64,2048]{1,0:T(8,128)(2,1)S(1)}, bf16[64,2048]{1,0:T(8,128)(2,1)S(1)}, u32[]{:S(2)}, u32[]{:S(2)}) collective-permute-start(bf16[64,2048]{1,0:T(8,128)(2,1)S(1)} %shard_map.59), channel_id=1, source_target_pairs={{0,16},{1,17},{2,18},{3,19},{4,20},{5,21},{6,22},{7,23},{8,9},{9,8... | collective-permute-start | bytes 786440 | tf_op jit(solution)/shard_map/ppermute | solution.py:228
  39.4 2.6 %collective-permute-start.10 = (bf16[64,2048]{1,0:T(8,128)(2,1)S(1)}, bf16[64,2048]{1,0:T(8,128)(2,1)S(1)}, u32[]{:S(2)}, u32[]{:S(2)}) collective-permute-start(bf16[64,2048]{1,0:T(8,128)(2,1)S(1)} %shard_map.55.rest_0_), channel_id=1, source_target_pairs={{0,8},{8,0},{16,24},{24,16},{1,9},{9,1},{17,25},{25,17},{2,10},{10... | collective-permute-start | bytes 786440 | tf_op jit(solution)/shard_map/ppermute | solution.py:217
  39.5 3.0 %collective-permute-start.12 = (bf16[64,2048]{1,0:T(8,128)(2,1)S(1)}, bf16[64,2048]{1,0:T(8,128)(2,1)S(1)}, u32[]{:S(2)}, u32[]{:S(2)}) collective-permute-start(bf16[64,2048]{1,0:T(8,128)(2,1)S(1)} %shard_map.56.rest_2_), channel_id=1, source_target_pairs={{0,8},{8,0},{16,24},{24,16},{1,9},{9,1},{17,25},{25,17},{2,10},{10... | collective-permute-start | bytes 786440 | tf_op jit(solution)/shard_map/ppermute | solution.py:217
  40.0 4.1 %collective-permute-start.14 = (bf16[64,2048]{1,0:T(8,128)(2,1)S(1)}, bf16[64,2048]{1,0:T(8,128)(2,1)S(1)}, u32[]{:S(2)}, u32[]{:S(2)}) collective-permute-start(bf16[64,2048]{1,0:T(8,128)(2,1)S(1)} %shard_map.57.rest_4_.second_ref), channel_id=1, source_target_pairs={{0,8},{8,0},{16,24},{24,16},{1,9},{9,1},{17,25},{25,17},{2,10},{10... | collective-permute-start | bytes 786440 | tf_op jit(solution)/shard_map/ppermute | solution.py:217
  40.1 4.5 %collective-permute-start.16 = (bf16[64,2048]{1,0:T(8,128)(2,1)S(1)}, bf16[64,2048]{1,0:T(8,128)(2,1)S(1)}, u32[]{:S(2)}, u32[]{:S(2)}) collective-permute-start(bf16[64,2048]{1,0:T(8,128)(2,1)S(1)} %shard_map.58.rest_6_.first_ref), channel_id=1, source_target_pairs={{0,8},{8,0},{16,24},{24,16},{1,9},{9,1},{17,25},{25,17},{2,10},{10... | collective-permute-start | bytes 786440 | tf_op jit(solution)/shard_map/ppermute | solution.py:217
  40.5 11.5 %collective-permute-start.18 = (bf16[64,2048]{1,0:T(8,128)(2,1)S(1)}, bf16[64,2048]{1,0:T(8,128)(2,1)S(1)}, u32[]{:S(2)}, u32[]{:S(2)}) collective-permute-start(bf16[64,2048]{1,0:T(8,128)(2,1)S(1)} %shard_map.56.rest_2_), channel_id=1, source_target_pairs={{0,16},{8,24},{16,0},{24,8},{1,17},{9,25},{17,1},{25,9},{2,18},{10... | collective-permute-start | bytes 786440 | tf_op jit(solution)/shard_map/ppermute | solution.py:217
  42.0 10.6 %collective-permute-start.20 = (bf16[64,2048]{1,0:T(8,128)(2,1)S(1)}, bf16[64,2048]{1,0:T(8,128)(2,1)S(1)}, u32[]{:S(2)}, u32[]{:S(2)}) collective-permute-start(bf16[64,2048]{1,0:T(8,128)(2,1)S(1)} %shard_map.53.rest_6_.first_ref), channel_id=1, source_target_pairs={{0,2},{1,3},{2,4},{3,5},{4,6},{5,7},{6,0},{7,1},{8,10},{9,11},{10,... | collective-permute-start | bytes 786440 | tf_op jit(solution)/shard_map/ppermute | solution.py:223
  42.6 10.2 %collective-permute-start.22 = (bf16[64,2048]{1,0:T(8,128)(2,1)S(1)}, bf16[64,2048]{1,0:T(8,128)(2,1)S(1)}, u32[]{:S(2)}, u32[]{:S(2)}) collective-permute-start(bf16[64,2048]{1,0:T(8,128)(2,1)S(1)} %shard_map.56.rest_2_), channel_id=1, source_target_pairs={{0,1},{1,0},{2,3},{3,2},{4,5},{5,4},{6,7},{7,6},{8,9},{9,8},{10,11... | collective-permute-start | bytes 786440 | tf_op jit(solution)/shard_map/ppermute | solution.py:220
  44.1 10.8 %collective-permute-start.25 = (bf16[64,2048]{1,0:T(8,128)(2,1)S(1)}, bf16[64,2048]{1,0:T(8,128)(2,1)S(1)}, u32[]{:S(2)}, u32[]{:S(2)}) collective-permute-start(bf16[64,2048]{1,0:T(8,128)(2,1)S(1)} %shard_map.55.rest_0_), channel_id=1, source_target_pairs={{0,16},{8,24},{16,0},{24,8},{1,17},{9,25},{17,1},{25,9},{2,18},{10... | collective-permute-start | bytes 786440 | tf_op jit(solution)/shard_map/ppermute | solution.py:217
  44.6 8.5 %collective-permute-start.24 = (bf16[64,2048]{1,0:T(8,128)(2,1)S(1)}, bf16[64,2048]{1,0:T(8,128)(2,1)S(1)}, u32[]{:S(2)}, u32[]{:S(2)}) collective-permute-start(bf16[64,2048]{1,0:T(8,128)(2,1)S(1)} %shard_map.60.rest_8_.rest_6_), channel_id=1, source_target_pairs={{0,8},{8,0},{16,24},{24,16},{1,9},{9,1},{17,25},{25,17},{2,10},{10... | collective-permute-start | bytes 786440 | tf_op jit(solution)/shard_map/ppermute | solution.py:217
  52.0 4.4 %collective-permute-start.19 = (bf16[64,2048]{1,0:T(8,128)(2,1)S(1)}, bf16[64,2048]{1,0:T(8,128)(2,1)S(1)}, u32[]{:S(2)}, u32[]{:S(2)}) collective-permute-start(bf16[64,2048]{1,0:T(8,128)(2,1)S(1)} %shard_map.62.rest_0_.second_ref), channel_id=1, source_target_pairs={{0,8},{8,0},{16,24},{24,16},{1,9},{9,1},{17,25},{25,17},{2,10},{10... | collective-permute-start | bytes 786440 | tf_op jit(solution)/shard_map/ppermute | solution.py:217
  52.6 4.5 %collective-permute-start.21 = (bf16[64,2048]{1,0:T(8,128)(2,1)S(1)}, bf16[64,2048]{1,0:T(8,128)(2,1)S(1)}, u32[]{:S(2)}, u32[]{:S(2)}) collective-permute-start(bf16[64,2048]{1,0:T(8,128)(2,1)S(1)} %shard_map.63.rest_2_), channel_id=1, source_target_pairs={{0,8},{8,0},{16,24},{24,16},{1,9},{9,1},{17,25},{25,17},{2,10},{10... | collective-permute-start | bytes 786440 | tf_op jit(solution)/shard_map/ppermute | solution.py:217
  52.7 4.4 %collective-permute-start.23 = (bf16[64,2048]{1,0:T(8,128)(2,1)S(1)}, bf16[64,2048]{1,0:T(8,128)(2,1)S(1)}, u32[]{:S(2)}, u32[]{:S(2)}) collective-permute-start(bf16[64,2048]{1,0:T(8,128)(2,1)S(1)} %shard_map.64.rest_4_.first_ref), channel_id=1, source_target_pairs={{0,8},{8,0},{16,24},{24,16},{1,9},{9,1},{17,25},{25,17},{2,10},{10... | collective-permute-start | bytes 786440 | tf_op jit(solution)/shard_map/ppermute | solution.py:217
  53.1 11.4 %collective-permute-start.26 = (bf16[64,2048]{1,0:T(8,128)(2,1)S(1)}, bf16[64,2048]{1,0:T(8,128)(2,1)S(1)}, u32[]{:S(2)}, u32[]{:S(2)}) collective-permute-start(bf16[64,2048]{1,0:T(8,128)(2,1)S(1)} %shard_map.60.rest_8_.rest_6_), channel_id=1, source_target_pairs={{0,2},{1,3},{2,4},{3,5},{4,6},{5,7},{6,0},{7,1},{8,10},{9,11},{10,... | collective-permute-start | bytes 786440 | tf_op jit(solution)/shard_map/ppermute | solution.py:223
  54.9 10.2 %collective-permute-start.28 = (bf16[64,2048]{1,0:T(8,128)(2,1)S(1)}, bf16[64,2048]{1,0:T(8,128)(2,1)S(1)}, u32[]{:S(2)}, u32[]{:S(2)}) collective-permute-start(bf16[64,2048]{1,0:T(8,128)(2,1)S(1)} %shard_map.68), channel_id=1, source_target_pairs={{0,16},{1,17},{2,18},{3,19},{4,20},{5,21},{6,22},{7,23},{8,9},{9,8... | collective-permute-start | bytes 786440 | tf_op jit(solution)/shard_map/ppermute | solution.py:228
  56.5 8.7 %collective-permute-start.31 = (bf16[64,2048]{1,0:T(8,128)(2,1)S(1)}, bf16[64,2048]{1,0:T(8,128)(2,1)S(1)}, u32[]{:S(2)}, u32[]{:S(2)}) collective-permute-start(bf16[64,2048]{1,0:T(8,128)(2,1)S(1)} %shard_map.70), channel_id=1, source_target_pairs={{0,16},{1,17},{2,18},{3,19},{4,20},{5,21},{6,22},{7,23},{8,9},{9,8... | collective-permute-start | bytes 786440 | tf_op jit(solution)/shard_map/ppermute | solution.py:228
  57.1 8.5 %collective-permute-start.30 = (bf16[64,2048]{1,0:T(8,128)(2,1)S(1)}, bf16[64,2048]{1,0:T(8,128)(2,1)S(1)}, u32[]{:S(2)}, u32[]{:S(2)}) collective-permute-start(bf16[64,2048]{1,0:T(8,128)(2,1)S(1)} %shard_map.65.rest_8_.rest_4_), channel_id=1, source_target_pairs={{0,8},{8,0},{16,24},{24,16},{1,9},{9,1},{17,25},{25,17},{2,10},{10... | collective-permute-start | bytes 786440 | tf_op jit(solution)/shard_map/ppermute | solution.py:217
  64.5 1.7 %collective-permute-start.27 = (bf16[64,2048]{1,0:T(8,128)(2,1)S(1)}, bf16[64,2048]{1,0:T(8,128)(2,1)S(1)}, u32[]{:S(2)}, u32[]{:S(2)}) collective-permute-start(bf16[64,2048]{1,0:T(8,128)(2,1)S(1)} %shard_map.67.rest_0_), channel_id=1, source_target_pairs={{0,8},{8,0},{16,24},{24,16},{1,9},{9,1},{17,25},{25,17},{2,10},{10... | collective-permute-start | bytes 786440 | tf_op jit(solution)/shard_map/ppermute | solution.py:217
  65.1 1.5 %collective-permute-start.29 = (bf16[64,2048]{1,0:T(8,128)(2,1)S(1)}, bf16[64,2048]{1,0:T(8,128)(2,1)S(1)}, u32[]{:S(2)}, u32[]{:S(2)}) collective-permute-start(bf16[64,2048]{1,0:T(8,128)(2,1)S(1)} %shard_map.69.rest_2_), channel_id=1, source_target_pairs={{0,8},{8,0},{16,24},{24,16},{1,9},{9,1},{17,25},{25,17},{2,10},{10... | collective-permute-start | bytes 786440 | tf_op jit(solution)/shard_map/ppermute | solution.py:217
  65.2 1.8 %collective-permute-start.32 = (bf16[64,2048]{1,0:T(8,128)(2,1)S(1)}, bf16[64,2048]{1,0:T(8,128)(2,1)S(1)}, u32[]{:S(2)}, u32[]{:S(2)}) collective-permute-start(bf16[64,2048]{1,0:T(8,128)(2,1)S(1)} %shard_map.71.rest_6_), channel_id=1, source_target_pairs={{0,8},{8,0},{16,24},{24,16},{1,9},{9,1},{17,25},{25,17},{2,10},{10... | collective-permute-start | bytes 786440 | tf_op jit(solution)/shard_map/ppermute | solution.py:217
